TPU v7x, 32 devices: a whole 2x2x4 slice. The times are simulated.
32 devices in a mesh: groups: 2 (over x), gx: 16 (over z, y, core).
Axes of the slice: x: 2, y: 2, z: 4, core: 2. Of those that a mesh axis runs over, the one named last changes fastest.
Arguments:
- adjoint_state: float32 [8, 96, 128, 128], P(None, 'groups', 'gx'), parts along dimension 1, may hold values from -6 to 6
- forward_fields: bfloat16 [2, 3, 96, 128, 128], P(None, None, 'groups', 'gx'), parts along dimension 2, may hold values from -6 to 6
- vel_coeffs: float32 [8, 128], P('groups'), parts along dimension 0, may hold values from 0.2 to 0.8
- stress_coeffs: float32 [8, 128], P('groups'), parts along dimension 0, may hold values from 0.15 to 0.6
- drm_cells: int32 [4096], P('gx'), may hold values from 120 to 16383, as said below
- drm_force: float32 [32, 2, 2, 4096], P('groups', None, None, 'gx'), parts along dimension 0, may hold values from -6 to 6
- source_id: int32 [96], P('groups'), parts along dimension 0, may hold values from 0 to 15
Outputs:
- adjoint_out: float32 [8, 96, 128, 128], P(None, 'groups', 'gx'), parts along dimension 1
- gradients: float32 [4, 128], P('groups'), parts along dimension 0
There are 2 independent parts, one for each index of `groups`. A program takes and returns all parts, laid end to end along the dimension named above; an argument that names none is the same for every part. Nothing has to cross between parts.
Inputs may be any that keep to these rules, and one draw needn't show every extreme that they name: `drm_cells`: in each aligned block b of 256 entries, every entry names a cell x * 128 + z with b * 8 <= x < (b + 1) * 8 and 120 <= z < 128; cells may repeat.
All inputs are finite; a program needn't handle non-finite values.
Results may differ from a plain program's by a relative error of at most 0.0003.
Values sent between devices are 32-bit elements; how exact they have to be, the bound alone decides.
No kernel may reach another device: no remote copies, remote signals or barrier semaphores. Data moves between devices by JAX's collectives and lax.ppermute only.
A program may use at most 64 MiB of HBM per device.

v0:
```python
import jax
import jax.numpy as jnp
from jax import lax
from jax.sharding import PartitionSpec as P

LAYER = 8


def passed_along(block, axis, distance):
    devices = range(lax.axis_size(axis))
    route = [(i - distance, i) for i in devices if i - distance in devices]
    return lax.ppermute(block, axis, route)


def lower_diff(values, before):
    return values - jnp.concatenate([before, values[:, :-1]], axis=1)


def upper_diff(values, beyond):
    return jnp.concatenate([values[:, 1:], beyond], axis=1) - values


def depth_lower(values):
    return values - jnp.concatenate([jnp.zeros_like(values[:, :, :1]), values[:, :, :-1]], axis=2)


def depth_upper(values):
    return jnp.concatenate([values[:, :, 1:], jnp.zeros_like(values[:, :, :1])], axis=2) - values


def velocity_update(fields, before, forcing_layer, vel_coeffs):
    vel_x, vel_z, flow_x, flow_z, stress_xx, stress_zz, stress_xz, pressure = fields
    mass_solid, mass_couple, mass_fluid, drag_rate = (
        vel_coeffs[0],
        vel_coeffs[1],
        vel_coeffs[2],
        vel_coeffs[3],
    )
    force_x = lower_diff(stress_xx, before[0]) + depth_lower(stress_xz)
    force_z = lower_diff(stress_xz, before[1]) + depth_lower(stress_zz)
    push_x = lower_diff(pressure, before[2]) + drag_rate * flow_x
    push_z = depth_lower(pressure) + drag_rate * flow_z
    vel_x = vel_x + mass_solid * force_x + mass_couple * push_x
    vel_z = vel_z + mass_solid * force_z + mass_couple * push_z
    layer_start = vel_x.shape[2] - forcing_layer.shape[3]
    vel_x = vel_x.at[:, :, layer_start:].add(forcing_layer[0])
    vel_z = vel_z.at[:, :, layer_start:].add(forcing_layer[1])
    flow_x = flow_x - mass_couple * force_x - mass_fluid * push_x
    flow_z = flow_z - mass_couple * force_z - mass_fluid * push_z
    return [vel_x, vel_z, flow_x, flow_z, stress_xx, stress_zz, stress_xz, pressure]


def stress_update(fields, beyond, stress_coeffs):
    vel_x, vel_z, flow_x, flow_z, stress_xx, stress_zz, stress_xz, pressure = fields
    lame_total, shear_modulus, coupling, fluid_modulus = (
        stress_coeffs[0],
        stress_coeffs[1],
        stress_coeffs[2],
        stress_coeffs[3],
    )
    strain_x = upper_diff(vel_x, beyond[0])
    strain_z = depth_upper(vel_z)
    dilation = strain_x + strain_z
    inflow = upper_diff(flow_x, beyond[2]) + depth_upper(flow_z)
    stress_xx = (
        stress_xx + lame_total * dilation + 2.0 * shear_modulus * strain_x - coupling * inflow
    )
    stress_zz = (
        stress_zz + lame_total * dilation + 2.0 * shear_modulus * strain_z - coupling * inflow
    )
    stress_xz = stress_xz + shear_modulus * (depth_upper(vel_x) + upper_diff(vel_z, beyond[1]))
    pressure = pressure - coupling * dilation - fluid_modulus * inflow
    return [vel_x, vel_z, flow_x, flow_z, stress_xx, stress_zz, stress_xz, pressure]


def flow_term(fields, forward_fields, step_index):
    flow_prod = fields[2] * forward_fields[step_index, 0].astype(jnp.float32) + fields[
        3
    ] * forward_fields[step_index, 1].astype(jnp.float32)
    return jnp.sum(flow_prod, axis=(0, 1))


def pressure_term(fields, forward_fields, step_index):
    return jnp.sum(fields[7] * forward_fields[step_index, 2].astype(jnp.float32), axis=(0, 1))


def shards(
    adjoint_state, forward_fields, vel_coeffs, stress_coeffs, drm_cells, drm_force, source_id
):
    event_count = adjoint_state.shape[1]
    row_count = adjoint_state.shape[2]
    depth_cells = adjoint_state.shape[3]
    step_count = forward_fields.shape[0]
    local_cells = drm_cells % (row_count * depth_cells)
    layer_slot = (
        local_cells // depth_cells * LAYER + local_cells % depth_cells - (depth_cells - LAYER)
    )
    slot_ids = jnp.arange(row_count * LAYER, dtype=jnp.int32)
    one_hot = (layer_slot[:, None] == slot_ids[None, :]).astype(jnp.float32)
    selected = drm_force[source_id]
    layer_force = jnp.dot(
        selected.reshape(-1, selected.shape[3]),
        one_hot,
        precision=lax.Precision.HIGHEST,
        preferred_element_type=jnp.float32,
    )
    layer_force = layer_force.reshape(event_count, step_count, 2, row_count, LAYER)
    layer_planes = jnp.transpose(layer_force, (1, 2, 0, 3, 4))
    perm_part = jnp.zeros((depth_cells,), jnp.float32)
    poro_part = jnp.zeros((depth_cells,), jnp.float32)
    fields = [adjoint_state[field_index] for field_index in range(8)]
    for step_index in range(step_count):
        boundary_rows = jnp.stack([fields[4][:, -1:], fields[6][:, -1:], fields[7][:, -1:]])
        before = passed_along(boundary_rows, "gx", 1)
        fields = velocity_update(
            fields, [before[0], before[1], before[2]], layer_planes[step_index], vel_coeffs
        )
        perm_part = perm_part + flow_term(fields, forward_fields, step_index)
        boundary_rows = jnp.stack([fields[0][:, :1], fields[1][:, :1], fields[2][:, :1]])
        beyond = passed_along(boundary_rows, "gx", -1)
        fields = stress_update(fields, [beyond[0], beyond[1], beyond[2]], stress_coeffs)
        poro_part = poro_part + pressure_term(fields, forward_fields, step_index)
    totals = lax.psum(jnp.stack([perm_part, poro_part]), "gx")
    normalizer = (event_count * row_count * lax.axis_size("gx")) ** (-0.5)
    gradients = (
        jnp.stack([vel_coeffs[2] * vel_coeffs[3] * totals[0], stress_coeffs[3] * totals[1]])
        * normalizer
    )
    return (jnp.stack(fields), gradients)


def solution(mesh):
    in_specs = (
        P(None, "groups", "gx", None),
        P(None, None, "groups", "gx", None),
        P("groups", None),
        P("groups", None),
        P("gx"),
        P("groups", None, None, "gx"),
        P("groups"),
    )
    out_specs = (P(None, "groups", "gx", None), P("groups", None))
    return jax.shard_map(shards, mesh=mesh, in_specs=in_specs, out_specs=out_specs, check_vma=False)
```

profile of v0, /device:TPU:0, one launch (start us, length us, event | category | flops | bytes accessed | tf_op | source)
XLA Modules:
  0.0 111.2 jit_solution(2169771756858227441)
XLA Ops:
  0.6 1.6 %fusion.50 = (f32[1,48,8,128]{3,2,1,0:T(8,128)S(1)}, f32[1,48,8,128]{3,2,1,0:T(8,128)S(1)}, f32[1,48,8,128]{3,2,1,0:T(8,128)S(1)}, f32[1,48,8,128]{3,2,1,0:T(8,1...) fusion(f32[8,48,8,128]{3,2,1,0:T(8,128)} %param.15), kind=kLoop, calls=%fused_computation.147 | loop fusion | bytes 3145728 | tf_op jit(solution)/shard_map/slice | solution.py:111
  3.8 3.0 %collective-permute-start = (f32[3,48,1,128]{1,3,2,0:T(8,128)}, f32[3,48,1,128]{1,3,2,0:T(8,128)}, u32[]{:S(2)}, u32[]{:S(2)}) collective-permute-start(f32[3,48,1,128]{1,3,2,0:T(8,128)} %pad_maximum_fusion), channel_id=1, source_target_pairs={{0,1},{1,2},{2,3},{3,4},{4,5},{5,6},{6,7},{7,8},{8,9},{9,10},{10,1... | collective-permute-start | bytes 221192 | tf_op jit(solution)/shard_map/ppermute | solution.py:12
  6.8 1.9 %fusion.51 = (bf16[1,1,48,8,128]{4,3,2,1,0:T(8,128)(2,1)}, bf16[1,1,48,8,128]{4,3,2,1,0:T(8,128)(2,1)}, bf16[1,1,48,8,128]{4,3,2,1,0:T(8,128)(2,1)}, bf16[1,1,48...) fusion(bf16[2,3,48,8,128]{4,3,2,1,0:T(8,128)(2,1)} %param.16), kind=kLoop, calls=%fused_computation.148 | loop fusion | bytes 1179648 | tf_op jit(solution)/shard_map/slice | solution.py:84
  14.2 1.0 copy.169
  15.3 1.1 copy.170
  17.2 1.0 copy.162
  20.3 2.6 %fusion.20 = (f32[128]{0:T(128)S(1)}, f32[48,8,128]{0,2,1:T(8,128)S(1)}, f32[48,8,128]{0,2,1:T(8,128)S(1)}, f32[48,8,128]{0,2,1:T(8,128)S(1)}, f32[48,8,128]{0,2,1:T(8,128)S(1)}) fusion(bf16[1,1,48,8,128]{2,4,3,1,0:T(8,128)(2,1)} %copy.171, bf16[1,1,48,8,128]{2,4,3,1,0:T(8,128)(2,1)S(1)} %copy.170, f32[128]{0:T(128)S(1)} %get-tuple-element.115, ...), kind=kLoop, calls=%fused_computation.39 | loop fusion | flops 1425280 | bytes 3339776 | tf_op jit(solution)/shard_map/reduce_sum | solution.py:80
  24.8 1.3 %collective-permute-start.1 = (f32[3,48,1,128]{1,3,2,0:T(8,128)}, f32[3,48,1,128]{1,3,2,0:T(8,128)}, u32[]{:S(2)}, u32[]{:S(2)}) collective-permute-start(f32[3,48,1,128]{1,3,2,0:T(8,128)} %pad_maximum_fusion.1), channel_id=1, source_target_pairs={{1,0},{2,1},{3,2},{4,3},{5,4},{6,5},{7,6},{8,7},{9,8},{10,9},{11,1... | collective-permute-start | bytes 221192 | tf_op jit(solution)/shard_map/ppermute | solution.py:12
  26.1 1.1 copy.174
  27.4 2.5 %collective-permute-done.1 = f32[3,48,1,128]{1,3,2,0:T(8,128)} collective-permute-done((f32[3,48,1,128]{1,3,2,0:T(8,128)}, f32[3,48,1,128]{1,3,2,0:T(8,128)}, u32[]{:S(2)}, u32[]{:S(2)}) %collective-permute-start.1) | collective-permute-done | bytes 73760 | tf_op jit(solution)/shard_map/ppermute | solution.py:12
  30.9 1.1 %fusion.16 = (f32[128]{0:T(128)}, f32[48,8,128]{0,2,1:T(8,128)S(1)}, f32[48,8,128]{0,2,1:T(8,128)S(1)}) fusion(bf16[1,1,48,8,128]{2,4,3,1,0:T(8,128)(2,1)S(1)} %copy.174, f32[128]{0:T(128)S(1)} %get-tuple-element.110, f32[48,8,128]{0,2,1:T(8,128)S(1)} %get-tuple-element.106, f32[48,8,127]{0,2,1:T(8,128)S(1)} %slice.448, ...), kind=kLoop, calls=%fused_computation.32 | loop fusion | flops 737152 | bytes 2259456 | tf_op jit(solution)/shard_map/reduce_sum | solution.py:84
  34.4 6.7 %collective-permute-start.2 = (f32[3,48,1,128]{1,3,2,0:T(8,128)}, f32[3,48,1,128]{1,3,2,0:T(8,128)}, u32[]{:S(2)}, u32[]{:S(2)}) collective-permute-start(f32[3,48,1,128]{1,3,2,0:T(8,128)} %pad_maximum_fusion.2), channel_id=1, source_target_pairs={{0,1},{1,2},{2,3},{3,4},{4,5},{5,6},{6,7},{7,8},{8,9},{9,10},{10,1... | collective-permute-start | bytes 221192 | tf_op jit(solution)/shard_map/ppermute | solution.py:12
  41.1 1.1 copy.172
  42.1 1.7 %copy.173 = bf16[1,1,48,8,128]{2,4,3,1,0:T(8,128)(2,1)} copy(bf16[1,1,48,8,128]{4,3,2,1,0:T(8,128)(2,1)} %get-tuple-element.84) | data formatting | bytes 196608
  43.9 1.7 %copy.175 = bf16[1,1,48,8,128]{2,4,3,1,0:T(8,128)(2,1)} copy(bf16[1,1,48,8,128]{4,3,2,1,0:T(8,128)(2,1)} %get-tuple-element.82) | data formatting | bytes 196608
  53.9 1.3 %collective-permute-start.3 = (f32[3,48,1,128]{1,3,2,0:T(8,128)}, f32[3,48,1,128]{1,3,2,0:T(8,128)}, u32[]{:S(2)}, u32[]{:S(2)}) collective-permute-start(f32[3,48,1,128]{1,3,2,0:T(8,128)} %pad_maximum_fusion.3), channel_id=1, source_target_pairs={{1,0},{2,1},{3,2},{4,3},{5,4},{6,5},{7,6},{8,7},{9,8},{10,9},{11,1... | collective-permute-start | bytes 221192 | tf_op jit(solution)/shard_map/ppermute | solution.py:12
  58.9 1.7 %constant_dynamic-update-slice_fusion.6 = f32[8,48,8,128]{3,2,1,0:T(8,128)} fusion(f32[8,48,8,128]{3,2,1,0:T(8,128)} %constant_dynamic-update-slice_fusion.7, f32[1,48,8,128]{3,2,1,0:T(8,128)} %copy.145), kind=kLoop, calls=%fused_computation.116 | loop fusion | bytes 393216
  60.6 1.6 %constant_dynamic-update-slice_fusion.5 = f32[8,48,8,128]{3,2,1,0:T(8,128)} fusion(f32[8,48,8,128]{3,2,1,0:T(8,128)} %constant_dynamic-update-slice_fusion.6, f32[1,48,8,128]{3,2,1,0:T(8,128)} %copy.146), kind=kLoop, calls=%fused_computation.115 | loop fusion | bytes 393216
  62.9 1.5 %slice_bitcast_fusion = (f32[48,1,128]{0,2,1:T(8,128)}, f32[48,1,128]{0,2,1:T(8,128)S(1)}, f32[48,1,128]{0,2,1:T(8,128)S(1)}) fusion(f32[3,48,1,128]{1,3,2,0:T(8,128)} %collective-permute-done.3), kind=kLoop, calls=%fused_computation.70 | loop fusion | bytes 147456 | tf_op jit(solution)/shard_map/squeeze | solution.py:121
  64.5 2.9 %fusion.15 = (f32[128]{0:T(128)S(1)}, f32[48,8,128]{0,2,1:T(8,128)}, f32[48,8,128]{0,2,1:T(8,128)}) fusion(bf16[1,1,48,8,128]{2,4,3,1,0:T(8,128)(2,1)S(1)} %copy-done.29, f32[128]{0:T(128)} %copy-done.34, f32[48,8,128]{0,2,1:T(8,128)S(1)} %get-tuple-element.66, f32[48,8,128]{0,2,1:T(8,128)S(1)} %get-tuple-element.104, f32[48,8,127]{0,2,1:T(8,128)S(1)} %copy-done.22, ...), kind=kLoop, calls=%fused_computation.30 | loop fusion | flops 737152 | bytes 2259456 | tf_op jit(solution)/shard_map/reduce_sum | solution.py:84
  67.5 33.5 %psum.7 = f32[2,128]{1,0:T(2,128)S(1)} all-reduce(f32[2,128]{1,0:T(2,128)S(1)} %pad_maximum_fusion.4), channel_id=1, replica_groups=mesh['groups'=2,'gx'=16] {'gx'}, use_global_device_ids=true, to_apply=%region_4.5 | all-reduce | flops 256 | bytes 2048 | tf_op jit(solution)/shard_map/psum | solution.py:123
  101.7 3.2 %subtract_bitcast_fusion = (f32[1,48,8,128]{1,3,2,0:T(8,128)}, f32[1,48,8,128]{1,3,2,0:T(8,128)}, f32[1,48,8,128]{1,3,2,0:T(8,128)S(1)}) fusion(f32[48,8,128]{0,2,1:T(8,128)S(1)} %copy-done.7, f32[48,8,128]{0,2,1:T(8,128)} %get-tuple-element.64, f32[128]{0:T(128)S(1)} %get-tuple-element.111, f32[128]{0:T(128)} %copy-done.36, f32[128]{0:T(128)S(1)} %get-tuple-element.108, ...), kind=kLoop, calls=%fused_computation.53 | loop fusion | flops 983040 | bytes 2554880 | tf_op jit(solution)/shard_map/stack | solution.py:129
  104.9 1.3 %copy.148 = f32[1,48,8,128]{3,2,1,0:T(8,128)S(1)} copy(f32[1,48,8,128]{1,3,2,0:T(8,128)} %get-tuple-element.69) | data formatting | bytes 393216 | tf_op jit(solution)/shard_map/stack | solution.py:129
  106.2 1.2 %copy.149 = f32[1,48,8,128]{3,2,1,0:T(8,128)S(1)} copy(f32[1,48,8,128]{1,3,2,0:T(8,128)} %get-tuple-element.68) | data formatting | bytes 393216 | tf_op jit(solution)/shard_map/stack | solution.py:129
  (158 shorter events, 31.8 us)
Async XLA Ops:
  0.6 8.2 %copy-start = (f32[16,2,2,256]{3,2,1,0:T(2,128)S(1)}, f32[16,2,2,256]{3,2,1,0:T(2,128)}, u32[]{:S(2)}) copy-start(f32[16,2,2,256]{3,2,1,0:T(2,128)} %param.20) | copy-start | bytes 196612
  2.2 4.5 %copy-start.33 = (f32[4,128]{1,0:T(4,128)S(1)}, f32[4,128]{1,0:T(4,128)}, u32[]{:S(2)}) copy-start(f32[4,128]{1,0:T(4,128)} %param.17) | copy-start | bytes 6148
  2.5 6.3 %copy-start.39 = (s32[48]{0:T(128)S(1)}, s32[48]{0:T(128)}, u32[]{:S(2)}) copy-start(s32[48]{0:T(128)} %param.21) | copy-start | bytes 580
  2.5 6.3 %copy-start.37 = (s32[256]{0:T(256)S(1)}, s32[256]{0:T(256)}, u32[]{:S(2)}) copy-start(s32[256]{0:T(256)} %param.19) | copy-start | bytes 3076
  2.7 7.8 %copy-start.35 = (f32[4,128]{1,0:T(4,128)S(1)}, f32[4,128]{1,0:T(4,128)}, u32[]{:S(2)}) copy-start(f32[4,128]{1,0:T(4,128)} %param.18) | copy-start | bytes 6148
  3.0 17.2 %copy-start.13 = (f32[1,48,8,128]{1,3,2,0:T(8,128)}, f32[1,48,8,128]{1,3,2,0:T(8,128)S(1)}, u32[]{:S(2)}) copy-start(f32[1,48,8,128]{1,3,2,0:T(8,128)S(1)} %copy.163) | copy-start | bytes 589828
  3.8 15.5 %collective-permute-start = (f32[3,48,1,128]{1,3,2,0:T(8,128)}, f32[3,48,1,128]{1,3,2,0:T(8,128)}, u32[]{:S(2)}, u32[]{:S(2)}) collective-permute-start(f32[3,48,1,128]{1,3,2,0:T(8,128)} %pad_maximum_fusion), channel_id=1, source_target_pairs={{0,1},{1,2},{2,3},{3,4},{4,5},{5,6},{6,7},{7,8},{8,9},{9,10},{10,1... | collective-permute-start | bytes 221192 | tf_op jit(solution)/shard_map/ppermute | solution.py:12
  10.6 20.3 %copy-start.34 = (f32[128]{0:T(128)}, f32[128]{0:T(128)S(1)}, u32[]{:S(2)}) copy-start(f32[128]{0:T(128)S(1)} %get-tuple-element.110) | copy-start | bytes 1540
  13.2 7.0 %copy-start.11 = (f32[1,48,8,128]{1,3,2,0:T(8,128)}, f32[1,48,8,128]{1,3,2,0:T(8,128)S(1)}, u32[]{:S(2)}) copy-start(f32[1,48,8,128]{1,3,2,0:T(8,128)S(1)} %copy.168) | copy-start | bytes 589828
  22.9 7.9 %copy-start.1 = (f32[48,8,128]{0,2,1:T(8,128)}, f32[48,8,128]{0,2,1:T(8,128)S(1)}, u32[]{:S(2)}) copy-start(f32[48,8,128]{0,2,1:T(8,128)S(1)} %get-tuple-element.58) | copy-start | bytes 589828
  24.8 5.2 %collective-permute-start.1 = (f32[3,48,1,128]{1,3,2,0:T(8,128)}, f32[3,48,1,128]{1,3,2,0:T(8,128)}, u32[]{:S(2)}, u32[]{:S(2)}) collective-permute-start(f32[3,48,1,128]{1,3,2,0:T(8,128)} %pad_maximum_fusion.1), channel_id=1, source_target_pairs={{1,0},{2,1},{3,2},{4,3},{5,4},{6,5},{7,6},{8,7},{9,8},{10,9},{11,1... | collective-permute-start | bytes 221192 | tf_op jit(solution)/shard_map/ppermute | solution.py:12
  26.1 6.0 %copy-start.36 = (f32[128]{0:T(128)}, f32[128]{0:T(128)S(1)}, u32[]{:S(2)}) copy-start(f32[128]{0:T(128)S(1)} %broadcast_multiply_fusion) | copy-start | bytes 1540
  32.8 13.9 %copy-start.6 = (f32[48,8,128]{0,2,1:T(8,128)}, f32[48,8,128]{0,2,1:T(8,128)S(1)}, u32[]{:S(2)}) copy-start(f32[48,8,128]{0,2,1:T(8,128)S(1)} %get-tuple-element.70) | copy-start | bytes 589828
  33.6 12.0 %copy-start.9 = (f32[48,8,128]{0,2,1:T(8,128)S(1)}, f32[48,8,128]{0,2,1:T(8,128)}, u32[]{:S(2)}) copy-start(f32[48,8,128]{0,2,1:T(8,128)} %copy-done.8) | copy-start | bytes 589828
  34.4 11.4 %collective-permute-start.2 = (f32[3,48,1,128]{1,3,2,0:T(8,128)}, f32[3,48,1,128]{1,3,2,0:T(8,128)}, u32[]{:S(2)}, u32[]{:S(2)}) collective-permute-start(f32[3,48,1,128]{1,3,2,0:T(8,128)} %pad_maximum_fusion.2), channel_id=1, source_target_pairs={{0,1},{1,2},{2,3},{3,4},{4,5},{5,6},{6,7},{7,8},{8,9},{9,10},{10,1... | collective-permute-start | bytes 221192 | tf_op jit(solution)/shard_map/ppermute | solution.py:12
  47.9 7.2 %copy-start.17 = (f32[48,8,128]{0,2,1:T(8,128)}, f32[48,8,128]{0,2,1:T(8,128)S(1)}, u32[]{:S(2)}) copy-start(f32[48,8,128]{0,2,1:T(8,128)S(1)} %get-tuple-element.53) | copy-start | bytes 589828
  53.2 4.6 %copy-start.16 = (f32[48,8,128]{0,2,1:T(8,128)S(1)}, f32[48,8,128]{0,2,1:T(8,128)}, u32[]{:S(2)}) copy-start(f32[48,8,128]{0,2,1:T(8,128)} %copy-done.15) | copy-start | bytes 589828
  53.9 9.0 %collective-permute-start.3 = (f32[3,48,1,128]{1,3,2,0:T(8,128)}, f32[3,48,1,128]{1,3,2,0:T(8,128)}, u32[]{:S(2)}, u32[]{:S(2)}) collective-permute-start(f32[3,48,1,128]{1,3,2,0:T(8,128)} %pad_maximum_fusion.3), channel_id=1, source_target_pairs={{1,0},{2,1},{3,2},{4,3},{5,4},{6,5},{7,6},{8,7},{9,8},{10,9},{11,1... | collective-permute-start | bytes 221192 | tf_op jit(solution)/shard_map/ppermute | solution.py:12
  57.8 6.7 %copy-start.29 = (bf16[1,1,48,8,128]{2,4,3,1,0:T(8,128)(2,1)S(1)}, bf16[1,1,48,8,128]{2,4,3,1,0:T(8,128)(2,1)}, u32[]{:S(2)}) copy-start(bf16[1,1,48,8,128]{2,4,3,1,0:T(8,128)(2,1)} %copy.175) | copy-start | bytes 294916
  58.8 5.6 %copy-start.19 = (f32[48,8,128]{0,2,1:T(8,128)S(1)}, f32[48,8,128]{0,2,1:T(8,128)}, u32[]{:S(2)}) copy-start(f32[48,8,128]{0,2,1:T(8,128)} %copy-done.17) | copy-start | bytes 589828
  58.8 5.6 %copy-start.22 = (f32[48,8,127]{0,2,1:T(8,128)S(1)}, f32[48,8,127]{0,2,1:T(8,128)}, u32[]{:S(2)}) copy-start(f32[48,8,127]{0,2,1:T(8,128)} %slice.476) | copy-start | bytes 585220
  58.8 5.6 %copy-start.23 = (f32[48,7,128]{0,2,1:T(8,128)S(1)}, f32[48,7,128]{0,2,1:T(8,128)}, u32[]{:S(2)}) copy-start(f32[48,7,128]{0,2,1:T(8,128)} %slice.471) | copy-start | bytes 516100
  64.5 37.2 %copy-start.7 = (f32[48,8,128]{0,2,1:T(8,128)S(1)}, f32[48,8,128]{0,2,1:T(8,128)}, u32[]{:S(2)}) copy-start(f32[48,8,128]{0,2,1:T(8,128)} %copy-done.6) | copy-start | bytes 589828
  64.5 37.2 %copy-start.10 = (f32[48,8,128]{0,2,1:T(8,128)S(1)}, f32[48,8,128]{0,2,1:T(8,128)}, u32[]{:S(2)}) copy-start(f32[48,8,128]{0,2,1:T(8,128)} %copy-done.8) | copy-start | bytes 589828
  (20 other events, 47.4 us)
where the time goes:
time: 112 us; the launch traced here: 111 us
  local copies, waits for them, and re-layouts  43.6 us (39%)
  blocking collectives  33.5 us (30%)
  other arithmetic  16.9 us (15%)
  starting transfers between devices  12.3 us (11%)
  waiting for transfers between devices  2.49 us (2%)
  between operations  1.4 us (1%)
    psum x1, blocking collectives, shards(): totals = lax.psum(jnp.stack([perm_part, poro_part]), 'gx')  33.5 us
    unnamed x101, local copies, waits for them, and re-layouts  21.5 us
    ppermute x4, starting transfers between devices, passed_along(): return lax.ppermute(block, axis, route)  12.3 us
    another operation x9, local copies, waits for them, and re-layouts, shards(): return (jnp.stack(fields), gradients)  5.68 us
    reduce_sum x2, other arithmetic, pressure_term(): jnp.sum(fields[7] * forward_fields[step_index, 2].astype(jnp.float32), ax...  4.09 us
    reduce_sum x2, other arithmetic, flow_term(): return jnp.sum(flow_prod, axis=(0, 1))  3.57 us
    another operation x1, other arithmetic, shards(): return (jnp.stack(fields), gradients)  3.22 us
    slice x6, local copies, waits for them, and re-layouts, depth_upper(): values[:, :, 1:]  2.66 us
  transfers between devices with their start and end apart: 4, of which 1 were waited for; matrix products, arithmetic and copies ran while one was open for 23% of the time, Pallas kernels for 0%

commit v1 on v0

v1 whole, which is shorter than its diff:
```python
import functools

import jax
import jax.numpy as jnp
from jax import lax
from jax.experimental import pallas as pl
from jax.experimental.pallas import tpu as pltpu
from jax.sharding import PartitionSpec as P

LAYER = 8
FIELDS = 8
VX, VZ, QX, QZ, SXX, SZZ, SXZ, PR = range(FIELDS)
HALO = 6
EXACT = lax.Precision.HIGHEST


def depth_lower(values):
    lane = lax.broadcasted_iota(jnp.int32, values.shape, 1)
    return values - jnp.where(lane == 0, 0.0, pltpu.roll(values, 1, 1))


def depth_upper(values):
    depth = values.shape[1]
    lane = lax.broadcasted_iota(jnp.int32, values.shape, 1)
    return jnp.where(lane == depth - 1, 0.0, pltpu.roll(values, depth - 1, 1)) - values


def row_lower(values):
    row = lax.broadcasted_iota(jnp.int32, values.shape, 0)
    return values - jnp.where(row == 0, 0.0, pltpu.roll(values, 1, 0))


def row_upper(values):
    rows = values.shape[0]
    row = lax.broadcasted_iota(jnp.int32, values.shape, 0)
    return jnp.where(row == rows - 1, 0.0, pltpu.roll(values, rows - 1, 0)) - values


def velocity_gain(coeffs, force_x, force_z, push_x, push_z):
    solid, couple, fluid, _ = coeffs
    return (
        solid * force_x + couple * push_x,
        solid * force_z + couple * push_z,
        -couple * force_x - fluid * push_x,
        -couple * force_z - fluid * push_z,
    )


def stress_gain(coeffs, strain_x, strain_z, inflow, shear):
    lame, modulus, coupling, fluid = coeffs
    dilation = strain_x + strain_z
    common = lame * dilation - coupling * inflow
    return (
        common + 2.0 * modulus * strain_x,
        common + 2.0 * modulus * strain_z,
        modulus * shear,
        -coupling * dilation - fluid * inflow,
    )


def beyond_gain(coeffs, vel_x, vel_z, flow_x):
    lame, modulus, coupling, fluid = coeffs
    return (
        (lame + 2.0 * modulus) * vel_x - coupling * flow_x,
        lame * vel_x - coupling * flow_x,
        modulus * vel_z,
        -coupling * vel_x - fluid * flow_x,
    )


def plus(left, right):
    return tuple(a + b for a, b in zip(left, right))


def minus(left, right):
    return tuple(a - b for a, b in zip(left, right))


def load_coeffs(ref):
    return tuple(ref[pl.ds(i, 1), :] for i in range(4))


def edge_kernel(
    sizes,
    state_hbm,
    forward_hbm,
    vel_hbm,
    stress_hbm,
    cells_hbm,
    force_hbm,
    source_hbm,
    state,
    forward,
    forcing,
    message_core,
    message_chip,
    vel_ref,
    stress_ref,
    cells,
    force,
    by_source,
    source,
    sems,
):
    events, rows, depth, steps, sources = sizes
    copies = [
        pltpu.make_async_copy(src, dst, sems.at[i])
        for i, (src, dst) in enumerate(
            [
                (cells_hbm, cells),
                (force_hbm, force),
                (source_hbm, source),
                (vel_hbm, vel_ref),
                (stress_hbm, stress_ref),
                (state_hbm, state),
                (forward_hbm, forward),
            ]
        )
    ]
    for copy in copies:
        copy.start()
    copies[0].wait()
    copies[1].wait()
    lanes = cells.shape[1]
    local = cells[...] & (rows * depth - 1)
    slot = (local // depth) * LAYER + (local & (depth - 1)) - (depth - LAYER)
    layers = None
    for block in range(cells.shape[0]):
        spots = lax.broadcasted_iota(jnp.int32, (depth, lanes), 0)
        hit = (spots == slot[block : block + 1, :]).astype(jnp.float32)
        part = lax.dot_general(
            force[...],
            hit,
            (((1,), (1,)), ((), ())),
            precision=EXACT,
            preferred_element_type=jnp.float32,
        )
        if block:
            part = pltpu.roll(part, part.shape[0] - 2 * block, 0)
        layers = part if layers is None else layers + part
    lane = lax.broadcasted_iota(jnp.int32, layers.shape, 1)
    for row in range(rows):
        moved = pltpu.roll(layers, (depth - LAYER - LAYER * row) % depth, 1)
        by_source[pl.ds(row, layers.shape[0], stride=rows), :] = jnp.where(
            lane >= depth - LAYER, moved, 0.0
        )
    copies[2].wait()
    blocks = cells.shape[0]
    for event in range(events):
        record = source[event]
        for step in range(steps):
            for part in range(2):
                at = (record * steps + step) * 2 * blocks + part
                forcing[pl.ds(((step * 2 + part) * events + event) * rows, rows), :] = by_source[
                    pl.ds(pl.multiple_of(at * rows, rows), rows), :
                ]
    for copy in copies[3:6]:
        copy.wait()
    vel = load_coeffs(vel_ref)
    stress = load_coeffs(stress_ref)
    odd = lax.rem(lax.axis_index("gx"), 2) == 1
    last = rows - 1

    def rim(chunk, field, row):
        return state[pl.ds((field * events + chunk) * rows + row, 8, stride=rows), :]

    def pushed(chunk, step, part, row):
        return forcing[
            pl.ds(((step * 2 + part) * events + chunk) * rows + row, 8, stride=rows), :
        ]

    for chunk in range(0, events, 8):
        first = [rim(chunk, f, 0) for f in range(FIELDS)]
        second = [rim(chunk, f, 1) for f in range(FIELDS)]
        final = [rim(chunk, f, last) for f in range(FIELDS)]
        inner = {f: rim(chunk, f, last - 1) for f in (SXX, SXZ, PR)}

        def kicked(fields, gains, step, row):
            vel_x, vel_z, flow_x, flow_z = plus(fields, gains)
            return (
                vel_x + pushed(chunk, step, 0, row),
                vel_z + pushed(chunk, step, 1, row),
                flow_x,
                flow_z,
            )

        def forces(fields, before):
            return (
                fields[SXX] - before[SXX] + depth_lower(fields[SXZ]),
                fields[SXZ] - before[SXZ] + depth_lower(fields[SZZ]),
                fields[PR] - before[PR] + vel[3] * fields[QX],
                depth_lower(fields[PR]) + vel[3] * fields[QZ],
            )

        nothing = {SXX: 0.0, SXZ: 0.0, PR: 0.0}
        vel_first = kicked(first[:4], velocity_gain(vel, *forces(first, nothing)), 0, 0)
        vel_second = kicked(second[:4], velocity_gain(vel, *forces(second, first)), 0, 1)
        vel_final = kicked(final[:4], velocity_gain(vel, *forces(final, inner)), 0, last)
        stress_first = plus(
            first[4:],
            stress_gain(
                stress,
                vel_second[0] - vel_first[0],
                depth_upper(vel_first[1]),
                vel_second[2] - vel_first[2] + depth_upper(vel_first[3]),
                depth_upper(vel_first[0]) + vel_second[1] - vel_first[1],
            ),
        )
        stress_final = plus(
            final[4:],
            stress_gain(
                stress,
                -vel_final[0],
                depth_upper(vel_final[1]),
                -vel_final[2] + depth_upper(vel_final[3]),
                depth_upper(vel_final[0]) - vel_final[1],
            ),
        )
        again = kicked(
            vel_first,
            velocity_gain(vel, *forces(list(vel_first) + list(stress_first), nothing)),
            1,
            0,
        )
        right = [final[SXX], final[SXZ], final[PR], stress_final[0], stress_final[2], stress_final[3]]
        left = [vel_first[0], vel_first[1], vel_first[2], again[0], again[1], again[2]]
        for i in range(HALO):
            at = pl.ds(i * events + chunk, 8)
            message_core[at, :] = jnp.where(odd, left[i], right[i])
            message_chip[at, :] = jnp.where(odd, right[i], left[i])
    copies[6].wait()


def bulk_kernel(
    sizes, state_in, forward, forcing, vel_ref, stress_ref, state, weights, sums
):
    events, rows, depth, steps, _ = sizes
    vel = tuple(jnp.broadcast_to(c, (rows, depth)) for c in load_coeffs(vel_ref))
    stress = tuple(jnp.broadcast_to(c, (rows, depth)) for c in load_coeffs(stress_ref))
    pair = 2

    def body(i, carry):
        perm, poro = carry
        for sub in range(pair):
            event = i * pair + sub

            def tile(kind):
                return pl.ds(pl.multiple_of((kind * events + event) * rows, rows), rows)

            fields = [state_in[tile(f), :] for f in range(FIELDS)]
            for step in range(steps):
                factors = []
                for kind in range(3):
                    at = (step * 3 + kind) * events * rows
                    both = forward[pl.ds(pl.multiple_of(at + i * pair * rows, pair * rows), pair * rows), :]
                    value = both.astype(jnp.float32)[sub * rows : (sub + 1) * rows, :]
                    weights[tile(step * 3 + kind), :] = value
                    factors.append(value)
                gains = velocity_gain(
                    vel,
                    row_lower(fields[SXX]) + depth_lower(fields[SXZ]),
                    row_lower(fields[SXZ]) + depth_lower(fields[SZZ]),
                    row_lower(fields[PR]) + vel[3] * fields[QX],
                    depth_lower(fields[PR]) + vel[3] * fields[QZ],
                )
                fields[:4] = plus(fields[:4], gains)
                fields[VX] = fields[VX] + forcing[tile(step * 2), :]
                fields[VZ] = fields[VZ] + forcing[tile(step * 2 + 1), :]
                perm = perm + fields[QX] * factors[0] + fields[QZ] * factors[1]
                fields[4:] = plus(
                    fields[4:],
                    stress_gain(
                        stress,
                        row_upper(fields[VX]),
                        depth_upper(fields[VZ]),
                        row_upper(fields[QX]) + depth_upper(fields[QZ]),
                        depth_upper(fields[VX]) + row_upper(fields[VZ]),
                    ),
                )
                poro = poro + fields[PR] * factors[2]
            for f in range(FIELDS):
                state[tile(f), :] = fields[f]
        return perm, poro

    zero = jnp.zeros((rows, depth), jnp.float32)
    perm, poro = lax.fori_loop(0, events // pair, body, (zero, zero))
    sums[pl.ds(0, rows), :] = perm
    sums[pl.ds(rows, rows), :] = poro


def join_kernel(
    sizes,
    normalizer,
    state_in,
    weights,
    sums,
    sent_core,
    sent_chip,
    got_core,
    got_chip,
    vel_ref,
    stress_ref,
    state,
    totals,
):
    events, rows, depth, _, _ = sizes
    vel = load_coeffs(vel_ref)
    stress = load_coeffs(stress_ref)
    place = lax.axis_index("gx")
    odd = lax.rem(place, 2) == 1
    has_left = place > 0
    has_right = place < lax.axis_size("gx") - 1
    last = rows - 1
    perm = sums[pl.ds(0, rows), :]
    poro = sums[pl.ds(rows, rows), :]

    def forces(stresses, flows):
        return (
            stresses[0] + depth_lower(stresses[2]),
            stresses[2] + depth_lower(stresses[1]),
            stresses[3] + vel[3] * flows[0],
            depth_lower(stresses[3]) + vel[3] * flows[1],
        )

    def from_before(stress_x, stress_xz, pressure):
        return velocity_gain(vel, -stress_x, -stress_xz, -pressure, 0.0)

    def strains(vels, after):
        return stress_gain(
            stress,
            after[0] - vels[0],
            depth_upper(vels[1]),
            after[2] - vels[2] + depth_upper(vels[3]),
            depth_upper(vels[0]) + after[1] - vels[1],
        )

    for chunk in range(0, events, 8):

        def row_of(ref, i):
            return ref[pl.ds(i * events + chunk, 8), :]

        own_core = [row_of(sent_core, i) for i in range(HALO)]
        own_chip = [row_of(sent_chip, i) for i in range(HALO)]
        new_core = [row_of(got_core, i) for i in range(HALO)]
        new_chip = [row_of(got_chip, i) for i in range(HALO)]
        left_own = [jnp.where(odd, a, b) for a, b in zip(own_core, own_chip)]
        right_own = [jnp.where(odd, b, a) for a, b in zip(own_core, own_chip)]
        left = [jnp.where(has_left, jnp.where(odd, a, b), 0.0) for a, b in zip(new_core, new_chip)]
        right = [jnp.where(has_right, jnp.where(odd, b, a), 0.0) for a, b in zip(new_core, new_chip)]

        gain_first = from_before(*left[:3])
        true_first = plus(left_own[:3], gain_first[:3])
        before = beyond_gain(stress, *true_first)
        before = [
            jnp.where(has_left, a + b, 0.0)
            for a, b in zip(left[3:], (before[0], before[2], before[3]))
        ]
        nothing = (0.0, 0.0, 0.0)
        stress_first = strains(gain_first, nothing)
        gain_after = from_before(*right_own[:3])
        after = plus(right[:3], gain_after[:3])
        after = [jnp.where(has_right, a, 0.0) for a in after]
        stress_last = beyond_gain(stress, *after)
        true_last = plus(right_own[3:], (stress_last[0], stress_last[2], stress_last[3]))

        vel_first = plus(
            plus(gain_first, velocity_gain(vel, *forces(stress_first, gain_first[2:]))),
            from_before(*before),
        )
        vel_second = from_before(stress_first[0], stress_first[2], stress_first[3])
        vel_last = velocity_gain(
            vel,
            stress_last[0] + depth_lower(stress_last[2]),
            stress_last[2] + depth_lower(stress_last[1]),
            stress_last[3],
            depth_lower(stress_last[3]),
        )
        stress_after = strains(gain_after, nothing)
        again = plus(
            plus(gain_after, velocity_gain(vel, *forces(stress_after, gain_after[2:]))),
            from_before(*true_last),
        )
        again = [jnp.where(has_right, a + b, 0.0) for a, b in zip(right[3:], again)]
        end_first = plus(stress_first, strains(vel_first, vel_second))
        end_second = strains(vel_second, nothing)
        end_inner = beyond_gain(stress, *vel_last[:3])
        end_last = plus(stress_last, strains(vel_last, again))

        def factor(step, kind, row):
            return weights[pl.ds(((step * 3 + kind) * events + chunk) * rows + row, 8, stride=rows), :]

        perm = perm + gain_first[2] * factor(0, 0, 0) + gain_first[3] * factor(0, 1, 0)
        for row, vels in ((0, vel_first), (1, vel_second), (last, vel_last)):
            perm = perm + vels[2] * factor(1, 0, row) + vels[3] * factor(1, 1, row)
        poro = poro + stress_first[3] * factor(0, 2, 0) + stress_last[3] * factor(0, 2, last)
        ends = ((0, end_first), (1, end_second), (last - 1, end_inner), (last, end_last))
        for row, stresses in ends:
            poro = poro + stresses[3] * factor(1, 2, row)

        changes = [(0, 0, vel_first), (1, 0, vel_second), (last, 0, vel_last)]
        changes += [(row, 4, stresses) for row, stresses in ends]
        for row, start, values in changes:
            for i, value in enumerate(values):
                at = pl.ds(((start + i) * events + chunk) * rows + row, 8, stride=rows)
                state[at, :] = state_in[at, :] + value

    perm = jnp.sum(perm, axis=0, keepdims=True) * (vel[2] * vel[3] * normalizer)
    poro = jnp.sum(poro, axis=0, keepdims=True) * (stress[3] * normalizer)
    totals[pl.ds(0, 1), :] = perm
    totals[pl.ds(1, 1), :] = poro


def swap_with(value, size, mask):
    return lax.ppermute(value, "gx", [(i, i ^ mask) for i in range(size)])


def swap_over_chips(value, groups, size):
    route = []
    for group in range(groups):
        base = group * size
        other = (group ^ 1) * size
        for i in range(1, size - 1, 2):
            route += [(base + i, base + i + 1), (base + i + 1, base + i)]
        route += [(base, other), (base + size - 1, other + size - 1)]
    return lax.ppermute(value, ("groups", "gx"), route)


def shards(
    adjoint_state, forward_fields, vel_coeffs, stress_coeffs, drm_cells, drm_force, source_id
):
    fields, events, rows, depth = adjoint_state.shape
    steps = forward_fields.shape[0]
    sources = drm_force.shape[0]
    entries = drm_cells.shape[0]
    size = lax.axis_size("gx")
    groups = lax.axis_size("groups")
    sizes = (events, rows, depth, steps, sources)
    blocks = entries // 128
    tiles = events * rows
    f32 = jnp.float32
    any_space = pl.BlockSpec(memory_space=pl.ANY)
    vmem = pl.BlockSpec(memory_space=pltpu.VMEM)
    state = adjoint_state.reshape(fields * tiles, depth)
    forward = forward_fields.reshape(steps * 3 * tiles, depth)
    cells = drm_cells.reshape(blocks, 128)
    force = drm_force.reshape(sources * steps, 2, blocks, 128).transpose(0, 2, 1, 3)
    force = force.reshape(sources * steps * 2 * blocks, 128)
    message = jax.ShapeDtypeStruct((HALO * events, depth), f32)

    state, forward, forcing, message_core, message_chip = pl.pallas_call(
        functools.partial(edge_kernel, sizes),
        out_shape=(
            pltpu.VMEM(state.shape, f32),
            pltpu.VMEM(forward.shape, forward.dtype),
            pltpu.VMEM((steps * 2 * tiles, depth), f32),
            message,
            message,
        ),
        in_specs=[any_space] * 7,
        out_specs=(vmem,) * 5,
        scratch_shapes=[
            pltpu.VMEM(vel_coeffs.shape, f32),
            pltpu.VMEM(stress_coeffs.shape, f32),
            pltpu.VMEM(cells.shape, jnp.int32),
            pltpu.VMEM(force.shape, f32),
            pltpu.VMEM((force.shape[0] * rows, depth), f32),
            pltpu.SMEM(source_id.shape, jnp.int32),
            pltpu.SemaphoreType.DMA((7,)),
        ],
        name="edges",
    )(state, forward, vel_coeffs, stress_coeffs, cells, force, source_id)

    got_chip = swap_over_chips(message_chip, groups, size)
    got_core = swap_with(message_core, size, 1)

    state, weights, sums = pl.pallas_call(
        functools.partial(bulk_kernel, sizes),
        out_shape=(
            pltpu.VMEM(state.shape, f32),
            pltpu.VMEM((steps * 3 * tiles, depth), f32),
            pltpu.VMEM((2 * rows, depth), f32),
        ),
        in_specs=[vmem] * 5,
        out_specs=(vmem,) * 3,
        input_output_aliases={0: 0},
        cost_estimate=pl.CostEstimate(
            flops=steps * 80 * tiles * depth, bytes_accessed=8 * state.size, transcendentals=0
        ),
        name="bulk",
    )(state, forward, forcing, vel_coeffs, stress_coeffs)

    normalizer = (events * rows * size) ** (-0.5)
    state, totals = pl.pallas_call(
        functools.partial(join_kernel, sizes, normalizer),
        out_shape=(
            pltpu.VMEM(state.shape, f32),
            jax.ShapeDtypeStruct((2, depth), f32),
        ),
        in_specs=[vmem] * 9,
        out_specs=(vmem,) * 2,
        input_output_aliases={0: 0},
        name="join",
    )(
        state,
        weights,
        sums,
        message_core,
        message_chip,
        got_core,
        got_chip,
        vel_coeffs,
        stress_coeffs,
    )
    mask = 1
    while mask < size:
        totals = totals + swap_with(totals, size, mask | 1)
        mask *= 2
    return state.reshape(adjoint_state.shape), totals


def solution(mesh):
    in_specs = (
        P(None, "groups", "gx", None),
        P(None, None, "groups", "gx", None),
        P("groups", None),
        P("groups", None),
        P("gx"),
        P("groups", None, None, "gx"),
        P("groups"),
    )
    out_specs = (P(None, "groups", "gx", None), P("groups", None))
    return jax.shard_map(shards, mesh=mesh, in_specs=in_specs, out_specs=out_specs, check_vma=False)
```

time: 112 us -> 41.3 us (0.37)
  local copies, waits for them, and re-layouts: 43.6 us -> 5.13 us
  blocking collectives: 33.5 us -> 0 us
  Pallas kernels: 0 us -> 21 us
  other arithmetic: 16.9 us -> 1.25 us
  starting transfers between devices: 12.3 us -> 8.16 us
  waiting for transfers between devices: 2.49 us -> 4.88 us
    psum x1 -> x0, blocking collectives: 33.5 us -> none  [shards(): totals = lax.psum(jnp.stack([perm_part, poro_part]), 'gx')]
    pallas_call x0 -> x3, Pallas kernels: none -> 21 us  [the longest x1 15.7 us: shards(): pl.pallas_call(functools.partial(bulk_kernel, sizes), out_shape=(pltpu.VM...]
    unnamed x101 -> x13, local copies, waits for them, and re-layouts: 21.5 us -> 5.13 us
    slice x20 -> x0, local copies, waits for them, and re-layouts: 11.2 us -> none  [the longest x6 2.66 us: depth_upper(): values[:, :, 1:]]
    reduce_sum x4 -> x0, other arithmetic: 7.66 us -> none  [the longest x2 4.09 us: pressure_term(): jnp.sum(fields[7] * forward_fields[step_index, 2].astype(jnp.float32), ax...]
    another operation x6 -> x0, other arithmetic: 6.08 us -> none  [the longest x1 3.22 us: shards(): return (jnp.stack(fields), gradients)]
    another operation x20 -> x0, local copies, waits for them, and re-layouts: 5.75 us -> none  [the longest x9 5.68 us: shards(): return (jnp.stack(fields), gradients)]
    squeeze x4 -> x0, local copies, waits for them, and re-layouts: 4.37 us -> none  [the longest x2 2.46 us: shards(): beyond[1]]
  transfers between devices with their start and end apart: 4 -> 6, of which waited for: 1 -> 4; matrix products, arithmetic and copies ran while one was open for 23% -> 3% of each run, Pallas kernels for 0% -> 38%
where the time goes in v1:
time: 41.3 us; the launch traced here: 41.1 us
  Pallas kernels  21 us (51%)
  starting transfers between devices  8.16 us (20%)
  local copies, waits for them, and re-layouts  5.13 us (12%)
  waiting for transfers between devices  4.88 us (12%)
  other arithmetic  1.25 us (3%)
  between operations  0.68 us (2%)
    pallas_call x1, Pallas kernels, shards(): pl.pallas_call(functools.partial(bulk_kernel, sizes), out_shape=(pltpu.VM...  15.7 us
    ppermute x5, starting transfers between devices, swap_with(): return lax.ppermute(value, 'gx', [(i, i ^ mask) for i in range(size)])  5.67 us
    unnamed x13, local copies, waits for them, and re-layouts  5.13 us
    ppermute x5, waiting for transfers between devices, swap_with(): return lax.ppermute(value, 'gx', [(i, i ^ mask) for i in range(size)])  4.87 us
    pallas_call x1, Pallas kernels, shards(): pl.pallas_call(functools.partial(join_kernel, sizes, normalizer), out_sha...  2.68 us
    pallas_call x1, Pallas kernels, shards(): pl.pallas_call(functools.partial(edge_kernel, sizes), out_shape=(pltpu.VM...  2.6 us
    ppermute x1, starting transfers between devices, swap_over_chips(): return lax.ppermute(value, ('groups', 'gx'), route)  2.49 us
    add x4, other arithmetic, shards(): totals = totals + swap_with(totals, size, mask | 1)  1.25 us
  transfers between devices with their start and end apart: 6, of which 4 were waited for; matrix products, arithmetic and copies ran while one was open for 3% of the time, Pallas kernels for 38%

profile of v1, /device:TPU:0, one launch (start us, length us, event | category | flops | bytes accessed | tf_op | source)
XLA Modules:
  0.0 41.1 jit_solution(4495373433609499685)
XLA Ops:
  0.6 2.6 %edges.1 = (f32[3072,128]{1,0:T(8,128)S(1)}, bf16[2304,128]{1,0:T(8,128)(2,1)S(1)}, f32[1536,128]{1,0:T(8,128)S(1)}, f32[288,128]{1,0:T(8,128)}, f32[288,128]{1,0:T(8,128)}) custom-call(f32[3072,128]{1,0:T(8,128)} %bitcast.10, bf16[2304,128]{1,0:T(8,128)(2,1)} %bitcast.11, f32[4,128]{1,0:T(4,128)} %vel_ref.3, f32[4,128]{1,0:T(4,128)} %stress_ref.3, ...), custom_call_target="tpu_custom_call" | custom-call | tf_op jit(solution)/shard_map/edges/pallas_call | solution.py:450
  3.2 0.0 copy-start.1
  3.3 0.9 %copy-done.1 = f32[1536,128]{1,0:T(8,128)} copy-done((f32[1536,128]{1,0:T(8,128)}, f32[1536,128]{1,0:T(8,128)S(1)}, u32[]{:S(2)}) %copy-start.1) | copy-done | bytes 786456
  4.1 0.8 %copy-done.2 = bf16[2304,128]{1,0:T(8,128)(2,1)} copy-done((bf16[2304,128]{1,0:T(8,128)(2,1)}, bf16[2304,128]{1,0:T(8,128)(2,1)S(1)}, u32[]{:S(2)}) %copy-start.2) | copy-done | bytes 589848
  4.9 0.5 %collective-permute-start = (f32[288,128]{1,0:T(8,128)}, f32[288,128]{1,0:T(8,128)S(1)}, u32[]{:S(2)}, u32[]{:S(2)}) collective-permute-start(f32[288,128]{1,0:T(8,128)} %get-tuple-element.18.sent_core), channel_id=1, source_target_pairs={{0,1},{1,0},{2,3},{3,2},{4,5},{5,4},{6,7},{7,6},{8,9},{9,8},{10,11... | collective-permute-start | bytes 442376 | tf_op jit(solution)/shard_map/ppermute | solution.py:414
  5.4 2.5 %collective-permute-start.1 = (f32[288,128]{1,0:T(8,128)}, f32[288,128]{1,0:T(8,128)S(1)}, u32[]{:S(2)}, u32[]{:S(2)}) collective-permute-start(f32[288,128]{1,0:T(8,128)} %get-tuple-element.19.sent_chip), channel_id=1, source_target_pairs={{1,2},{2,1},{3,4},{4,3},{5,6},{6,5},{7,8},{8,7},{9,10},{10,9},{11,... | collective-permute-start | bytes 442376 | tf_op jit(solution)/shard_map/ppermute | solution.py:425
  7.9 15.7 %bulk.1 = (f32[3072,128]{1,0:T(8,128)S(1)}, f32[2304,128]{1,0:T(8,128)S(1)}, f32[16,128]{1,0:T(8,128)S(1)}) custom-call(f32[3072,128]{1,0:T(8,128)S(1)} %get-tuple-element.12.state_in, bf16[2304,128]{1,0:T(8,128)(2,1)} %copy-done.2, f32[1536,128]{1,0:T(8,128)} %copy-done.1, f32[4,128]{1,0:T(4,128)} %vel_ref.3, ...), custom_call_target="tpu_custom_call", output_to_operand_aliasing={{0}: (0, {})} | custom-call | flops 7864320 | bytes 3145728 | tf_op jit(solution)/shard_map/bulk/pallas_call | solution.py:476
  23.6 1.0 %copy-done = f32[2304,128]{1,0:T(8,128)} copy-done((f32[2304,128]{1,0:T(8,128)}, f32[2304,128]{1,0:T(8,128)S(1)}, u32[]{:S(2)}) %copy-start) | copy-done | bytes 1179672
  24.6 0.6 %copy-done.3 = f32[16,128]{1,0:T(8,128)} copy-done((f32[16,128]{1,0:T(8,128)}, f32[16,128]{1,0:T(8,128)S(1)}, u32[]{:S(2)}) %copy-start.3) | copy-done | bytes 8216
  25.2 0.0 collective-permute-done.1.got_chip
  25.3 0.6 %copy-done.4 = f32[288,128]{1,0:T(8,128)} copy-done((f32[288,128]{1,0:T(8,128)}, f32[288,128]{1,0:T(8,128)S(1)}, u32[]{:S(2)}) %copy-start.4) | copy-done | bytes 147480
  25.9 0.0 copy-done.5
  25.9 2.7 %join.1 = (f32[3072,128]{1,0:T(8,128)S(1)}, f32[2,128]{1,0:T(2,128)}) custom-call(f32[3072,128]{1,0:T(8,128)S(1)} %get-tuple-element.15.state_in, f32[2304,128]{1,0:T(8,128)} %copy-done, f32[16,128]{1,0:T(8,128)} %copy-done.3, f32[288,128]{1,0:T(8,128)} %get-tuple-element.18.sent_core, ...), custom_call_target="tpu_custom_call", output_to_operand_aliasing={{0}: (0, {})} | custom-call | tf_op jit(solution)/shard_map/join/pallas_call | solution.py:493
  28.6 0.1 collective-permute-start.2
  28.8 1.2 %collective-permute-done.2 = f32[2,128]{1,0:T(2,128)S(1)} collective-permute-done((f32[2,128]{1,0:T(2,128)}, f32[2,128]{1,0:T(2,128)S(1)}, u32[]{:S(2)}, u32[]{:S(2)}) %collective-permute-start.2) | collective-permute-done | bytes 1056 | tf_op jit(solution)/shard_map/ppermute | solution.py:414
  30.0 0.7 %add.12 = f32[2,128]{1,0:T(2,128)S(1)} add(f32[2,128]{1,0:T(2,128)} %get-tuple-element.21, f32[2,128]{1,0:T(2,128)S(1)} %collective-permute-done.2) | non-fusion elementwise | flops 256 | bytes 3072 | tf_op jit(solution)/shard_map/add | solution.py:516
  30.7 1.3 %collective-permute-start.3 = (f32[2,128]{1,0:T(2,128)S(1)}, f32[2,128]{1,0:T(2,128)S(1)}, u32[]{:S(2)}, u32[]{:S(2)}) collective-permute-start(f32[2,128]{1,0:T(2,128)S(1)} %add.12), channel_id=1, source_target_pairs={{0,3},{1,2},{2,1},{3,0},{4,7},{5,6},{6,5},{7,4},{8,11},{9,10},{10,... | collective-permute-start | bytes 3080 | tf_op jit(solution)/shard_map/ppermute | solution.py:414
  31.9 1.7 %collective-permute-done.3 = f32[2,128]{1,0:T(2,128)S(1)} collective-permute-done((f32[2,128]{1,0:T(2,128)S(1)}, f32[2,128]{1,0:T(2,128)S(1)}, u32[]{:S(2)}, u32[]{:S(2)}) %collective-permute-start.3) | collective-permute-done | bytes 1056 | tf_op jit(solution)/shard_map/ppermute | solution.py:414
  33.7 1.4 %collective-permute-start.4 = (f32[2,128]{1,0:T(2,128)S(1)}, f32[2,128]{1,0:T(2,128)S(1)}, u32[]{:S(2)}, u32[]{:S(2)}) collective-permute-start(f32[2,128]{1,0:T(2,128)S(1)} %add.13), channel_id=1, source_target_pairs={{0,5},{1,4},{2,7},{3,6},{4,1},{5,0},{6,3},{7,2},{8,13},{9,12},{10,... | collective-permute-start | bytes 3080 | tf_op jit(solution)/shard_map/ppermute | solution.py:414
  35.1 1.6 %collective-permute-done.4 = f32[2,128]{1,0:T(2,128)S(1)} collective-permute-done((f32[2,128]{1,0:T(2,128)S(1)}, f32[2,128]{1,0:T(2,128)S(1)}, u32[]{:S(2)}, u32[]{:S(2)}) %collective-permute-start.4) | collective-permute-done | bytes 1056 | tf_op jit(solution)/shard_map/ppermute | solution.py:414
  36.7 2.4 %collective-permute-start.5 = (f32[2,128]{1,0:T(2,128)S(1)}, f32[2,128]{1,0:T(2,128)S(1)}, u32[]{:S(2)}, u32[]{:S(2)}) collective-permute-start(f32[2,128]{1,0:T(2,128)S(1)} %add.14), channel_id=1, source_target_pairs={{0,9},{1,8},{2,11},{3,10},{4,13},{5,12},{6,15},{7,14},{8,1},{9,0},... | collective-permute-start | bytes 3080 | tf_op jit(solution)/shard_map/ppermute | solution.py:414
  39.1 1.1 %copy.14 = f32[8,48,8,128]{3,2,1,0:T(8,128)} copy(f32[8,48,8,128]{3,2,1,0:T(8,128)S(1)} %bitcast.9) | data formatting | bytes 3145728
  40.2 0.3 collective-permute-done.5
  40.5 0.6 %add.15 = f32[2,128]{1,0:T(2,128)} add(f32[2,128]{1,0:T(2,128)S(1)} %add.14, f32[2,128]{1,0:T(2,128)S(1)} %collective-permute-done.5) | non-fusion elementwise | flops 256 | bytes 3072 | tf_op jit(solution)/shard_map/add | solution.py:516
  (8 shorter events, 0.0 us)
Async XLA Ops:
  3.2 0.9 %copy-start.1 = (f32[1536,128]{1,0:T(8,128)}, f32[1536,128]{1,0:T(8,128)S(1)}, u32[]{:S(2)}) copy-start(f32[1536,128]{1,0:T(8,128)S(1)} %get-tuple-element.14.forcing) | copy-start | bytes 2359300
  4.1 0.8 %copy-start.2 = (bf16[2304,128]{1,0:T(8,128)(2,1)}, bf16[2304,128]{1,0:T(8,128)(2,1)S(1)}, u32[]{:S(2)}) copy-start(bf16[2304,128]{1,0:T(8,128)(2,1)S(1)} %get-tuple-element.13.forward) | copy-start | bytes 1769476
  4.9 20.3 %collective-permute-start = (f32[288,128]{1,0:T(8,128)}, f32[288,128]{1,0:T(8,128)S(1)}, u32[]{:S(2)}, u32[]{:S(2)}) collective-permute-start(f32[288,128]{1,0:T(8,128)} %get-tuple-element.18.sent_core), channel_id=1, source_target_pairs={{0,1},{1,0},{2,3},{3,2},{4,5},{5,4},{6,7},{7,6},{8,9},{9,8},{10,11... | collective-permute-start | bytes 442376 | tf_op jit(solution)/shard_map/ppermute | solution.py:414
  5.4 19.8 %collective-permute-start.1 = (f32[288,128]{1,0:T(8,128)}, f32[288,128]{1,0:T(8,128)S(1)}, u32[]{:S(2)}, u32[]{:S(2)}) collective-permute-start(f32[288,128]{1,0:T(8,128)} %get-tuple-element.19.sent_chip), channel_id=1, source_target_pairs={{1,2},{2,1},{3,4},{4,3},{5,6},{6,5},{7,8},{8,7},{9,10},{10,9},{11,... | collective-permute-start | bytes 442376 | tf_op jit(solution)/shard_map/ppermute | solution.py:425
  23.6 1.0 %copy-start = (f32[2304,128]{1,0:T(8,128)}, f32[2304,128]{1,0:T(8,128)S(1)}, u32[]{:S(2)}) copy-start(f32[2304,128]{1,0:T(8,128)S(1)} %get-tuple-element.16.weights) | copy-start | bytes 3538948
  24.6 0.6 %copy-start.3 = (f32[16,128]{1,0:T(8,128)}, f32[16,128]{1,0:T(8,128)S(1)}, u32[]{:S(2)}) copy-start(f32[16,128]{1,0:T(8,128)S(1)} %get-tuple-element.17.sums) | copy-start | bytes 24580
  25.2 0.7 %copy-start.4 = (f32[288,128]{1,0:T(8,128)}, f32[288,128]{1,0:T(8,128)S(1)}, u32[]{:S(2)}) copy-start(f32[288,128]{1,0:T(8,128)S(1)} %collective-permute-done.got_core) | copy-start | bytes 442372
  25.2 0.7 %copy-start.5 = (f32[288,128]{1,0:T(8,128)}, f32[288,128]{1,0:T(8,128)S(1)}, u32[]{:S(2)}) copy-start(f32[288,128]{1,0:T(8,128)S(1)} %collective-permute-done.1.got_chip) | copy-start | bytes 442372
  28.6 1.4 %collective-permute-start.2 = (f32[2,128]{1,0:T(2,128)}, f32[2,128]{1,0:T(2,128)S(1)}, u32[]{:S(2)}, u32[]{:S(2)}) collective-permute-start(f32[2,128]{1,0:T(2,128)} %get-tuple-element.21), channel_id=1, source_target_pairs={{0,1},{1,0},{2,3},{3,2},{4,5},{5,4},{6,7},{7,6},{8,9},{9,8},{10,11... | collective-permute-start | bytes 3080 | tf_op jit(solution)/shard_map/ppermute | solution.py:414
  30.7 3.0 %collective-permute-start.3 = (f32[2,128]{1,0:T(2,128)S(1)}, f32[2,128]{1,0:T(2,128)S(1)}, u32[]{:S(2)}, u32[]{:S(2)}) collective-permute-start(f32[2,128]{1,0:T(2,128)S(1)} %add.12), channel_id=1, source_target_pairs={{0,3},{1,2},{2,1},{3,0},{4,7},{5,6},{6,5},{7,4},{8,11},{9,10},{10,... | collective-permute-start | bytes 3080 | tf_op jit(solution)/shard_map/ppermute | solution.py:414
  33.7 3.0 %collective-permute-start.4 = (f32[2,128]{1,0:T(2,128)S(1)}, f32[2,128]{1,0:T(2,128)S(1)}, u32[]{:S(2)}, u32[]{:S(2)}) collective-permute-start(f32[2,128]{1,0:T(2,128)S(1)} %add.13), channel_id=1, source_target_pairs={{0,5},{1,4},{2,7},{3,6},{4,1},{5,0},{6,3},{7,2},{8,13},{9,12},{10,... | collective-permute-start | bytes 3080 | tf_op jit(solution)/shard_map/ppermute | solution.py:414
  36.7 3.9 %collective-permute-start.5 = (f32[2,128]{1,0:T(2,128)S(1)}, f32[2,128]{1,0:T(2,128)S(1)}, u32[]{:S(2)}, u32[]{:S(2)}) collective-permute-start(f32[2,128]{1,0:T(2,128)S(1)} %add.14), channel_id=1, source_target_pairs={{0,9},{1,8},{2,11},{3,10},{4,13},{5,12},{6,15},{7,14},{8,1},{9,0},... | collective-permute-start | bytes 3080 | tf_op jit(solution)/shard_map/ppermute | solution.py:414

commit v2 on v1

--- a/solution.py
+++ b/solution.py
@@ -11,6 +11,8 @@
 FIELDS = 8
 VX, VZ, QX, QZ, SXX, SZZ, SXZ, PR = range(FIELDS)
 HALO = 6
+GROUPS = (16, 8, 4, 2)
+ROOM = 16 << 20
 EXACT = lax.Precision.HIGHEST
 
 
@@ -237,53 +239,56 @@
     events, rows, depth, steps, _ = sizes
     vel = tuple(jnp.broadcast_to(c, (rows, depth)) for c in load_coeffs(vel_ref))
     stress = tuple(jnp.broadcast_to(c, (rows, depth)) for c in load_coeffs(stress_ref))
-    pair = 2
+    group = next(g for g in GROUPS if events % g == 0)
 
     def body(i, carry):
         perm, poro = carry
-        for sub in range(pair):
-            event = i * pair + sub
-
-            def tile(kind):
-                return pl.ds(pl.multiple_of((kind * events + event) * rows, rows), rows)
-
-            fields = [state_in[tile(f), :] for f in range(FIELDS)]
-            for step in range(steps):
-                factors = []
-                for kind in range(3):
-                    at = (step * 3 + kind) * events * rows
-                    both = forward[pl.ds(pl.multiple_of(at + i * pair * rows, pair * rows), pair * rows), :]
-                    value = both.astype(jnp.float32)[sub * rows : (sub + 1) * rows, :]
-                    weights[tile(step * 3 + kind), :] = value
-                    factors.append(value)
+
+        def tile(kind, sub):
+            return pl.ds(pl.multiple_of((kind * events + i * group + sub) * rows, rows), rows)
+
+        fields = [[state_in[tile(f, sub), :] for f in range(FIELDS)] for sub in range(group)]
+        for step in range(steps):
+            factors = [[] for _ in range(group)]
+            for kind in range(3):
+                for sub in range(0, group, 2):
+                    at = ((step * 3 + kind) * events + i * group + sub) * rows
+                    both = forward[pl.ds(pl.multiple_of(at, 2 * rows), 2 * rows), :].astype(jnp.float32)
+                    for half in range(2):
+                        value = both[half * rows : (half + 1) * rows]
+                        weights[tile(step * 3 + kind, sub + half), :] = value
+                        factors[sub + half].append(value)
+            for sub, own in enumerate(fields):
                 gains = velocity_gain(
                     vel,
-                    row_lower(fields[SXX]) + depth_lower(fields[SXZ]),
-                    row_lower(fields[SXZ]) + depth_lower(fields[SZZ]),
-                    row_lower(fields[PR]) + vel[3] * fields[QX],
-                    depth_lower(fields[PR]) + vel[3] * fields[QZ],
+                    row_lower(own[SXX]) + depth_lower(own[SXZ]),
+                    row_lower(own[SXZ]) + depth_lower(own[SZZ]),
+                    row_lower(own[PR]) + vel[3] * own[QX],
+                    depth_lower(own[PR]) + vel[3] * own[QZ],
                 )
-                fields[:4] = plus(fields[:4], gains)
-                fields[VX] = fields[VX] + forcing[tile(step * 2), :]
-                fields[VZ] = fields[VZ] + forcing[tile(step * 2 + 1), :]
-                perm = perm + fields[QX] * factors[0] + fields[QZ] * factors[1]
-                fields[4:] = plus(
-                    fields[4:],
+                own[:4] = plus(own[:4], gains)
+                own[VX] = own[VX] + forcing[tile(step * 2, sub), :]
+                own[VZ] = own[VZ] + forcing[tile(step * 2 + 1, sub), :]
+                perm = perm + own[QX] * factors[sub][0] + own[QZ] * factors[sub][1]
+            for sub, own in enumerate(fields):
+                own[4:] = plus(
+                    own[4:],
                     stress_gain(
                         stress,
-                        row_upper(fields[VX]),
-                        depth_upper(fields[VZ]),
-                        row_upper(fields[QX]) + depth_upper(fields[QZ]),
-                        depth_upper(fields[VX]) + row_upper(fields[VZ]),
+                        row_upper(own[VX]),
+                        depth_upper(own[VZ]),
+                        row_upper(own[QX]) + depth_upper(own[QZ]),
+                        depth_upper(own[VX]) + row_upper(own[VZ]),
                     ),
                 )
-                poro = poro + fields[PR] * factors[2]
+                poro = poro + own[PR] * factors[sub][2]
+        for sub, own in enumerate(fields):
             for f in range(FIELDS):
-                state[tile(f), :] = fields[f]
+                state[tile(f, sub), :] = own[f]
         return perm, poro
 
     zero = jnp.zeros((rows, depth), jnp.float32)
-    perm, poro = lax.fori_loop(0, events // pair, body, (zero, zero))
+    perm, poro = lax.fori_loop(0, events // group, body, (zero, zero))
     sums[pl.ds(0, rows), :] = perm
     sums[pl.ds(rows, rows), :] = poro
 
@@ -445,9 +450,13 @@
     cells = drm_cells.reshape(blocks, 128)
     force = drm_force.reshape(sources * steps, 2, blocks, 128).transpose(0, 2, 1, 3)
     force = force.reshape(sources * steps * 2 * blocks, 128)
-    message = jax.ShapeDtypeStruct((HALO * events, depth), f32)
-
-    state, forward, forcing, message_core, message_chip = pl.pallas_call(
+    message = pltpu.VMEM((HALO * events, depth), f32)
+    limits = pltpu.CompilerParams(vmem_limit_bytes=ROOM)
+
+    def kept(space, *values):
+        return tuple(pltpu.with_memory_space_constraint(v, space) for v in values)
+
+    state, forward, forcing, message_core, message_chip, vel, stress = pl.pallas_call(
         functools.partial(edge_kernel, sizes),
         out_shape=(
             pltpu.VMEM(state.shape, f32),
@@ -455,20 +464,21 @@
             pltpu.VMEM((steps * 2 * tiles, depth), f32),
             message,
             message,
+            pltpu.VMEM(vel_coeffs.shape, f32),
+            pltpu.VMEM(stress_coeffs.shape, f32),
         ),
         in_specs=[any_space] * 7,
-        out_specs=(vmem,) * 5,
+        out_specs=(vmem,) * 7,
         scratch_shapes=[
-            pltpu.VMEM(vel_coeffs.shape, f32),
-            pltpu.VMEM(stress_coeffs.shape, f32),
             pltpu.VMEM(cells.shape, jnp.int32),
             pltpu.VMEM(force.shape, f32),
             pltpu.VMEM((force.shape[0] * rows, depth), f32),
             pltpu.SMEM(source_id.shape, jnp.int32),
             pltpu.SemaphoreType.DMA((7,)),
         ],
+        compiler_params=limits,
         name="edges",
-    )(state, forward, vel_coeffs, stress_coeffs, cells, force, source_id)
+    )(*kept(pltpu.HBM, state, forward, vel_coeffs, stress_coeffs, cells, force, source_id))
 
     got_chip = swap_over_chips(message_chip, groups, size)
     got_core = swap_with(message_core, size, 1)
@@ -483,34 +493,26 @@
         in_specs=[vmem] * 5,
         out_specs=(vmem,) * 3,
         input_output_aliases={0: 0},
+        compiler_params=limits,
         cost_estimate=pl.CostEstimate(
             flops=steps * 80 * tiles * depth, bytes_accessed=8 * state.size, transcendentals=0
         ),
         name="bulk",
-    )(state, forward, forcing, vel_coeffs, stress_coeffs)
+    )(*kept(pltpu.VMEM, state, forward, forcing, vel, stress))
 
     normalizer = (events * rows * size) ** (-0.5)
     state, totals = pl.pallas_call(
         functools.partial(join_kernel, sizes, normalizer),
         out_shape=(
             pltpu.VMEM(state.shape, f32),
-            jax.ShapeDtypeStruct((2, depth), f32),
+            pltpu.VMEM((2, depth), f32),
         ),
         in_specs=[vmem] * 9,
         out_specs=(vmem,) * 2,
         input_output_aliases={0: 0},
+        compiler_params=limits,
         name="join",
-    )(
-        state,
-        weights,
-        sums,
-        message_core,
-        message_chip,
-        got_core,
-        got_chip,
-        vel_coeffs,
-        stress_coeffs,
-    )
+    )(*kept(pltpu.VMEM, state, weights, sums, message_core, message_chip, got_core, got_chip, vel, stress))
     mask = 1
     while mask < size:
         totals = totals + swap_with(totals, size, mask | 1)

time: 41.3 us -> 22.8 us (0.55)
  Pallas kernels: 21 us -> 3.95 us
  local copies, waits for them, and re-layouts: 5.13 us -> 1.14 us
  starting transfers between devices: 8.16 us -> 10.8 us
  other arithmetic: 1.25 us -> 0.57 us
  waiting for transfers between devices: 4.88 us -> 5.47 us
    pallas_call x1, Pallas kernels: 15.7 us -> 1.42 us  [shards(): pl.pallas_call(functools.partial(bulk_kernel, sizes), out_shape=(pltpu.VM...]
    unnamed x13 -> x1, local copies, waits for them, and re-layouts: 5.13 us -> 1.14 us
    ppermute x5, starting transfers between devices: 5.67 us -> 8.25 us  [swap_with(): return lax.ppermute(value, 'gx', [(i, i ^ mask) for i in range(size)])]
    pallas_call x1, Pallas kernels: 2.68 us -> 0.64 us  [shards(): pl.pallas_call(functools.partial(join_kernel, sizes, normalizer), out_sha...]
    ppermute x1, waiting for transfers between devices: 0.01 us -> 1.68 us  [swap_over_chips(): return lax.ppermute(value, ('groups', 'gx'), route)]
    ppermute x5, waiting for transfers between devices: 4.87 us -> 3.78 us  [swap_with(): return lax.ppermute(value, 'gx', [(i, i ^ mask) for i in range(size)])]
    pallas_call x1, Pallas kernels: 2.6 us -> 1.89 us  [shards(): pl.pallas_call(functools.partial(edge_kernel, sizes), out_shape=(pltpu.VM...]
    add x4, other arithmetic: 1.25 us -> 0.57 us  [shards(): totals = totals + swap_with(totals, size, mask | 1)]
  transfers between devices with their start and end apart: 6 -> 6, of which waited for: 4 -> 5; matrix products, arithmetic and copies ran while one was open for 3% -> 5% of each run, Pallas kernels for 38% -> 6%
where the time goes in v2:
time: 22.8 us; the launch traced here: 22.6 us
  starting transfers between devices  10.8 us (47%)
  waiting for transfers between devices  5.47 us (24%)
  Pallas kernels  3.95 us (17%)
  local copies, waits for them, and re-layouts  1.14 us (5%)
  between operations  0.67 us (3%)
  other arithmetic  0.57 us (2%)
    ppermute x5, starting transfers between devices, swap_with(): return lax.ppermute(value, 'gx', [(i, i ^ mask) for i in range(size)])  8.25 us
    ppermute x5, waiting for transfers between devices, swap_with(): return lax.ppermute(value, 'gx', [(i, i ^ mask) for i in range(size)])  3.78 us
    ppermute x1, starting transfers between devices, swap_over_chips(): return lax.ppermute(value, ('groups', 'gx'), route)  2.56 us
    pallas_call x1, Pallas kernels, shards(): pl.pallas_call(functools.partial(edge_kernel, sizes), out_shape=(pltpu.VM...  1.89 us
    ppermute x1, waiting for transfers between devices, swap_over_chips(): return lax.ppermute(value, ('groups', 'gx'), route)  1.68 us
    pallas_call x1, Pallas kernels, shards(): pl.pallas_call(functools.partial(bulk_kernel, sizes), out_shape=(pltpu.VM...  1.42 us
    unnamed x1, local copies, waits for them, and re-layouts  1.14 us
    pallas_call x1, Pallas kernels, shards(): pl.pallas_call(functools.partial(join_kernel, sizes, normalizer), out_sha...  0.64 us
  transfers between devices with their start and end apart: 6, of which 5 were waited for; matrix products, arithmetic and copies ran while one was open for 5% of the time, Pallas kernels for 6%

profile of v2, /device:TPU:0, one launch (start us, length us, event | category | flops | bytes accessed | tf_op | source)
XLA Modules:
  0.0 22.6 jit_solution(17100262629373861709)
XLA Ops:
  0.6 1.9 %edges.1 = (f32[3072,128]{1,0:T(8,128)S(1)}, bf16[2304,128]{1,0:T(8,128)(2,1)S(1)}, f32[1536,128]{1,0:T(8,128)S(1)}, f32[288,128]{1,0:T(8,128)S(1)}, f32[288,128...) custom-call(f32[3072,128]{1,0:T(8,128)} %bitcast.10, bf16[2304,128]{1,0:T(8,128)(2,1)} %bitcast.11, ...), custom_call_target="tpu_custom_call" | custom-call | tf_op jit(solution)/shard_map/edges/pallas_call | solution.py:459
  2.5 0.5 %collective-permute-start = (f32[288,128]{1,0:T(8,128)S(1)}, f32[288,128]{1,0:T(8,128)S(1)}, u32[]{:S(2)}, u32[]{:S(2)}) collective-permute-start(f32[288,128]{1,0:T(8,128)S(1)} %get-tuple-element.22.sent_core), channel_id=1, source_target_pairs={{0,1},{1,0},{2,3},{3,2},{4,5},{5,4},{6,7},{7,6},{8,9},{9,8},{10,11... | collective-permute-start | bytes 442376 | tf_op jit(solution)/shard_map/ppermute | solution.py:419
  3.0 2.6 %collective-permute-start.1 = (f32[288,128]{1,0:T(8,128)S(1)}, f32[288,128]{1,0:T(8,128)S(1)}, u32[]{:S(2)}, u32[]{:S(2)}) collective-permute-start(f32[288,128]{1,0:T(8,128)S(1)} %get-tuple-element.23.sent_chip), channel_id=1, source_target_pairs={{1,2},{2,1},{3,4},{4,3},{5,6},{6,5},{7,8},{8,7},{9,10},{10,9},{11,... | collective-permute-start | bytes 442376 | tf_op jit(solution)/shard_map/ppermute | solution.py:430
  5.6 1.4 %bulk.1 = (f32[3072,128]{1,0:T(8,128)S(1)}, f32[2304,128]{1,0:T(8,128)S(1)}, f32[16,128]{1,0:T(8,128)S(1)}) custom-call(f32[3072,128]{1,0:T(8,128)S(1)} %get-tuple-element.14.state_in, bf16[2304,128]{1,0:T(8,128)(2,1)S(1)} %get-tuple-element.15.forward, f32[1536,128]{1,0:T(8,128)S(1)} %get-tuple-element.16.forcing, ...), custom_call_target="tpu_custom_call", output_to_operand_aliasing={{0}: (0, {})} | custom-call | flops 7864320 | bytes 3145728 | tf_op jit(solution)/shard_map/bulk/pallas_call | solution.py:486
  7.0 0.0 collective-permute-done.got_core
  7.0 1.7 %collective-permute-done.1.got_chip = f32[288,128]{1,0:T(8,128)S(1)} collective-permute-done((f32[288,128]{1,0:T(8,128)S(1)}, f32[288,128]{1,0:T(8,128)S(1)}, u32[]{:S(2)}, u32[]{:S(2)}) %collective-permute-start.1) | collective-permute-done | bytes 147488 | tf_op jit(solution)/shard_map/ppermute | solution.py:430
  8.7 0.6 %join.1 = (f32[3072,128]{1,0:T(8,128)S(1)}, f32[2,128]{1,0:T(2,128)S(1)}) custom-call(f32[3072,128]{1,0:T(8,128)S(1)} %get-tuple-element.19.state_in, f32[2304,128]{1,0:T(8,128)S(1)} %get-tuple-element.20.weights, f32[16,128]{1,0:T(8,128)S(1)} %get-tuple-element.21.sums, ...), custom_call_target="tpu_custom_call", output_to_operand_aliasing={{0}: (0, {})} | custom-call | tf_op jit(solution)/shard_map/join/pallas_call | solution.py:504
  9.4 0.2 collective-permute-start.2
  9.6 1.0 %collective-permute-done.2 = f32[2,128]{1,0:T(2,128)S(1)} collective-permute-done((f32[2,128]{1,0:T(2,128)S(1)}, f32[2,128]{1,0:T(2,128)S(1)}, u32[]{:S(2)}, u32[]{:S(2)}) %collective-permute-start.2) | collective-permute-done | bytes 1056 | tf_op jit(solution)/shard_map/ppermute | solution.py:419
  10.6 2.5 %collective-permute-start.3 = (f32[2,128]{1,0:T(2,128)S(1)}, f32[2,128]{1,0:T(2,128)S(1)}, u32[]{:S(2)}, u32[]{:S(2)}) collective-permute-start(f32[2,128]{1,0:T(2,128)S(1)} %add.12), channel_id=1, source_target_pairs={{0,3},{1,2},{2,1},{3,0},{4,7},{5,6},{6,5},{7,4},{8,11},{9,10},{10,... | collective-permute-start | bytes 3080 | tf_op jit(solution)/shard_map/ppermute | solution.py:419
  13.1 1.3 %collective-permute-done.3 = f32[2,128]{1,0:T(2,128)S(1)} collective-permute-done((f32[2,128]{1,0:T(2,128)S(1)}, f32[2,128]{1,0:T(2,128)S(1)}, u32[]{:S(2)}, u32[]{:S(2)}) %collective-permute-start.3) | collective-permute-done | bytes 1056 | tf_op jit(solution)/shard_map/ppermute | solution.py:419
  14.4 2.4 %collective-permute-start.4 = (f32[2,128]{1,0:T(2,128)S(1)}, f32[2,128]{1,0:T(2,128)S(1)}, u32[]{:S(2)}, u32[]{:S(2)}) collective-permute-start(f32[2,128]{1,0:T(2,128)S(1)} %add.13), channel_id=1, source_target_pairs={{0,5},{1,4},{2,7},{3,6},{4,1},{5,0},{6,3},{7,2},{8,13},{9,12},{10,... | collective-permute-start | bytes 3080 | tf_op jit(solution)/shard_map/ppermute | solution.py:419
  16.7 1.3 %collective-permute-done.4 = f32[2,128]{1,0:T(2,128)S(1)} collective-permute-done((f32[2,128]{1,0:T(2,128)S(1)}, f32[2,128]{1,0:T(2,128)S(1)}, u32[]{:S(2)}, u32[]{:S(2)}) %collective-permute-start.4) | collective-permute-done | bytes 1056 | tf_op jit(solution)/shard_map/ppermute | solution.py:419
  18.0 2.7 %collective-permute-start.5 = (f32[2,128]{1,0:T(2,128)S(1)}, f32[2,128]{1,0:T(2,128)S(1)}, u32[]{:S(2)}, u32[]{:S(2)}) collective-permute-start(f32[2,128]{1,0:T(2,128)S(1)} %add.14), channel_id=1, source_target_pairs={{0,9},{1,8},{2,11},{3,10},{4,13},{5,12},{6,15},{7,14},{8,1},{9,0},... | collective-permute-start | bytes 3080 | tf_op jit(solution)/shard_map/ppermute | solution.py:419
  20.7 1.1 %copy.14 = f32[8,48,8,128]{3,2,1,0:T(8,128)} copy(f32[8,48,8,128]{3,2,1,0:T(8,128)S(1)} %bitcast.9) | data formatting | bytes 3145728
  21.9 0.2 collective-permute-done.5
  22.0 0.6 %add.15 = f32[2,128]{1,0:T(2,128)} add(f32[2,128]{1,0:T(2,128)S(1)} %add.14, f32[2,128]{1,0:T(2,128)S(1)} %collective-permute-done.5) | non-fusion elementwise | flops 256 | bytes 3072 | tf_op jit(solution)/shard_map/add | solution.py:518
  (3 shorter events, 0.0 us)
Async XLA Ops:
  2.5 4.5 %collective-permute-start = (f32[288,128]{1,0:T(8,128)S(1)}, f32[288,128]{1,0:T(8,128)S(1)}, u32[]{:S(2)}, u32[]{:S(2)}) collective-permute-start(f32[288,128]{1,0:T(8,128)S(1)} %get-tuple-element.22.sent_core), channel_id=1, source_target_pairs={{0,1},{1,0},{2,3},{3,2},{4,5},{5,4},{6,7},{7,6},{8,9},{9,8},{10,11... | collective-permute-start | bytes 442376 | tf_op jit(solution)/shard_map/ppermute | solution.py:419
  3.0 5.7 %collective-permute-start.1 = (f32[288,128]{1,0:T(8,128)S(1)}, f32[288,128]{1,0:T(8,128)S(1)}, u32[]{:S(2)}, u32[]{:S(2)}) collective-permute-start(f32[288,128]{1,0:T(8,128)S(1)} %get-tuple-element.23.sent_chip), channel_id=1, source_target_pairs={{1,2},{2,1},{3,4},{4,3},{5,6},{6,5},{7,8},{8,7},{9,10},{10,9},{11,... | collective-permute-start | bytes 442376 | tf_op jit(solution)/shard_map/ppermute | solution.py:430
  9.4 1.2 %collective-permute-start.2 = (f32[2,128]{1,0:T(2,128)S(1)}, f32[2,128]{1,0:T(2,128)S(1)}, u32[]{:S(2)}, u32[]{:S(2)}) collective-permute-start(f32[2,128]{1,0:T(2,128)S(1)} %get-tuple-element.25), channel_id=1, source_target_pairs={{0,1},{1,0},{2,3},{3,2},{4,5},{5,4},{6,7},{7,6},{8,9},{9,8},{10,11... | collective-permute-start | bytes 3080 | tf_op jit(solution)/shard_map/ppermute | solution.py:419
  10.6 3.8 %collective-permute-start.3 = (f32[2,128]{1,0:T(2,128)S(1)}, f32[2,128]{1,0:T(2,128)S(1)}, u32[]{:S(2)}, u32[]{:S(2)}) collective-permute-start(f32[2,128]{1,0:T(2,128)S(1)} %add.12), channel_id=1, source_target_pairs={{0,3},{1,2},{2,1},{3,0},{4,7},{5,6},{6,5},{7,4},{8,11},{9,10},{10,... | collective-permute-start | bytes 3080 | tf_op jit(solution)/shard_map/ppermute | solution.py:419
  14.4 3.7 %collective-permute-start.4 = (f32[2,128]{1,0:T(2,128)S(1)}, f32[2,128]{1,0:T(2,128)S(1)}, u32[]{:S(2)}, u32[]{:S(2)}) collective-permute-start(f32[2,128]{1,0:T(2,128)S(1)} %add.13), channel_id=1, source_target_pairs={{0,5},{1,4},{2,7},{3,6},{4,1},{5,0},{6,3},{7,2},{8,13},{9,12},{10,... | collective-permute-start | bytes 3080 | tf_op jit(solution)/shard_map/ppermute | solution.py:419
  18.0 4.0 %collective-permute-start.5 = (f32[2,128]{1,0:T(2,128)S(1)}, f32[2,128]{1,0:T(2,128)S(1)}, u32[]{:S(2)}, u32[]{:S(2)}) collective-permute-start(f32[2,128]{1,0:T(2,128)S(1)} %add.14), channel_id=1, source_target_pairs={{0,9},{1,8},{2,11},{3,10},{4,13},{5,12},{6,15},{7,14},{8,1},{9,0},... | collective-permute-start | bytes 3080 | tf_op jit(solution)/shard_map/ppermute | solution.py:419

commit v3 on v2

--- a/solution.py
+++ b/solution.py
@@ -11,9 +11,9 @@
 FIELDS = 8
 VX, VZ, QX, QZ, SXX, SZZ, SXZ, PR = range(FIELDS)
 HALO = 6
+PUSHED = ((0, 0), (0, 1), (1, 0), (0, -1))
 GROUPS = (16, 8, 4, 2)
 ROOM = 16 << 20
-EXACT = lax.Precision.HIGHEST
 
 
 def depth_lower(values):
@@ -82,25 +82,30 @@
     return tuple(ref[pl.ds(i, 1), :] for i in range(4))
 
 
+def at_row(layers, row, depth):
+    lane = lax.broadcasted_iota(jnp.int32, layers.shape, 1)
+    moved = pltpu.roll(layers, (depth - LAYER - LAYER * row) % depth, 1)
+    return jnp.where(lane >= depth - LAYER, moved, 0.0)
+
+
 def edge_kernel(
     sizes,
     state_hbm,
-    forward_hbm,
     vel_hbm,
     stress_hbm,
     cells_hbm,
     force_hbm,
     source_hbm,
-    state,
-    forward,
-    forcing,
+    table_ref,
     message_core,
     message_chip,
     vel_ref,
     stress_ref,
+    near,
     cells,
     force,
-    by_source,
+    near_force,
+    pushes,
     source,
     sems,
 ):
@@ -114,8 +119,8 @@
                 (source_hbm, source),
                 (vel_hbm, vel_ref),
                 (stress_hbm, stress_ref),
-                (state_hbm, state),
-                (forward_hbm, forward),
+                (state_hbm.at[:, pl.ds(0, 2)], near.at[:, pl.ds(0, 2)]),
+                (state_hbm.at[:, pl.ds(rows - 2, 2)], near.at[:, pl.ds(rows - 2, 2)]),
             ]
         )
     ]
@@ -127,49 +132,48 @@
     local = cells[...] & (rows * depth - 1)
     slot = (local // depth) * LAYER + (local & (depth - 1)) - (depth - LAYER)
     layers = None
+    rest = force[...]
+    pieces = []
+    for _ in range(3):
+        pieces.append(rest.astype(jnp.bfloat16))
+        rest = rest - pieces[-1].astype(jnp.float32)
     for block in range(cells.shape[0]):
         spots = lax.broadcasted_iota(jnp.int32, (depth, lanes), 0)
-        hit = (spots == slot[block : block + 1, :]).astype(jnp.float32)
-        part = lax.dot_general(
-            force[...],
-            hit,
-            (((1,), (1,)), ((), ())),
-            precision=EXACT,
-            preferred_element_type=jnp.float32,
-        )
+        hit = (spots == slot[block : block + 1, :]).astype(jnp.float32).astype(jnp.bfloat16)
+        part = None
+        for piece in pieces:
+            term = lax.dot_general(
+                piece, hit, (((1,), (1,)), ((), ())), preferred_element_type=jnp.float32
+            )
+            part = term if part is None else part + term
         if block:
             part = pltpu.roll(part, part.shape[0] - 2 * block, 0)
         layers = part if layers is None else layers + part
-    lane = lax.broadcasted_iota(jnp.int32, layers.shape, 1)
-    for row in range(rows):
-        moved = pltpu.roll(layers, (depth - LAYER - LAYER * row) % depth, 1)
-        by_source[pl.ds(row, layers.shape[0], stride=rows), :] = jnp.where(
-            lane >= depth - LAYER, moved, 0.0
-        )
+    table_ref[...] = layers
+    def moved(row):
+        return at_row(layers, row, depth)
+
+    own = lax.broadcasted_iota(jnp.int32, layers.shape, 0) & (rows - 1)
+    picked = jnp.where(own < 6, pltpu.roll(moved(1), 2, 0), pltpu.roll(moved(rows - 1), 6, 0))
+    near_force[...] = jnp.where((own & 2) == 0, moved(0), picked)
     copies[2].wait()
-    blocks = cells.shape[0]
     for event in range(events):
-        record = source[event]
-        for step in range(steps):
-            for part in range(2):
-                at = (record * steps + step) * 2 * blocks + part
-                forcing[pl.ds(((step * 2 + part) * events + event) * rows, rows), :] = by_source[
-                    pl.ds(pl.multiple_of(at * rows, rows), rows), :
-                ]
-    for copy in copies[3:6]:
+        record = pl.multiple_of(source[event] * rows, rows)
+        pushes[pl.ds(event * rows, rows), :] = near_force[pl.ds(record, rows), :]
+    for copy in copies[3:]:
         copy.wait()
     vel = load_coeffs(vel_ref)
     stress = load_coeffs(stress_ref)
     odd = lax.rem(lax.axis_index("gx"), 2) == 1
     last = rows - 1
+    state = near.reshape(near.shape[0] * rows, depth)
 
     def rim(chunk, field, row):
         return state[pl.ds((field * events + chunk) * rows + row, 8, stride=rows), :]
 
     def pushed(chunk, step, part, row):
-        return forcing[
-            pl.ds(((step * 2 + part) * events + chunk) * rows + row, 8, stride=rows), :
-        ]
+        at = PUSHED.index((step, row if row < last else -1)) * 2 + part
+        return pushes[pl.ds(chunk * rows + at, 8, stride=rows), :]
 
     for chunk in range(0, events, 8):
         first = [rim(chunk, f, 0) for f in range(FIELDS)]
@@ -230,33 +234,67 @@
             at = pl.ds(i * events + chunk, 8)
             message_core[at, :] = jnp.where(odd, left[i], right[i])
             message_chip[at, :] = jnp.where(odd, right[i], left[i])
-    copies[6].wait()
-
 
 def bulk_kernel(
-    sizes, state_in, forward, forcing, vel_ref, stress_ref, state, weights, sums
+    sizes,
+    state_hbm,
+    forward_hbm,
+    source_hbm,
+    table_ref,
+    vel_ref,
+    stress_ref,
+    state,
+    weights,
+    sums,
+    forward,
+    by_source,
+    source,
+    sems,
 ):
     events, rows, depth, steps, _ = sizes
+    group = next(g for g in GROUPS if events % g == 0)
+
+    def copies(i):
+        at = i * group * rows
+        own = pl.ds(at if isinstance(at, int) else pl.multiple_of(at, group * rows), group * rows)
+        return (
+            pltpu.make_async_copy(state_hbm.at[:, own], state.at[:, own], sems.at[0, i]),
+            pltpu.make_async_copy(forward_hbm.at[:, own], forward.at[:, own], sems.at[1, i]),
+        )
+
+    source_copy = pltpu.make_async_copy(source_hbm, source, sems.at[2, 0])
+    source_copy.start()
+    for i in range(events // group):
+        for copy in copies(i):
+            copy.start()
+    layers = table_ref[...]
+    for row in range(rows):
+        by_source[pl.ds(row, layers.shape[0], stride=rows), :] = at_row(layers, row, depth)
     vel = tuple(jnp.broadcast_to(c, (rows, depth)) for c in load_coeffs(vel_ref))
     stress = tuple(jnp.broadcast_to(c, (rows, depth)) for c in load_coeffs(stress_ref))
-    group = next(g for g in GROUPS if events % g == 0)
 
     def body(i, carry):
         perm, poro = carry
 
-        def tile(kind, sub):
-            return pl.ds(pl.multiple_of((kind * events + i * group + sub) * rows, rows), rows)
-
-        fields = [[state_in[tile(f, sub), :] for f in range(FIELDS)] for sub in range(group)]
+        def tile(sub, count=1):
+            at = (i * group + sub) * rows
+            return pl.ds(pl.multiple_of(at, count * rows), count * rows)
+
+        def pushed(step, part, sub):
+            at = source[i * group + sub] * rows + step * 4 + part
+            return by_source[pl.ds(pl.multiple_of(at * rows, rows), rows), :]
+
+        for copy in copies(i):
+            copy.wait()
+        fields = [[state[f, tile(sub), :] for f in range(FIELDS)] for sub in range(group)]
         for step in range(steps):
             factors = [[] for _ in range(group)]
             for kind in range(3):
                 for sub in range(0, group, 2):
-                    at = ((step * 3 + kind) * events + i * group + sub) * rows
-                    both = forward[pl.ds(pl.multiple_of(at, 2 * rows), 2 * rows), :].astype(jnp.float32)
+                    both = forward[step * 3 + kind, tile(sub, 2), :].astype(jnp.float32)
                     for half in range(2):
                         value = both[half * rows : (half + 1) * rows]
-                        weights[tile(step * 3 + kind, sub + half), :] = value
+                        weights[step * 3 + kind, tile(sub + half), :] = value
                         factors[sub + half].append(value)
             for sub, own in enumerate(fields):
                 gains = velocity_gain(
@@ -267,8 +305,8 @@
                     depth_lower(own[PR]) + vel[3] * own[QZ],
                 )
                 own[:4] = plus(own[:4], gains)
-                own[VX] = own[VX] + forcing[tile(step * 2, sub), :]
-                own[VZ] = own[VZ] + forcing[tile(step * 2 + 1, sub), :]
+                own[VX] = own[VX] + pushed(step, 0, sub)
+                own[VZ] = own[VZ] + pushed(step, 1, sub)
                 perm = perm + own[QX] * factors[sub][0] + own[QZ] * factors[sub][1]
             for sub, own in enumerate(fields):
                 own[4:] = plus(
@@ -284,10 +322,11 @@
                 poro = poro + own[PR] * factors[sub][2]
         for sub, own in enumerate(fields):
             for f in range(FIELDS):
-                state[tile(f, sub), :] = own[f]
+                state[f, tile(sub), :] = own[f]
         return perm, poro
 
     zero = jnp.zeros((rows, depth), jnp.float32)
+    source_copy.wait()
     perm, poro = lax.fori_loop(0, events // group, body, (zero, zero))
     sums[pl.ds(0, rows), :] = perm
     sums[pl.ds(rows, rows), :] = poro
@@ -296,16 +335,15 @@
 def join_kernel(
     sizes,
     normalizer,
-    state_in,
     weights,
     sums,
+    sent_chip,
     sent_core,
-    sent_chip,
+    got_chip,
     got_core,
-    got_chip,
     vel_ref,
     stress_ref,
-    state,
+    changes,
     totals,
 ):
     events, rows, depth, _, _ = sizes
@@ -392,7 +430,7 @@
         end_last = plus(stress_last, strains(vel_last, again))
 
         def factor(step, kind, row):
-            return weights[pl.ds(((step * 3 + kind) * events + chunk) * rows + row, 8, stride=rows), :]
+            return weights[step * 3 + kind, pl.ds(chunk * rows + row, 8, stride=rows), :]
 
         perm = perm + gain_first[2] * factor(0, 0, 0) + gain_first[3] * factor(0, 1, 0)
         for row, vels in ((0, vel_first), (1, vel_second), (last, vel_last)):
@@ -402,17 +440,30 @@
         for row, stresses in ends:
             poro = poro + stresses[3] * factor(1, 2, row)
 
-        changes = [(0, 0, vel_first), (1, 0, vel_second), (last, 0, vel_last)]
-        changes += [(row, 4, stresses) for row, stresses in ends]
-        for row, start, values in changes:
-            for i, value in enumerate(values):
-                at = pl.ds(((start + i) * events + chunk) * rows + row, 8, stride=rows)
-                state[at, :] = state_in[at, :] + value
+        values = vel_first + vel_second + vel_last + end_first + end_second + end_inner + end_last
+        for i, value in enumerate(values):
+            changes[i, pl.ds(chunk, 8), :] = value
 
     perm = jnp.sum(perm, axis=0, keepdims=True) * (vel[2] * vel[3] * normalizer)
     poro = jnp.sum(poro, axis=0, keepdims=True) * (stress[3] * normalizer)
     totals[pl.ds(0, 1), :] = perm
     totals[pl.ds(1, 1), :] = poro
+
+
+def finish_kernel(sizes, state_in, changes, state, out_hbm, sems):
+    events, rows, _, _, _ = sizes
+    last = rows - 1
+    places = [(start, row, f) for start, ends in ((0, (0, 1, last)), (4, (0, 1, last - 1, last))) for row in ends for f in range(4)]
+    copies = []
+    for field in range(FIELDS):
+        for i, (start, row, f) in enumerate(places):
+            if start + f == field:
+                at = pl.ds(row, events, stride=rows)
+                state[field, at, :] = state_in[field, at, :] + changes[i]
+        copies.append(pltpu.make_async_copy(state.at[field], out_hbm.at[field], sems.at[field]))
+        copies[-1].start()
+    for copy in copies:
+        copy.wait()
 
 
 def swap_with(value, size, mask):
@@ -445,8 +496,8 @@
     f32 = jnp.float32
     any_space = pl.BlockSpec(memory_space=pl.ANY)
     vmem = pl.BlockSpec(memory_space=pltpu.VMEM)
-    state = adjoint_state.reshape(fields * tiles, depth)
-    forward = forward_fields.reshape(steps * 3 * tiles, depth)
+    state = adjoint_state.reshape(fields, tiles, depth)
+    forward = forward_fields.reshape(steps * 3, tiles, depth)
     cells = drm_cells.reshape(blocks, 128)
     force = drm_force.reshape(sources * steps, 2, blocks, 128).transpose(0, 2, 1, 3)
     force = force.reshape(sources * steps * 2 * blocks, 128)
@@ -456,68 +507,95 @@
     def kept(space, *values):
         return tuple(pltpu.with_memory_space_constraint(v, space) for v in values)
 
-    state, forward, forcing, message_core, message_chip, vel, stress = pl.pallas_call(
+    table, message_core, message_chip, vel, stress = pl.pallas_call(
         functools.partial(edge_kernel, sizes),
         out_shape=(
-            pltpu.VMEM(state.shape, f32),
-            pltpu.VMEM(forward.shape, forward.dtype),
-            pltpu.VMEM((steps * 2 * tiles, depth), f32),
+            pltpu.VMEM(force.shape, f32),
             message,
             message,
             pltpu.VMEM(vel_coeffs.shape, f32),
             pltpu.VMEM(stress_coeffs.shape, f32),
         ),
-        in_specs=[any_space] * 7,
-        out_specs=(vmem,) * 7,
+        in_specs=[any_space] * 6,
+        out_specs=(vmem,) * 5,
         scratch_shapes=[
+            pltpu.VMEM((fields * events, rows, depth), f32),
             pltpu.VMEM(cells.shape, jnp.int32),
             pltpu.VMEM(force.shape, f32),
-            pltpu.VMEM((force.shape[0] * rows, depth), f32),
+            pltpu.VMEM(force.shape, f32),
+            pltpu.VMEM((tiles, depth), f32),
             pltpu.SMEM(source_id.shape, jnp.int32),
             pltpu.SemaphoreType.DMA((7,)),
         ],
         compiler_params=limits,
         name="edges",
-    )(*kept(pltpu.HBM, state, forward, vel_coeffs, stress_coeffs, cells, force, source_id))
-
+    )(
+        *kept(
+            pltpu.HBM,
+            state.reshape(fields * events, rows, depth),
+            vel_coeffs,
+            stress_coeffs,
+            cells,
+            force,
+            source_id,
+        )
+    )
+
+    got_core = swap_with(message_core, size, 1)
     got_chip = swap_over_chips(message_chip, groups, size)
-    got_core = swap_with(message_core, size, 1)
 
     state, weights, sums = pl.pallas_call(
         functools.partial(bulk_kernel, sizes),
         out_shape=(
             pltpu.VMEM(state.shape, f32),
-            pltpu.VMEM((steps * 3 * tiles, depth), f32),
+            pltpu.VMEM(forward.shape, f32),
             pltpu.VMEM((2 * rows, depth), f32),
         ),
-        in_specs=[vmem] * 5,
+        in_specs=[any_space] * 3 + [vmem] * 3,
         out_specs=(vmem,) * 3,
-        input_output_aliases={0: 0},
+        scratch_shapes=[
+            pltpu.VMEM(forward.shape, forward.dtype),
+            pltpu.VMEM((force.shape[0] * rows, depth), f32),
+            pltpu.SMEM(source_id.shape, jnp.int32),
+            pltpu.SemaphoreType.DMA((3, events)),
+        ],
         compiler_params=limits,
         cost_estimate=pl.CostEstimate(
             flops=steps * 80 * tiles * depth, bytes_accessed=8 * state.size, transcendentals=0
         ),
         name="bulk",
-    )(*kept(pltpu.VMEM, state, forward, forcing, vel, stress))
+    )(*kept(pltpu.HBM, state, forward, source_id), *kept(pltpu.VMEM, table, vel, stress))
 
     normalizer = (events * rows * size) ** (-0.5)
-    state, totals = pl.pallas_call(
+    rows_changed = 28
+    changes, totals = pl.pallas_call(
         functools.partial(join_kernel, sizes, normalizer),
         out_shape=(
-            pltpu.VMEM(state.shape, f32),
+            pltpu.VMEM((rows_changed, events, depth), f32),
             pltpu.VMEM((2, depth), f32),
         ),
-        in_specs=[vmem] * 9,
+        in_specs=[vmem] * 8,
         out_specs=(vmem,) * 2,
-        input_output_aliases={0: 0},
         compiler_params=limits,
         name="join",
-    )(*kept(pltpu.VMEM, state, weights, sums, message_core, message_chip, got_core, got_chip, vel, stress))
+    )(*kept(pltpu.VMEM, weights, sums, message_chip, message_core, got_chip, got_core, vel, stress))
+
+    _, out = pl.pallas_call(
+        functools.partial(finish_kernel, sizes),
+        out_shape=(pltpu.VMEM(state.shape, f32), jax.ShapeDtypeStruct(state.shape, f32)),
+        in_specs=[vmem] * 2,
+        out_specs=(vmem, any_space),
+        input_output_aliases={0: 0},
+        scratch_shapes=[pltpu.SemaphoreType.DMA((fields,))],
+        compiler_params=limits,
+        cost_estimate=pl.CostEstimate(flops=0, bytes_accessed=2 * 4 * state.size, transcendentals=0),
+        name="finish",
+    )(*kept(pltpu.VMEM, state, changes))
     mask = 1
     while mask < size:
         totals = totals + swap_with(totals, size, mask | 1)
         mask *= 2
-    return state.reshape(adjoint_state.shape), totals
+    return out.reshape(adjoint_state.shape), totals
 
 
 def solution(mesh):

time: 22.8 us -> 21.8 us (0.956)
  Pallas kernels: 3.95 us -> 7.12 us
  waiting for transfers between devices: 5.47 us -> 3.85 us
  starting transfers between devices: 10.8 us -> 9.41 us
  local copies, waits for them, and re-layouts: 1.14 us -> 0 us
    pallas_call x1, Pallas kernels: 1.42 us -> 3.83 us  [shards(): pl.pallas_call(functools.partial(bulk_kernel, sizes), out_shape=(pltpu.VM...]
    ppermute x5, starting transfers between devices: 8.25 us -> 6.41 us  [swap_with(): return lax.ppermute(value, 'gx', [(i, i ^ mask) for i in range(size)])]
    ppermute x1, waiting for transfers between devices: 1.68 us -> 0.01 us  [swap_over_chips(): return lax.ppermute(value, ('groups', 'gx'), route)]
    pallas_call x0 -> x1, Pallas kernels: none -> 1.24 us  [shards(): pl.pallas_call(functools.partial(finish_kernel, sizes), out_shape=(pltpu....]
    unnamed x1 -> x0, local copies, waits for them, and re-layouts: 1.14 us -> none
    ppermute x1, starting transfers between devices: 2.56 us -> 3 us  [swap_over_chips(): return lax.ppermute(value, ('groups', 'gx'), route)]
    pallas_call x1, Pallas kernels: 1.89 us -> 1.64 us  [shards(): pl.pallas_call(functools.partial(edge_kernel, sizes), out_shape=(pltpu.VM...]
    pallas_call x1, Pallas kernels: 0.64 us -> 0.41 us  [shards(): pl.pallas_call(functools.partial(join_kernel, sizes, normalizer), out_sha...]
  transfers between devices with their start and end apart: 6 -> 6, of which waited for: 5 -> 4; matrix products, arithmetic and copies ran while one was open for 5% -> 0% of each run, Pallas kernels for 6% -> 23%
where the time goes in v3:
time: 21.8 us; the launch traced here: 21.6 us
  starting transfers between devices  9.41 us (43%)
  Pallas kernels  7.12 us (33%)
  waiting for transfers between devices  3.85 us (18%)
  between operations  0.68 us (3%)
  other arithmetic  0.57 us (3%)
    ppermute x5, starting transfers between devices, swap_with(): return lax.ppermute(value, 'gx', [(i, i ^ mask) for i in range(size)])  6.41 us
    ppermute x5, waiting for transfers between devices, swap_with(): return lax.ppermute(value, 'gx', [(i, i ^ mask) for i in range(size)])  3.85 us
    pallas_call x1, Pallas kernels, shards(): pl.pallas_call(functools.partial(bulk_kernel, sizes), out_shape=(pltpu.VM...  3.83 us
    ppermute x1, starting transfers between devices, swap_over_chips(): return lax.ppermute(value, ('groups', 'gx'), route)  3 us
    pallas_call x1, Pallas kernels, shards(): pl.pallas_call(functools.partial(edge_kernel, sizes), out_shape=(pltpu.VM...  1.64 us
    pallas_call x1, Pallas kernels, shards(): pl.pallas_call(functools.partial(finish_kernel, sizes), out_shape=(pltpu....  1.24 us
    add x4, other arithmetic, shards(): totals = totals + swap_with(totals, size, mask | 1)  0.57 us
  transfers between devices with their start and end apart: 6, of which 4 were waited for; matrix products, arithmetic and copies ran while one was open for 0% of the time, Pallas kernels for 23%

profile of v3, /device:TPU:0, one launch (start us, length us, event | category | flops | bytes accessed | tf_op | source)
XLA Modules:
  0.0 21.6 jit_solution(14106459333349082199)
XLA Ops:
  0.6 1.6 %edges.1 = (f32[128,128]{1,0:T(8,128)S(1)}, f32[288,128]{1,0:T(8,128)S(1)}, f32[288,128]{1,0:T(8,128)S(1)}, f32[4,128]{1,0:T(4,128)S(1)}, f32[4,128]{1,0:T(4,128)S(1)}) custom-call(f32[384,8,128]{2,1,0:T(8,128)} %bitcast.10, f32[4,128]{1,0:T(4,128)} %vel_hbm.1, f32[4,128]{1,0:T(4,128)} %stress_hbm.1, s32[2,128]{1,0:T(2,128)} %bitcast.14, ...), custom_call_target="tpu_custom_call" | custom-call | tf_op jit(solution)/shard_map/edges/pallas_call | solution.py:510
  2.3 3.0 %collective-permute-start = (f32[288,128]{1,0:T(8,128)S(1)}, f32[288,128]{1,0:T(8,128)S(1)}, u32[]{:S(2)}, u32[]{:S(2)}) collective-permute-start(f32[288,128]{1,0:T(8,128)S(1)} %get-tuple-element.19.sent_chip), channel_id=1, source_target_pairs={{1,2},{2,1},{3,4},{4,3},{5,6},{6,5},{7,8},{8,7},{9,10},{10,9},{11,... | collective-permute-start | bytes 442376 | tf_op jit(solution)/shard_map/ppermute | solution.py:481
  5.3 0.1 collective-permute-start.1
  5.4 3.8 %bulk.1 = (f32[8,384,128]{2,1,0:T(8,128)S(1)}, f32[6,384,128]{2,1,0:T(8,128)S(1)}, f32[16,128]{1,0:T(8,128)S(1)}) custom-call(f32[8,384,128]{2,1,0:T(8,128)} %bitcast.11, bf16[6,384,128]{2,1,0:T(8,128)(2,1)} %bitcast.12, s32[48]{0:T(128)} %source_hbm.3, f32[128,128]{1,0:T(8,128)S(1)} %get-tuple-element.13.table_ref, f32[4,128]{1,0:T(4,128)S(1)} %get-tuple-element.14.vel_ref, ...), custom_call_target="tpu_custom_call" | custom-call | flops 7864320 | bytes 3145728 | tf_op jit(solution)/shard_map/bulk/pallas_call | solution.py:547
  9.3 0.0 collective-permute-done.got_chip
  9.3 0.0 collective-permute-done.1.got_core
  9.3 0.4 %join.1 = (f32[28,48,128]{2,1,0:T(8,128)S(1)}, f32[2,128]{1,0:T(2,128)S(1)}) custom-call(f32[6,384,128]{2,1,0:T(8,128)S(1)} %get-tuple-element.17.weights, f32[16,128]{1,0:T(8,128)S(1)} %get-tuple-element.18.sums, f32[288,128]{1,0:T(8,128)S(1)} %get-tuple-element.19.sent_chip, f32[288,128]{1,0:T(8,128)S(1)} %get-tuple-element.20.sent_core, ...), custom_call_target="tpu_custom_call" | custom-call | tf_op jit(solution)/shard_map/join/pallas_call | solution.py:571
  9.7 0.4 %collective-permute-start.2 = (f32[2,128]{1,0:T(2,128)S(1)}, f32[2,128]{1,0:T(2,128)S(1)}, u32[]{:S(2)}, u32[]{:S(2)}) collective-permute-start(f32[2,128]{1,0:T(2,128)S(1)} %get-tuple-element.23), channel_id=1, source_target_pairs={{0,1},{1,0},{2,3},{3,2},{4,5},{5,4},{6,7},{7,6},{8,9},{9,8},{10,11... | collective-permute-start | bytes 3080 | tf_op jit(solution)/shard_map/ppermute | solution.py:470
  10.1 0.8 %collective-permute-done.2 = f32[2,128]{1,0:T(2,128)S(1)} collective-permute-done((f32[2,128]{1,0:T(2,128)S(1)}, f32[2,128]{1,0:T(2,128)S(1)}, u32[]{:S(2)}, u32[]{:S(2)}) %collective-permute-start.2) | collective-permute-done | bytes 1056 | tf_op jit(solution)/shard_map/ppermute | solution.py:470
  11.0 1.9 %collective-permute-start.3 = (f32[2,128]{1,0:T(2,128)S(1)}, f32[2,128]{1,0:T(2,128)S(1)}, u32[]{:S(2)}, u32[]{:S(2)}) collective-permute-start(f32[2,128]{1,0:T(2,128)S(1)} %add.12), channel_id=1, source_target_pairs={{0,3},{1,2},{2,1},{3,0},{4,7},{5,6},{6,5},{7,4},{8,11},{9,10},{10,... | collective-permute-start | bytes 3080 | tf_op jit(solution)/shard_map/ppermute | solution.py:470
  12.9 1.3 %collective-permute-done.3 = f32[2,128]{1,0:T(2,128)S(1)} collective-permute-done((f32[2,128]{1,0:T(2,128)S(1)}, f32[2,128]{1,0:T(2,128)S(1)}, u32[]{:S(2)}, u32[]{:S(2)}) %collective-permute-start.3) | collective-permute-done | bytes 1056 | tf_op jit(solution)/shard_map/ppermute | solution.py:470
  14.2 1.4 %collective-permute-start.4 = (f32[2,128]{1,0:T(2,128)S(1)}, f32[2,128]{1,0:T(2,128)S(1)}, u32[]{:S(2)}, u32[]{:S(2)}) collective-permute-start(f32[2,128]{1,0:T(2,128)S(1)} %add.13), channel_id=1, source_target_pairs={{0,5},{1,4},{2,7},{3,6},{4,1},{5,0},{6,3},{7,2},{8,13},{9,12},{10,... | collective-permute-start | bytes 3080 | tf_op jit(solution)/shard_map/ppermute | solution.py:470
  15.6 1.5 %collective-permute-done.4 = f32[2,128]{1,0:T(2,128)S(1)} collective-permute-done((f32[2,128]{1,0:T(2,128)S(1)}, f32[2,128]{1,0:T(2,128)S(1)}, u32[]{:S(2)}, u32[]{:S(2)}) %collective-permute-start.4) | collective-permute-done | bytes 1056 | tf_op jit(solution)/shard_map/ppermute | solution.py:470
  17.2 2.5 %collective-permute-start.5 = (f32[2,128]{1,0:T(2,128)S(1)}, f32[2,128]{1,0:T(2,128)S(1)}, u32[]{:S(2)}, u32[]{:S(2)}) collective-permute-start(f32[2,128]{1,0:T(2,128)S(1)} %add.14), channel_id=1, source_target_pairs={{0,9},{1,8},{2,11},{3,10},{4,13},{5,12},{6,15},{7,14},{8,1},{9,0},... | collective-permute-start | bytes 3080 | tf_op jit(solution)/shard_map/ppermute | solution.py:470
  19.6 1.2 %finish.1 = (f32[8,384,128]{2,1,0:T(8,128)S(1)}, f32[8,384,128]{2,1,0:T(8,128)}) custom-call(f32[8,384,128]{2,1,0:T(8,128)S(1)} %get-tuple-element.16.state_in, f32[28,48,128]{2,1,0:T(8,128)S(1)} %get-tuple-element.21.changes), custom_call_target="tpu_custom_call", output_to_operand_aliasing={{0}: (0, {})} | custom-call | bytes 3145728 | tf_op jit(solution)/shard_map/finish/pallas_call | solution.py:583
  20.9 0.2 collective-permute-done.5
  21.1 0.6 %add.15 = f32[2,128]{1,0:T(2,128)} add(f32[2,128]{1,0:T(2,128)S(1)} %add.14, f32[2,128]{1,0:T(2,128)S(1)} %collective-permute-done.5) | non-fusion elementwise | flops 256 | bytes 3072 | tf_op jit(solution)/shard_map/add | solution.py:596
  (3 shorter events, 0.0 us)
Async XLA Ops:
  2.3 7.0 %collective-permute-start = (f32[288,128]{1,0:T(8,128)S(1)}, f32[288,128]{1,0:T(8,128)S(1)}, u32[]{:S(2)}, u32[]{:S(2)}) collective-permute-start(f32[288,128]{1,0:T(8,128)S(1)} %get-tuple-element.19.sent_chip), channel_id=1, source_target_pairs={{1,2},{2,1},{3,4},{4,3},{5,6},{6,5},{7,8},{8,7},{9,10},{10,9},{11,... | collective-permute-start | bytes 442376 | tf_op jit(solution)/shard_map/ppermute | solution.py:481
  5.3 4.0 %collective-permute-start.1 = (f32[288,128]{1,0:T(8,128)S(1)}, f32[288,128]{1,0:T(8,128)S(1)}, u32[]{:S(2)}, u32[]{:S(2)}) collective-permute-start(f32[288,128]{1,0:T(8,128)S(1)} %get-tuple-element.20.sent_core), channel_id=1, source_target_pairs={{0,1},{1,0},{2,3},{3,2},{4,5},{5,4},{6,7},{7,6},{8,9},{9,8},{10,11... | collective-permute-start | bytes 442376 | tf_op jit(solution)/shard_map/ppermute | solution.py:470
  9.7 1.3 %collective-permute-start.2 = (f32[2,128]{1,0:T(2,128)S(1)}, f32[2,128]{1,0:T(2,128)S(1)}, u32[]{:S(2)}, u32[]{:S(2)}) collective-permute-start(f32[2,128]{1,0:T(2,128)S(1)} %get-tuple-element.23), channel_id=1, source_target_pairs={{0,1},{1,0},{2,3},{3,2},{4,5},{5,4},{6,7},{7,6},{8,9},{9,8},{10,11... | collective-permute-start | bytes 3080 | tf_op jit(solution)/shard_map/ppermute | solution.py:470
  11.0 3.2 %collective-permute-start.3 = (f32[2,128]{1,0:T(2,128)S(1)}, f32[2,128]{1,0:T(2,128)S(1)}, u32[]{:S(2)}, u32[]{:S(2)}) collective-permute-start(f32[2,128]{1,0:T(2,128)S(1)} %add.12), channel_id=1, source_target_pairs={{0,3},{1,2},{2,1},{3,0},{4,7},{5,6},{6,5},{7,4},{8,11},{9,10},{10,... | collective-permute-start | bytes 3080 | tf_op jit(solution)/shard_map/ppermute | solution.py:470
  14.2 3.0 %collective-permute-start.4 = (f32[2,128]{1,0:T(2,128)S(1)}, f32[2,128]{1,0:T(2,128)S(1)}, u32[]{:S(2)}, u32[]{:S(2)}) collective-permute-start(f32[2,128]{1,0:T(2,128)S(1)} %add.13), channel_id=1, source_target_pairs={{0,5},{1,4},{2,7},{3,6},{4,1},{5,0},{6,3},{7,2},{8,13},{9,12},{10,... | collective-permute-start | bytes 3080 | tf_op jit(solution)/shard_map/ppermute | solution.py:470
  17.2 3.9 %collective-permute-start.5 = (f32[2,128]{1,0:T(2,128)S(1)}, f32[2,128]{1,0:T(2,128)S(1)}, u32[]{:S(2)}, u32[]{:S(2)}) collective-permute-start(f32[2,128]{1,0:T(2,128)S(1)} %add.14), channel_id=1, source_target_pairs={{0,9},{1,8},{2,11},{3,10},{4,13},{5,12},{6,15},{7,14},{8,1},{9,0},... | collective-permute-start | bytes 3080 | tf_op jit(solution)/shard_map/ppermute | solution.py:470

commit v4 on v3

--- a/solution.py
+++ b/solution.py
@@ -97,7 +97,8 @@
     force_hbm,
     source_hbm,
     table_ref,
-    message_core,
+    message_first,
+    message_second,
     message_chip,
     vel_ref,
     stress_ref,
@@ -131,24 +132,28 @@
     lanes = cells.shape[1]
     local = cells[...] & (rows * depth - 1)
     slot = (local // depth) * LAYER + (local & (depth - 1)) - (depth - LAYER)
-    layers = None
+    blocks = cells.shape[0]
+    spots = lax.broadcasted_iota(jnp.int32, (depth, lanes), 0)
+    hits = [(spots == slot[i : i + 1, :]).astype(jnp.float32).astype(jnp.bfloat16) for i in range(blocks)]
     rest = force[...]
     pieces = []
     for _ in range(3):
         pieces.append(rest.astype(jnp.bfloat16))
         rest = rest - pieces[-1].astype(jnp.float32)
-    for block in range(cells.shape[0]):
-        spots = lax.broadcasted_iota(jnp.int32, (depth, lanes), 0)
-        hit = (spots == slot[block : block + 1, :]).astype(jnp.float32).astype(jnp.bfloat16)
-        part = None
-        for piece in pieces:
-            term = lax.dot_general(
-                piece, hit, (((1,), (1,)), ((), ())), preferred_element_type=jnp.float32
-            )
-            part = term if part is None else part + term
-        if block:
-            part = pltpu.roll(part, part.shape[0] - 2 * block, 0)
-        layers = part if layers is None else layers + part
+    terms = [
+        lax.dot_general(
+            jnp.concatenate(pieces, axis=0),
+            hit,
+            (((1,), (1,)), ((), ())),
+            preferred_element_type=jnp.float32,
+        )
+        for hit in hits
+    ]
+    count = force.shape[0]
+    terms = [t[:count] + t[count : 2 * count] + t[2 * count :] for t in terms]
+    layers = terms[0]
+    for block in range(1, blocks):
+        layers = layers + pltpu.roll(terms[block], count - 2 * block, 0)
     table_ref[...] = layers
     def moved(row):
         return at_row(layers, row, depth)
@@ -165,6 +170,7 @@
     vel = load_coeffs(vel_ref)
     stress = load_coeffs(stress_ref)
     odd = lax.rem(lax.axis_index("gx"), 2) == 1
+    message_core = (message_first, message_second)
     last = rows - 1
     state = near.reshape(near.shape[0] * rows, depth)
 
@@ -232,8 +238,13 @@
         left = [vel_first[0], vel_first[1], vel_first[2], again[0], again[1], again[2]]
         for i in range(HALO):
             at = pl.ds(i * events + chunk, 8)
-            message_core[at, :] = jnp.where(odd, left[i], right[i])
+            half = message_core[i // 3]
+            half[pl.ds(i % 3 * events + chunk, 8), :] = jnp.where(odd, left[i], right[i])
             message_chip[at, :] = jnp.where(odd, right[i], left[i])
+
+def group_of(events):
+    return next(g for g in GROUPS if events % g == 0)
+
 
 def bulk_kernel(
     sizes,
@@ -252,7 +263,7 @@
     sems,
 ):
     events, rows, depth, steps, _ = sizes
-    group = next(g for g in GROUPS if events % g == 0)
+    group = group_of(events)
 
     def copies(i):
         at = i * group * rows
@@ -262,7 +273,7 @@
             pltpu.make_async_copy(forward_hbm.at[:, own], forward.at[:, own], sems.at[1, i]),
         )
 
-    source_copy = pltpu.make_async_copy(source_hbm, source, sems.at[2, 0])
+    source_copy = pltpu.make_async_copy(source_hbm, source, sems.at[0, events // group])
     source_copy.start()
     for i in range(events // group):
         for copy in copies(i):
@@ -332,136 +343,171 @@
     sums[pl.ds(rows, rows), :] = poro
 
 
-def join_kernel(
-    sizes,
-    normalizer,
-    weights,
-    sums,
-    sent_chip,
-    sent_core,
-    got_chip,
-    got_core,
-    vel_ref,
-    stress_ref,
-    changes,
-    totals,
-):
+def from_before(vel, stress_x, stress_xz, pressure):
+    return velocity_gain(vel, -stress_x, -stress_xz, -pressure, 0.0)
+
+
+def forces(vel, stresses, flows):
+    return (
+        stresses[0] + depth_lower(stresses[2]),
+        stresses[2] + depth_lower(stresses[1]),
+        stresses[3] + vel[3] * flows[0],
+        depth_lower(stresses[3]) + vel[3] * flows[1],
+    )
+
+
+def strains(stress, vels, after):
+    return stress_gain(
+        stress,
+        after[0] - vels[0],
+        depth_upper(vels[1]),
+        after[2] - vels[2] + depth_upper(vels[3]),
+        depth_upper(vels[0]) + after[1] - vels[1],
+    )
+
+
+NOTHING = (0.0, 0.0, 0.0)
+
+
+def left_changes(vel, stress, sent, got, factor):
+    gain_first = from_before(vel, *got[:3])
+    before = beyond_gain(stress, *plus(sent[:3], gain_first[:3]))
+    before = plus(got[3:], (before[0], before[2], before[3]))
+    stress_first = strains(stress, gain_first, NOTHING)
+    vel_first = plus(
+        plus(gain_first, velocity_gain(vel, *forces(vel, stress_first, gain_first[2:]))),
+        from_before(vel, *before),
+    )
+    vel_second = from_before(vel, stress_first[0], stress_first[2], stress_first[3])
+    end_first = plus(stress_first, strains(stress, vel_first, vel_second))
+    end_second = strains(stress, vel_second, NOTHING)
+    perm = gain_first[2] * factor(0, 0, 0) + gain_first[3] * factor(0, 1, 0)
+    for row, vels in ((0, vel_first), (1, vel_second)):
+        perm = perm + vels[2] * factor(1, 0, row) + vels[3] * factor(1, 1, row)
+    poro = stress_first[3] * factor(0, 2, 0)
+    for row, stresses in ((0, end_first), (1, end_second)):
+        poro = poro + stresses[3] * factor(1, 2, row)
+    return vel_first + vel_second + end_first + end_second, perm, poro
+
+
+def right_changes(vel, stress, sent, got, factor, last):
+    gain_after = from_before(vel, *sent[:3])
+    stress_last = beyond_gain(stress, *plus(got[:3], gain_after[:3]))
+    true_last = plus(sent[3:], (stress_last[0], stress_last[2], stress_last[3]))
+    vel_last = velocity_gain(
+        vel,
+        stress_last[0] + depth_lower(stress_last[2]),
+        stress_last[2] + depth_lower(stress_last[1]),
+        stress_last[3],
+        depth_lower(stress_last[3]),
+    )
+    stress_after = strains(stress, gain_after, NOTHING)
+    again = plus(
+        plus(gain_after, velocity_gain(vel, *forces(vel, stress_after, gain_after[2:]))),
+        from_before(vel, *true_last),
+    )
+    again = plus(got[3:], again[:3])
+    end_inner = beyond_gain(stress, *vel_last[:3])
+    end_last = plus(stress_last, strains(stress, vel_last, again))
+    perm = vel_last[2] * factor(1, 0, last) + vel_last[3] * factor(1, 1, last)
+    poro = stress_last[3] * factor(0, 2, last)
+    for row, stresses in ((last - 1, end_inner), (last, end_last)):
+        poro = poro + stresses[3] * factor(1, 2, row)
+    return vel_last + end_inner + end_last, perm, poro
+
+
+def side_sums(sizes, over_chips, weights, sent, got, vel_ref, stress_ref, changes):
     events, rows, depth, _, _ = sizes
     vel = load_coeffs(vel_ref)
     stress = load_coeffs(stress_ref)
+    last = rows - 1
+    left, right = sides(over_chips)
+
+    def fill(changed, partial):
+        for chunk in range(0, events, 8):
+
+            def row_of(refs, i):
+                each = HALO // len(refs)
+                return refs[i // each][pl.ds(i % each * events + chunk, 8), :]
+
+            def factor(step, kind, row):
+                return weights[step * 3 + kind, pl.ds(chunk * rows + row, 8, stride=rows), :]
+
+            own = tuple(row_of(sent, i) for i in range(HALO))
+            new = tuple(row_of(got, i) for i in range(HALO))
+            values, perm, poro = changed(vel, stress, own, new, factor)
+            for i, value in enumerate(values):
+                changes[i, pl.ds(chunk, 8), :] = value
+            partial = (partial[0] + perm, partial[1] + poro)
+        return partial
+
+    zero = (jnp.zeros((8, depth), jnp.float32),) * 2
+    return lax.cond(
+        left,
+        lambda: fill(left_changes, zero),
+        lambda: lax.cond(
+            right, lambda: fill(functools.partial(right_changes, last=last), zero), lambda: zero
+        ),
+    )
+
+
+def sides(over_chips):
     place = lax.axis_index("gx")
     odd = lax.rem(place, 2) == 1
-    has_left = place > 0
-    has_right = place < lax.axis_size("gx") - 1
-    last = rows - 1
-    perm = sums[pl.ds(0, rows), :]
-    poro = sums[pl.ds(rows, rows), :]
-
-    def forces(stresses, flows):
-        return (
-            stresses[0] + depth_lower(stresses[2]),
-            stresses[2] + depth_lower(stresses[1]),
-            stresses[3] + vel[3] * flows[0],
-            depth_lower(stresses[3]) + vel[3] * flows[1],
-        )
-
-    def from_before(stress_x, stress_xz, pressure):
-        return velocity_gain(vel, -stress_x, -stress_xz, -pressure, 0.0)
-
-    def strains(vels, after):
-        return stress_gain(
-            stress,
-            after[0] - vels[0],
-            depth_upper(vels[1]),
-            after[2] - vels[2] + depth_upper(vels[3]),
-            depth_upper(vels[0]) + after[1] - vels[1],
-        )
-
-    for chunk in range(0, events, 8):
-
-        def row_of(ref, i):
-            return ref[pl.ds(i * events + chunk, 8), :]
-
-        own_core = [row_of(sent_core, i) for i in range(HALO)]
-        own_chip = [row_of(sent_chip, i) for i in range(HALO)]
-        new_core = [row_of(got_core, i) for i in range(HALO)]
-        new_chip = [row_of(got_chip, i) for i in range(HALO)]
-        left_own = [jnp.where(odd, a, b) for a, b in zip(own_core, own_chip)]
-        right_own = [jnp.where(odd, b, a) for a, b in zip(own_core, own_chip)]
-        left = [jnp.where(has_left, jnp.where(odd, a, b), 0.0) for a, b in zip(new_core, new_chip)]
-        right = [jnp.where(has_right, jnp.where(odd, b, a), 0.0) for a, b in zip(new_core, new_chip)]
-
-        gain_first = from_before(*left[:3])
-        true_first = plus(left_own[:3], gain_first[:3])
-        before = beyond_gain(stress, *true_first)
-        before = [
-            jnp.where(has_left, a + b, 0.0)
-            for a, b in zip(left[3:], (before[0], before[2], before[3]))
-        ]
-        nothing = (0.0, 0.0, 0.0)
-        stress_first = strains(gain_first, nothing)
-        gain_after = from_before(*right_own[:3])
-        after = plus(right[:3], gain_after[:3])
-        after = [jnp.where(has_right, a, 0.0) for a in after]
-        stress_last = beyond_gain(stress, *after)
-        true_last = plus(right_own[3:], (stress_last[0], stress_last[2], stress_last[3]))
-
-        vel_first = plus(
-            plus(gain_first, velocity_gain(vel, *forces(stress_first, gain_first[2:]))),
-            from_before(*before),
-        )
-        vel_second = from_before(stress_first[0], stress_first[2], stress_first[3])
-        vel_last = velocity_gain(
-            vel,
-            stress_last[0] + depth_lower(stress_last[2]),
-            stress_last[2] + depth_lower(stress_last[1]),
-            stress_last[3],
-            depth_lower(stress_last[3]),
-        )
-        stress_after = strains(gain_after, nothing)
-        again = plus(
-            plus(gain_after, velocity_gain(vel, *forces(stress_after, gain_after[2:]))),
-            from_before(*true_last),
-        )
-        again = [jnp.where(has_right, a + b, 0.0) for a, b in zip(right[3:], again)]
-        end_first = plus(stress_first, strains(vel_first, vel_second))
-        end_second = strains(vel_second, nothing)
-        end_inner = beyond_gain(stress, *vel_last[:3])
-        end_last = plus(stress_last, strains(vel_last, again))
-
-        def factor(step, kind, row):
-            return weights[step * 3 + kind, pl.ds(chunk * rows + row, 8, stride=rows), :]
-
-        perm = perm + gain_first[2] * factor(0, 0, 0) + gain_first[3] * factor(0, 1, 0)
-        for row, vels in ((0, vel_first), (1, vel_second), (last, vel_last)):
-            perm = perm + vels[2] * factor(1, 0, row) + vels[3] * factor(1, 1, row)
-        poro = poro + stress_first[3] * factor(0, 2, 0) + stress_last[3] * factor(0, 2, last)
-        ends = ((0, end_first), (1, end_second), (last - 1, end_inner), (last, end_last))
-        for row, stresses in ends:
-            poro = poro + stresses[3] * factor(1, 2, row)
-
-        values = vel_first + vel_second + vel_last + end_first + end_second + end_inner + end_last
-        for i, value in enumerate(values):
-            changes[i, pl.ds(chunk, 8), :] = value
-
-    perm = jnp.sum(perm, axis=0, keepdims=True) * (vel[2] * vel[3] * normalizer)
-    poro = jnp.sum(poro, axis=0, keepdims=True) * (stress[3] * normalizer)
-    totals[pl.ds(0, 1), :] = perm
-    totals[pl.ds(1, 1), :] = poro
-
-
-def finish_kernel(sizes, state_in, changes, state, out_hbm, sems):
+    if over_chips:
+        return jnp.logical_and(jnp.logical_not(odd), place > 0), jnp.logical_and(
+            odd, place < lax.axis_size("gx") - 1
+        )
+    return odd, jnp.logical_not(odd)
+
+
+def core_kernel(
+    sizes, sums_in, weights, sent_a, sent_b, got_a, got_b, vel_ref, stress_ref, changes, sums
+):
+    rows = sizes[1]
+    sent, got = (sent_a, sent_b), (got_a, got_b)
+    perm, poro = side_sums(sizes, False, weights, sent, got, vel_ref, stress_ref, changes)
+    sums[pl.ds(0, rows), :] = sums_in[pl.ds(0, rows), :] + perm
+    sums[pl.ds(rows, rows), :] = sums_in[pl.ds(rows, rows), :] + poro
+
+
+def chip_kernel(
+    sizes, normalizer, sums, weights, sent, got, vel_ref, stress_ref, changes, totals
+):
+    rows = sizes[1]
+    vel = load_coeffs(vel_ref)
+    stress = load_coeffs(stress_ref)
+    perm, poro = side_sums(sizes, True, weights, (sent,), (got,), vel_ref, stress_ref, changes)
+    perm = jnp.sum(sums[pl.ds(0, rows), :] + perm, axis=0, keepdims=True)
+    poro = jnp.sum(sums[pl.ds(rows, rows), :] + poro, axis=0, keepdims=True)
+    totals[pl.ds(0, 1), :] = perm * (vel[2] * vel[3] * normalizer)
+    totals[pl.ds(1, 1), :] = poro * (stress[3] * normalizer)
+
+
+def finish_kernel(sizes, state_in, changes_core, changes_chip, state, out_hbm, done, sems):
     events, rows, _, _, _ = sizes
     last = rows - 1
-    places = [(start, row, f) for start, ends in ((0, (0, 1, last)), (4, (0, 1, last - 1, last))) for row in ends for f in range(4)]
-    copies = []
-    for field in range(FIELDS):
-        for i, (start, row, f) in enumerate(places):
-            if start + f == field:
+    left_places = [(s + f, row) for s in (0, 4) for row in (0, 1) for f in range(4)]
+    right_places = [(f, last) for f in range(4)] + [(4 + f, row) for row in (last - 1, last) for f in range(4)]
+
+    def patch(changes, places, fields):
+        for i, (field, row) in enumerate(places):
+            if field in fields:
                 at = pl.ds(row, events, stride=rows)
                 state[field, at, :] = state_in[field, at, :] + changes[i]
-        copies.append(pltpu.make_async_copy(state.at[field], out_hbm.at[field], sems.at[field]))
-        copies[-1].start()
+
+    half = FIELDS // 2
+    copies = []
+    for i in range(2):
+        fields = range(i * half, (i + 1) * half)
+        for over_chips, changes in ((False, changes_core), (True, changes_chip)):
+            left, right = sides(over_chips)
+            pl.when(left)(functools.partial(patch, changes, left_places, fields))
+            pl.when(right)(functools.partial(patch, changes, right_places, fields))
+        own = pl.ds(i * half, half)
+        copies.append(pltpu.make_async_copy(state.at[own], out_hbm.at[own], sems.at[i]))
+        copies[i].start()
+    done[...] = jnp.zeros_like(done)
     for copy in copies:
         copy.wait()
 
@@ -493,6 +539,7 @@
     sizes = (events, rows, depth, steps, sources)
     blocks = entries // 128
     tiles = events * rows
+    group = group_of(events)
     f32 = jnp.float32
     any_space = pl.BlockSpec(memory_space=pl.ANY)
     vmem = pl.BlockSpec(memory_space=pltpu.VMEM)
@@ -502,22 +549,24 @@
     force = drm_force.reshape(sources * steps, 2, blocks, 128).transpose(0, 2, 1, 3)
     force = force.reshape(sources * steps * 2 * blocks, 128)
     message = pltpu.VMEM((HALO * events, depth), f32)
+    half = pltpu.VMEM((HALO // 2 * events, depth), f32)
     limits = pltpu.CompilerParams(vmem_limit_bytes=ROOM)
 
     def kept(space, *values):
         return tuple(pltpu.with_memory_space_constraint(v, space) for v in values)
 
-    table, message_core, message_chip, vel, stress = pl.pallas_call(
+    table, message_first, message_second, message_chip, vel, stress = pl.pallas_call(
         functools.partial(edge_kernel, sizes),
         out_shape=(
             pltpu.VMEM(force.shape, f32),
-            message,
+            half,
+            half,
             message,
             pltpu.VMEM(vel_coeffs.shape, f32),
             pltpu.VMEM(stress_coeffs.shape, f32),
         ),
         in_specs=[any_space] * 6,
-        out_specs=(vmem,) * 5,
+        out_specs=(vmem,) * 6,
         scratch_shapes=[
             pltpu.VMEM((fields * events, rows, depth), f32),
             pltpu.VMEM(cells.shape, jnp.int32),
@@ -541,7 +590,8 @@
         )
     )
 
-    got_core = swap_with(message_core, size, 1)
+    got_first = swap_with(message_first, size, 1)
+    got_second = swap_with(message_second, size, 1)
     got_chip = swap_over_chips(message_chip, groups, size)
 
     state, weights, sums = pl.pallas_call(
@@ -557,7 +607,7 @@
             pltpu.VMEM(forward.shape, forward.dtype),
             pltpu.VMEM((force.shape[0] * rows, depth), f32),
             pltpu.SMEM(source_id.shape, jnp.int32),
-            pltpu.SemaphoreType.DMA((3, events)),
+            pltpu.SemaphoreType.DMA((2, events // group + 1)),
         ],
         compiler_params=limits,
         cost_estimate=pl.CostEstimate(
@@ -567,33 +617,58 @@
     )(*kept(pltpu.HBM, state, forward, source_id), *kept(pltpu.VMEM, table, vel, stress))
 
     normalizer = (events * rows * size) ** (-0.5)
-    rows_changed = 28
-    changes, totals = pl.pallas_call(
-        functools.partial(join_kernel, sizes, normalizer),
-        out_shape=(
-            pltpu.VMEM((rows_changed, events, depth), f32),
-            pltpu.VMEM((2, depth), f32),
-        ),
+    changed = pltpu.VMEM((16, events, depth), f32)
+    changes_core, sums = pl.pallas_call(
+        functools.partial(core_kernel, sizes),
+        out_shape=(changed, pltpu.VMEM(sums.shape, f32)),
         in_specs=[vmem] * 8,
         out_specs=(vmem,) * 2,
         compiler_params=limits,
-        name="join",
-    )(*kept(pltpu.VMEM, weights, sums, message_chip, message_core, got_chip, got_core, vel, stress))
-
-    _, out = pl.pallas_call(
+        name="join_core",
+    )(
+        *kept(
+            pltpu.VMEM,
+            sums,
+            weights,
+            message_first,
+            message_second,
+            got_first,
+            got_second,
+            vel,
+            stress,
+        )
+    )
+
+    changes_chip, totals = pl.pallas_call(
+        functools.partial(chip_kernel, sizes, normalizer),
+        out_shape=(changed, pltpu.VMEM((2, depth), f32)),
+        in_specs=[vmem] * 6,
+        out_specs=(vmem,) * 2,
+        compiler_params=limits,
+        name="join_chip",
+    )(*kept(pltpu.VMEM, sums, weights, message_chip, got_chip, vel, stress))
+
+    _, out, done = pl.pallas_call(
         functools.partial(finish_kernel, sizes),
-        out_shape=(pltpu.VMEM(state.shape, f32), jax.ShapeDtypeStruct(state.shape, f32)),
-        in_specs=[vmem] * 2,
-        out_specs=(vmem, any_space),
+        out_shape=(
+            pltpu.VMEM(state.shape, f32),
+            jax.ShapeDtypeStruct(state.shape, f32),
+            pltpu.VMEM((2, depth), f32),
+        ),
+        in_specs=[vmem] * 3,
+        out_specs=(vmem, any_space, vmem),
         input_output_aliases={0: 0},
-        scratch_shapes=[pltpu.SemaphoreType.DMA((fields,))],
+        scratch_shapes=[pltpu.SemaphoreType.DMA((2,))],
         compiler_params=limits,
         cost_estimate=pl.CostEstimate(flops=0, bytes_accessed=2 * 4 * state.size, transcendentals=0),
         name="finish",
-    )(*kept(pltpu.VMEM, state, changes))
+    )(*kept(pltpu.VMEM, state, changes_core, changes_chip))
+
     mask = 1
     while mask < size:
         totals = totals + swap_with(totals, size, mask | 1)
+        if mask * 4 == size:
+            totals = totals + done
         mask *= 2
     return out.reshape(adjoint_state.shape), totals
 

time: 21.8 us -> 21.6 us (level)
  Pallas kernels: 7.12 us -> 5.64 us
  starting transfers between devices: 9.41 us -> 10.7 us
    ppermute x5 -> x6, starting transfers between devices: 6.41 us -> 7.68 us  [swap_with(): return lax.ppermute(value, 'gx', [(i, i ^ mask) for i in range(size)])]
    pallas_call x1, Pallas kernels: 3.83 us -> 2.58 us  [shards(): pl.pallas_call(functools.partial(bulk_kernel, sizes), out_shape=(pltpu.VM...]
    ppermute x5 -> x6, waiting for transfers between devices: 3.85 us -> 3.87 us  [swap_with(): return lax.ppermute(value, 'gx', [(i, i ^ mask) for i in range(size)])]
    add x4 -> x3, other arithmetic: 0.57 us -> 0.57 us  [shards(): totals = totals + swap_with(totals, size, mask | 1)]
  transfers between devices with their start and end apart: 6 -> 7, of which waited for: 4 -> 4; matrix products, arithmetic and copies ran while one was open for 0% -> 0% of each run, Pallas kernels for 23% -> 19%
where the time goes in v4:
time: 21.6 us; the launch traced here: 21.5 us
  starting transfers between devices  10.7 us (50%)
  Pallas kernels  5.64 us (26%)
  waiting for transfers between devices  3.87 us (18%)
  between operations  0.7 us (3%)
  other arithmetic  0.58 us (3%)
    ppermute x6, starting transfers between devices, swap_with(): return lax.ppermute(value, 'gx', [(i, i ^ mask) for i in range(size)])  7.68 us
    ppermute x6, waiting for transfers between devices, swap_with(): return lax.ppermute(value, 'gx', [(i, i ^ mask) for i in range(size)])  3.87 us
    ppermute x1, starting transfers between devices, swap_over_chips(): return lax.ppermute(value, ('groups', 'gx'), route)  3 us
    pallas_call x1, Pallas kernels, shards(): pl.pallas_call(functools.partial(bulk_kernel, sizes), out_shape=(pltpu.VM...  2.58 us
    pallas_call x1, Pallas kernels, shards(): pl.pallas_call(functools.partial(edge_kernel, sizes), out_shape=(pltpu.VM...  1.59 us
    pallas_call x1, Pallas kernels, shards(): pl.pallas_call(functools.partial(finish_kernel, sizes), out_shape=(pltpu....  1.21 us
    add x3, other arithmetic, shards(): totals = totals + swap_with(totals, size, mask | 1)  0.57 us
  transfers between devices with their start and end apart: 7, of which 4 were waited for; matrix products, arithmetic and copies ran while one was open for 0% of the time, Pallas kernels for 19%

profile of v4, /device:TPU:0, one launch (start us, length us, event | category | flops | bytes accessed | tf_op | source)
XLA Modules:
  0.0 21.5 jit_solution(5536306817049451043)
XLA Ops:
  0.6 1.6 %edges.1 = (f32[128,128]{1,0:T(8,128)S(1)}, f32[144,128]{1,0:T(8,128)S(1)}, f32[144,128]{1,0:T(8,128)S(1)}, f32[288,128]{1,0:T(8,128)S(1)}, f32[4,128]{1,0:T(4,128)S(1)}, /*index=5*/f32[4,128]{1,0:T(4,128)S(1)}) custom-call(f32[384,8,128]{2,1,0:T(8,128)} %bitcast.10, f32[4,128]{1,0:T(4,128)} %vel_hbm.1, f32[4,128]{1,0:T(4,128)} %stress_hbm.1, ...), custom_call_target="tpu_custom_call" | custom-call | tf_op jit(solution)/shard_map/edges/pallas_call | solution.py:558
  2.2 3.0 %collective-permute-start.2 = (f32[288,128]{1,0:T(8,128)S(1)}, f32[288,128]{1,0:T(8,128)S(1)}, u32[]{:S(2)}, u32[]{:S(2)}) collective-permute-start(f32[288,128]{1,0:T(8,128)S(1)} %get-tuple-element.27.sent), channel_id=1, source_target_pairs={{1,2},{2,1},{3,4},{4,3},{5,6},{6,5},{7,8},{8,7},{9,10},{10,9},{11,... | collective-permute-start | bytes 442376 | tf_op jit(solution)/shard_map/ppermute | solution.py:527
  5.2 0.1 collective-permute-start
  5.4 0.4 %collective-permute-start.1 = (f32[144,128]{1,0:T(8,128)S(1)}, f32[144,128]{1,0:T(8,128)S(1)}, u32[]{:S(2)}, u32[]{:S(2)}) collective-permute-start(f32[144,128]{1,0:T(8,128)S(1)} %get-tuple-element.24.sent_b), channel_id=1, source_target_pairs={{0,1},{1,0},{2,3},{3,2},{4,5},{5,4},{6,7},{7,6},{8,9},{9,8},{10,11... | collective-permute-start | bytes 221192 | tf_op jit(solution)/shard_map/ppermute | solution.py:516
  5.7 2.6 %bulk.1 = (f32[8,384,128]{2,1,0:T(8,128)S(1)}, f32[6,384,128]{2,1,0:T(8,128)S(1)}, f32[16,128]{1,0:T(8,128)S(1)}) custom-call(f32[8,384,128]{2,1,0:T(8,128)} %bitcast.11, bf16[6,384,128]{2,1,0:T(8,128)(2,1)} %bitcast.12, s32[48]{0:T(128)} %source_hbm.3, f32[128,128]{1,0:T(8,128)S(1)} %get-tuple-element.17.table_ref, f32[4,128]{1,0:T(4,128)S(1)} %get-tuple-element.18.vel_ref, ...), custom_call_target="tpu_custom_call" | custom-call | flops 7864320 | bytes 3145728 | tf_op jit(solution)/shard_map/bulk/pallas_call | solution.py:597
  8.3 0.0 collective-permute-done.got_a
  8.3 0.0 collective-permute-done.1.got_b
  8.4 0.2 %join_core.1 = (f32[16,48,128]{2,1,0:T(8,128)S(1)}, f32[16,128]{1,0:T(8,128)S(1)}) custom-call(f32[16,128]{1,0:T(8,128)S(1)} %get-tuple-element.21.sums_in, f32[6,384,128]{2,1,0:T(8,128)S(1)} %get-tuple-element.22.weights, f32[144,128]{1,0:T(8,128)S(1)} %get-tuple-element.23.sent_a, f32[144,128]{1,0:T(8,128)S(1)} %get-tuple-element.24.sent_b, ...), custom_call_target="tpu_custom_call" | custom-call | tf_op jit(solution)/shard_map/join_core/pallas_call | solution.py:621
  8.6 0.0 collective-permute-done.2.got
  8.6 0.7 %collective-permute-start.3 = (f32[2,128]{1,0:T(2,128)S(1)}, f32[2,128]{1,0:T(2,128)S(1)}, u32[]{:S(2)}, u32[]{:S(2)}) collective-permute-start(f32[2,128]{1,0:T(2,128)S(1)} %get-tuple-element.30), channel_id=1, source_target_pairs={{0,1},{1,0},{2,3},{3,2},{4,5},{5,4},{6,7},{7,6},{8,9},{9,8},{10,11... | collective-permute-start | bytes 3080 | tf_op jit(solution)/shard_map/ppermute | solution.py:516
  9.3 0.8 %collective-permute-done.3 = f32[2,128]{1,0:T(2,128)S(1)} collective-permute-done((f32[2,128]{1,0:T(2,128)S(1)}, f32[2,128]{1,0:T(2,128)S(1)}, u32[]{:S(2)}, u32[]{:S(2)}) %collective-permute-start.3) | collective-permute-done | bytes 1056 | tf_op jit(solution)/shard_map/ppermute | solution.py:516
  10.2 2.5 %collective-permute-start.4 = (f32[2,128]{1,0:T(2,128)S(1)}, f32[2,128]{1,0:T(2,128)S(1)}, u32[]{:S(2)}, u32[]{:S(2)}) collective-permute-start(f32[2,128]{1,0:T(2,128)S(1)} %add.15), channel_id=1, source_target_pairs={{0,3},{1,2},{2,1},{3,0},{4,7},{5,6},{6,5},{7,4},{8,11},{9,10},{10,... | collective-permute-start | bytes 3080 | tf_op jit(solution)/shard_map/ppermute | solution.py:516
  12.7 1.3 %collective-permute-done.4 = f32[2,128]{1,0:T(2,128)S(1)} collective-permute-done((f32[2,128]{1,0:T(2,128)S(1)}, f32[2,128]{1,0:T(2,128)S(1)}, u32[]{:S(2)}, u32[]{:S(2)}) %collective-permute-start.4) | collective-permute-done | bytes 1056 | tf_op jit(solution)/shard_map/ppermute | solution.py:516
  14.0 1.5 %collective-permute-start.5 = (f32[2,128]{1,0:T(2,128)S(1)}, f32[2,128]{1,0:T(2,128)S(1)}, u32[]{:S(2)}, u32[]{:S(2)}) collective-permute-start(f32[2,128]{1,0:T(2,128)S(1)} %add.16), channel_id=1, source_target_pairs={{0,5},{1,4},{2,7},{3,6},{4,1},{5,0},{6,3},{7,2},{8,13},{9,12},{10,... | collective-permute-start | bytes 3080 | tf_op jit(solution)/shard_map/ppermute | solution.py:516
  15.5 1.2 %finish.1 = (f32[8,384,128]{2,1,0:T(8,128)S(1)}, f32[8,384,128]{2,1,0:T(8,128)}, f32[2,128]{1,0:T(2,128)S(1)}) custom-call(f32[8,384,128]{2,1,0:T(8,128)S(1)} %get-tuple-element.20.state_in, f32[16,48,128]{2,1,0:T(8,128)S(1)} %get-tuple-element.25.changes_core, f32[16,48,128]{2,1,0:T(8,128)S(1)} %get-tuple-element.28.changes_chip), custom_call_target="tpu_custom_call", output_to_operand_aliasing={{0}: (0, {})} | custom-call | bytes 3145728 | tf_op jit(solution)/shard_map/finish/pallas_call | solution.py:651
  16.7 0.3 %collective-permute-done.5 = f32[2,128]{1,0:T(2,128)S(1)} collective-permute-done((f32[2,128]{1,0:T(2,128)S(1)}, f32[2,128]{1,0:T(2,128)S(1)}, u32[]{:S(2)}, u32[]{:S(2)}) %collective-permute-start.5) | collective-permute-done | bytes 1056 | tf_op jit(solution)/shard_map/ppermute | solution.py:516
  17.0 2.5 %collective-permute-start.6 = (f32[2,128]{1,0:T(2,128)S(1)}, f32[2,128]{1,0:T(2,128)S(1)}, u32[]{:S(2)}, u32[]{:S(2)}) collective-permute-start(f32[2,128]{1,0:T(2,128)S(1)} %add_add_fusion), channel_id=1, source_target_pairs={{0,9},{1,8},{2,11},{3,10},{4,13},{5,12},{6,15},{7,14},{8,1},{9,0},... | collective-permute-start | bytes 3080 | tf_op jit(solution)/shard_map/ppermute | solution.py:516
  19.5 1.4 %collective-permute-done.6 = f32[2,128]{1,0:T(2,128)S(1)} collective-permute-done((f32[2,128]{1,0:T(2,128)S(1)}, f32[2,128]{1,0:T(2,128)S(1)}, u32[]{:S(2)}, u32[]{:S(2)}) %collective-permute-start.6) | collective-permute-done | bytes 1056 | tf_op jit(solution)/shard_map/ppermute | solution.py:516
  20.9 0.6 %add.19 = f32[2,128]{1,0:T(2,128)} add(f32[2,128]{1,0:T(2,128)S(1)} %add_add_fusion, f32[2,128]{1,0:T(2,128)S(1)} %collective-permute-done.6) | non-fusion elementwise | flops 256 | bytes 3072 | tf_op jit(solution)/shard_map/add | solution.py:669
  (4 shorter events, 0.0 us)
Async XLA Ops:
  2.2 6.4 %collective-permute-start.2 = (f32[288,128]{1,0:T(8,128)S(1)}, f32[288,128]{1,0:T(8,128)S(1)}, u32[]{:S(2)}, u32[]{:S(2)}) collective-permute-start(f32[288,128]{1,0:T(8,128)S(1)} %get-tuple-element.27.sent), channel_id=1, source_target_pairs={{1,2},{2,1},{3,4},{4,3},{5,6},{6,5},{7,8},{8,7},{9,10},{10,9},{11,... | collective-permute-start | bytes 442376 | tf_op jit(solution)/shard_map/ppermute | solution.py:527
  5.2 3.1 %collective-permute-start = (f32[144,128]{1,0:T(8,128)S(1)}, f32[144,128]{1,0:T(8,128)S(1)}, u32[]{:S(2)}, u32[]{:S(2)}) collective-permute-start(f32[144,128]{1,0:T(8,128)S(1)} %get-tuple-element.23.sent_a), channel_id=1, source_target_pairs={{0,1},{1,0},{2,3},{3,2},{4,5},{5,4},{6,7},{7,6},{8,9},{9,8},{10,11... | collective-permute-start | bytes 221192 | tf_op jit(solution)/shard_map/ppermute | solution.py:516
  5.4 3.0 %collective-permute-start.1 = (f32[144,128]{1,0:T(8,128)S(1)}, f32[144,128]{1,0:T(8,128)S(1)}, u32[]{:S(2)}, u32[]{:S(2)}) collective-permute-start(f32[144,128]{1,0:T(8,128)S(1)} %get-tuple-element.24.sent_b), channel_id=1, source_target_pairs={{0,1},{1,0},{2,3},{3,2},{4,5},{5,4},{6,7},{7,6},{8,9},{9,8},{10,11... | collective-permute-start | bytes 221192 | tf_op jit(solution)/shard_map/ppermute | solution.py:516
  8.6 1.5 %collective-permute-start.3 = (f32[2,128]{1,0:T(2,128)S(1)}, f32[2,128]{1,0:T(2,128)S(1)}, u32[]{:S(2)}, u32[]{:S(2)}) collective-permute-start(f32[2,128]{1,0:T(2,128)S(1)} %get-tuple-element.30), channel_id=1, source_target_pairs={{0,1},{1,0},{2,3},{3,2},{4,5},{5,4},{6,7},{7,6},{8,9},{9,8},{10,11... | collective-permute-start | bytes 3080 | tf_op jit(solution)/shard_map/ppermute | solution.py:516
  10.2 3.8 %collective-permute-start.4 = (f32[2,128]{1,0:T(2,128)S(1)}, f32[2,128]{1,0:T(2,128)S(1)}, u32[]{:S(2)}, u32[]{:S(2)}) collective-permute-start(f32[2,128]{1,0:T(2,128)S(1)} %add.15), channel_id=1, source_target_pairs={{0,3},{1,2},{2,1},{3,0},{4,7},{5,6},{6,5},{7,4},{8,11},{9,10},{10,... | collective-permute-start | bytes 3080 | tf_op jit(solution)/shard_map/ppermute | solution.py:516
  14.0 3.0 %collective-permute-start.5 = (f32[2,128]{1,0:T(2,128)S(1)}, f32[2,128]{1,0:T(2,128)S(1)}, u32[]{:S(2)}, u32[]{:S(2)}) collective-permute-start(f32[2,128]{1,0:T(2,128)S(1)} %add.16), channel_id=1, source_target_pairs={{0,5},{1,4},{2,7},{3,6},{4,1},{5,0},{6,3},{7,2},{8,13},{9,12},{10,... | collective-permute-start | bytes 3080 | tf_op jit(solution)/shard_map/ppermute | solution.py:516
  17.0 3.9 %collective-permute-start.6 = (f32[2,128]{1,0:T(2,128)S(1)}, f32[2,128]{1,0:T(2,128)S(1)}, u32[]{:S(2)}, u32[]{:S(2)}) collective-permute-start(f32[2,128]{1,0:T(2,128)S(1)} %add_add_fusion), channel_id=1, source_target_pairs={{0,9},{1,8},{2,11},{3,10},{4,13},{5,12},{6,15},{7,14},{8,1},{9,0},... | collective-permute-start | bytes 3080 | tf_op jit(solution)/shard_map/ppermute | solution.py:516

commit v5 on v4

--- a/solution.py
+++ b/solution.py
@@ -11,6 +11,8 @@
 FIELDS = 8
 VX, VZ, QX, QZ, SXX, SZZ, SXZ, PR = range(FIELDS)
 HALO = 6
+SOON = 5
+LATE = 3
 PUSHED = ((0, 0), (0, 1), (1, 0), (0, -1))
 GROUPS = (16, 8, 4, 2)
 ROOM = 16 << 20
@@ -88,21 +90,35 @@
     return jnp.where(lane >= depth - LAYER, moved, 0.0)
 
 
+def exact_pieces(values):
+    pieces = []
+    for _ in range(3):
+        pieces.append(values.astype(jnp.bfloat16))
+        values = values - pieces[-1].astype(jnp.float32)
+    return pieces
+
+
 def edge_kernel(
     sizes,
     state_hbm,
+    forward_hbm,
     vel_hbm,
     stress_hbm,
     cells_hbm,
     force_hbm,
     source_hbm,
+    row_hbm,
+    forward,
+    source_row,
     table_ref,
     message_first,
     message_second,
     message_chip,
+    message_late,
     vel_ref,
     stress_ref,
     near,
+    weights,
     cells,
     force,
     near_force,
@@ -111,6 +127,7 @@
     sems,
 ):
     events, rows, depth, steps, sources = sizes
+    final_kind = steps * 3 - 1
     copies = [
         pltpu.make_async_copy(src, dst, sems.at[i])
         for i, (src, dst) in enumerate(
@@ -122,6 +139,9 @@
                 (stress_hbm, stress_ref),
                 (state_hbm.at[:, pl.ds(0, 2)], near.at[:, pl.ds(0, 2)]),
                 (state_hbm.at[:, pl.ds(rows - 2, 2)], near.at[:, pl.ds(rows - 2, 2)]),
+                (forward_hbm.at[pl.ds(final_kind, 1)], forward.at[pl.ds(final_kind, 1)]),
+                (row_hbm, source_row),
+                (forward_hbm.at[pl.ds(0, final_kind)], forward.at[pl.ds(0, final_kind)]),
             ]
         )
     ]
@@ -135,11 +155,7 @@
     blocks = cells.shape[0]
     spots = lax.broadcasted_iota(jnp.int32, (depth, lanes), 0)
     hits = [(spots == slot[i : i + 1, :]).astype(jnp.float32).astype(jnp.bfloat16) for i in range(blocks)]
-    rest = force[...]
-    pieces = []
-    for _ in range(3):
-        pieces.append(rest.astype(jnp.bfloat16))
-        rest = rest - pieces[-1].astype(jnp.float32)
+    pieces = exact_pieces(force[...])
     terms = [
         lax.dot_general(
             jnp.concatenate(pieces, axis=0),
@@ -165,8 +181,9 @@
     for event in range(events):
         record = pl.multiple_of(source[event] * rows, rows)
         pushes[pl.ds(event * rows, rows), :] = near_force[pl.ds(record, rows), :]
-    for copy in copies[3:]:
+    for copy in copies[3:-1]:
         copy.wait()
+    weights[...] = forward[final_kind].astype(jnp.float32)
     vel = load_coeffs(vel_ref)
     stress = load_coeffs(stress_ref)
     odd = lax.rem(lax.axis_index("gx"), 2) == 1
@@ -237,10 +254,20 @@
         right = [final[SXX], final[SXZ], final[PR], stress_final[0], stress_final[2], stress_final[3]]
         left = [vel_first[0], vel_first[1], vel_first[2], again[0], again[1], again[2]]
         for i in range(HALO):
-            at = pl.ds(i * events + chunk, 8)
             half = message_core[i // 3]
             half[pl.ds(i % 3 * events + chunk, 8), :] = jnp.where(odd, left[i], right[i])
-            message_chip[at, :] = jnp.where(odd, right[i], left[i])
+        flow = vel[1] * stress_final[0] + vel[2] * stress_final[3]
+        drain = stress[2] * again[0] + stress[3] * again[2]
+        weight = weights[pl.ds(chunk * rows, 8, stride=rows), :]
+        right_soon = right[:3] + [flow, stress_final[2]]
+        left_soon = left[:3] + [drain, weight]
+        right_late = [stress_final[0], stress_final[3], stress_final[3]]
+        for i in range(SOON):
+            message_chip[pl.ds(i * events + chunk, 8), :] = jnp.where(odd, right_soon[i], left_soon[i])
+        for i in range(LATE):
+            message_late[pl.ds(i * events + chunk, 8), :] = jnp.where(odd, right_late[i], left[3 + i])
+    copies[-1].wait()
+
 
 def group_of(events):
     return next(g for g in GROUPS if events % g == 0)
@@ -248,39 +275,44 @@
 
 def bulk_kernel(
     sizes,
-    state_hbm,
-    forward_hbm,
-    source_hbm,
+    state_in,
+    forward,
+    source_row,
     table_ref,
     vel_ref,
     stress_ref,
+    late_in,
     state,
     weights,
     sums,
-    forward,
-    by_source,
-    source,
-    sems,
+    late,
+    forcing,
 ):
-    events, rows, depth, steps, _ = sizes
+    events, rows, depth, steps, sources = sizes
     group = group_of(events)
-
-    def copies(i):
-        at = i * group * rows
-        own = pl.ds(at if isinstance(at, int) else pl.multiple_of(at, group * rows), group * rows)
-        return (
-            pltpu.make_async_copy(state_hbm.at[:, own], state.at[:, own], sems.at[0, i]),
-            pltpu.make_async_copy(forward_hbm.at[:, own], forward.at[:, own], sems.at[1, i]),
-        )
-
-    source_copy = pltpu.make_async_copy(source_hbm, source, sems.at[0, events // group])
-    source_copy.start()
-    for i in range(events // group):
-        for copy in copies(i):
-            copy.start()
-    layers = table_ref[...]
-    for row in range(rows):
-        by_source[pl.ds(row, layers.shape[0], stride=rows), :] = at_row(layers, row, depth)
+    each = table_ref.shape[0] // sources
+    kinds = [(step, part) for step in range(steps) for part in range(2)]
+    table = jnp.concatenate(
+        [
+            table_ref[pl.ds(step * (each // steps) + part, sources, stride=each), :]
+            for step, part in kinds
+        ],
+        axis=1,
+    )
+    pieces = exact_pieces(table)
+    records = lax.broadcasted_iota(jnp.int32, (sources, events), 0)
+    hit = (records == source_row[...]).astype(jnp.float32)
+    by_event = lax.dot_general(
+        jnp.concatenate([hit] * len(pieces), axis=0).astype(jnp.bfloat16),
+        jnp.concatenate(pieces, axis=0),
+        (((0,), (0,)), ((), ())),
+        preferred_element_type=jnp.float32,
+    )
+    for kind in range(len(kinds)):
+        layers = by_event[:, kind * depth : (kind + 1) * depth]
+        for row in range(rows):
+            at = pl.ds(kind * events * rows + row, events, stride=rows)
+            forcing[at, :] = at_row(layers, row, depth)
     vel = tuple(jnp.broadcast_to(c, (rows, depth)) for c in load_coeffs(vel_ref))
     stress = tuple(jnp.broadcast_to(c, (rows, depth)) for c in load_coeffs(stress_ref))
 
@@ -292,12 +324,10 @@
             return pl.ds(pl.multiple_of(at, count * rows), count * rows)
 
         def pushed(step, part, sub):
-            at = source[i * group + sub] * rows + step * 4 + part
-            return by_source[pl.ds(pl.multiple_of(at * rows, rows), rows), :]
-
-        for copy in copies(i):
-            copy.wait()
-        fields = [[state[f, tile(sub), :] for f in range(FIELDS)] for sub in range(group)]
+            at = ((step * 2 + part) * events + i * group + sub) * rows
+            return forcing[pl.ds(pl.multiple_of(at, rows), rows), :]
+
+        fields = [[state_in[f, tile(sub), :] for f in range(FIELDS)] for sub in range(group)]
         for step in range(steps):
             factors = [[] for _ in range(group)]
             for kind in range(3):
@@ -337,7 +367,6 @@
         return perm, poro
 
     zero = jnp.zeros((rows, depth), jnp.float32)
-    source_copy.wait()
     perm, poro = lax.fori_loop(0, events // group, body, (zero, zero))
     sums[pl.ds(0, rows), :] = perm
     sums[pl.ds(rows, rows), :] = poro
@@ -416,38 +445,90 @@
     return vel_last + end_inner + end_last, perm, poro
 
 
-def side_sums(sizes, over_chips, weights, sent, got, vel_ref, stress_ref, changes):
+def left_changes_soon(vel, stress, sent, own_late, got, factor):
+    gain_first = from_before(vel, *got[:3])
+    beyond = beyond_gain(stress, *plus(sent[:3], gain_first[:3]))
+    flow = got[3] + vel[1] * beyond[0] + vel[2] * beyond[3]
+    shear = got[4] + beyond[2]
+    stress_first = strains(stress, gain_first, NOTHING)
+    vel_first = plus(gain_first, velocity_gain(vel, *forces(vel, stress_first, gain_first[2:])))
+    vel_first = plus(vel_first, (0.0, -vel[0] * shear, flow, vel[1] * shear))
+    vel_second = from_before(vel, stress_first[0], stress_first[2], stress_first[3])
+    end_first = plus(stress_first, strains(stress, vel_first, vel_second))
+    end_second = strains(stress, vel_second, NOTHING)
+    perm = gain_first[2] * factor(0, 0, 0) + gain_first[3] * factor(0, 1, 0)
+    for row, vels in ((0, vel_first), (1, vel_second)):
+        perm = perm + vels[2] * factor(1, 0, row) + vels[3] * factor(1, 1, row)
+    poro = stress_first[3] * factor(0, 2, 0)
+    for row, stresses in ((0, end_first), (1, end_second)):
+        poro = poro + stresses[3] * factor(1, 2, row)
+    rest = (vel[0] * beyond[0] + vel[1] * beyond[3],)
+    return vel_first + vel_second + end_first + end_second + rest, perm, poro
+
+
+def right_changes_soon(vel, stress, sent, own_late, got, factor, last):
+    gain_after = from_before(vel, *sent[:3])
+    stress_last = beyond_gain(stress, *plus(got[:3], gain_after[:3]))
+    true_last = (own_late[0] + stress_last[0], sent[4] + stress_last[2], own_late[1] + stress_last[3])
+    vel_last = velocity_gain(
+        vel,
+        stress_last[0] + depth_lower(stress_last[2]),
+        stress_last[2] + depth_lower(stress_last[1]),
+        stress_last[3],
+        depth_lower(stress_last[3]),
+    )
+    stress_after = strains(stress, gain_after, NOTHING)
+    again = plus(
+        plus(gain_after, velocity_gain(vel, *forces(vel, stress_after, gain_after[2:]))),
+        from_before(vel, *true_last),
+    )
+    drain = got[3] + stress[2] * again[0] + stress[3] * again[2]
+    end_inner = beyond_gain(stress, *vel_last[:3])
+    end_last = plus(stress_last, strains(stress, vel_last, NOTHING))
+    perm = vel_last[2] * factor(1, 0, last) + vel_last[3] * factor(1, 1, last)
+    poro = stress_last[3] * factor(0, 2, last)
+    poro = poro + end_inner[3] * factor(1, 2, last - 1) + (end_last[3] - drain) * factor(1, 2, last)
+    poro = poro - stress[2] * (vel[0] * true_last[0] + vel[1] * true_last[2]) * got[4]
+    return vel_last + end_inner + end_last + again[:3], perm, poro
+
+
+def side_sums(sizes, over_chips, weights, sent, own_late, got, vel_ref, stress_ref, changes):
     events, rows, depth, _, _ = sizes
     vel = load_coeffs(vel_ref)
     stress = load_coeffs(stress_ref)
     last = rows - 1
     left, right = sides(over_chips)
+    count = SOON if over_chips else HALO
 
     def fill(changed, partial):
         for chunk in range(0, events, 8):
 
             def row_of(refs, i):
-                each = HALO // len(refs)
+                each = count // len(refs)
                 return refs[i // each][pl.ds(i % each * events + chunk, 8), :]
 
             def factor(step, kind, row):
                 return weights[step * 3 + kind, pl.ds(chunk * rows + row, 8, stride=rows), :]
 
-            own = tuple(row_of(sent, i) for i in range(HALO))
-            new = tuple(row_of(got, i) for i in range(HALO))
-            values, perm, poro = changed(vel, stress, own, new, factor)
+            own = tuple(row_of(sent, i) for i in range(count))
+            new = tuple(row_of(got, i) for i in range(count))
+            if over_chips:
+                late = tuple(own_late[pl.ds(i * events + chunk, 8), :] for i in range(LATE))
+                values, perm, poro = changed(vel, stress, own, late, new, factor)
+            else:
+                values, perm, poro = changed(vel, stress, own, new, factor)
             for i, value in enumerate(values):
                 changes[i, pl.ds(chunk, 8), :] = value
             partial = (partial[0] + perm, partial[1] + poro)
         return partial
 
     zero = (jnp.zeros((8, depth), jnp.float32),) * 2
+    from_left = left_changes_soon if over_chips else left_changes
+    from_right = functools.partial(right_changes_soon if over_chips else right_changes, last=last)
     return lax.cond(
         left,
-        lambda: fill(left_changes, zero),
-        lambda: lax.cond(
-            right, lambda: fill(functools.partial(right_changes, last=last), zero), lambda: zero
-        ),
+        lambda: fill(from_left, zero),
+        lambda: lax.cond(right, lambda: fill(from_right, zero), lambda: zero),
     )
 
 
@@ -466,35 +547,54 @@
 ):
     rows = sizes[1]
     sent, got = (sent_a, sent_b), (got_a, got_b)
-    perm, poro = side_sums(sizes, False, weights, sent, got, vel_ref, stress_ref, changes)
+    perm, poro = side_sums(sizes, False, weights, sent, None, got, vel_ref, stress_ref, changes)
     sums[pl.ds(0, rows), :] = sums_in[pl.ds(0, rows), :] + perm
     sums[pl.ds(rows, rows), :] = sums_in[pl.ds(rows, rows), :] + poro
 
 
 def chip_kernel(
-    sizes, normalizer, sums, weights, sent, got, vel_ref, stress_ref, changes, totals
+    sizes, normalizer, sums, weights, sent, late, got, vel_ref, stress_ref, changes, totals
 ):
     rows = sizes[1]
     vel = load_coeffs(vel_ref)
     stress = load_coeffs(stress_ref)
-    perm, poro = side_sums(sizes, True, weights, (sent,), (got,), vel_ref, stress_ref, changes)
+    perm, poro = side_sums(sizes, True, weights, (sent,), late, (got,), vel_ref, stress_ref, changes)
     perm = jnp.sum(sums[pl.ds(0, rows), :] + perm, axis=0, keepdims=True)
     poro = jnp.sum(sums[pl.ds(rows, rows), :] + poro, axis=0, keepdims=True)
     totals[pl.ds(0, 1), :] = perm * (vel[2] * vel[3] * normalizer)
     totals[pl.ds(1, 1), :] = poro * (stress[3] * normalizer)
 
 
-def finish_kernel(sizes, state_in, changes_core, changes_chip, state, out_hbm, done, sems):
+def finish_kernel(
+    sizes, state_in, changes_core, changes_chip, late, vel_ref, stress_ref, state, out_hbm, done, sems
+):
     events, rows, _, _, _ = sizes
+    vel = load_coeffs(vel_ref)
+    stress = load_coeffs(stress_ref)
     last = rows - 1
     left_places = [(s + f, row) for s in (0, 4) for row in (0, 1) for f in range(4)]
     right_places = [(f, last) for f in range(4)] + [(4 + f, row) for row in (last - 1, last) for f in range(4)]
-
-    def patch(changes, places, fields):
+    got = [late[pl.ds(i * events, events), :] for i in range(LATE)]
+
+    def left_late():
+        push = vel[0] * got[0] + vel[1] * got[1] + changes_chip[len(left_places)]
+        stresses = stress_gain(stress, push, 0.0, 0.0, depth_upper(-push))
+        return {(VX, 0): -push} | {(SXX + f, 0): stresses[f] for f in range(4)}
+
+    def right_late():
+        again = [got[i] + changes_chip[len(right_places) + i] for i in range(LATE)]
+        stresses = beyond_gain(stress, *again)
+        return {(SXX + f, last): stresses[f] for f in range(4)}
+
+    def patch(changes, places, fields, more):
+        added = more() if more else {}
         for i, (field, row) in enumerate(places):
             if field in fields:
                 at = pl.ds(row, events, stride=rows)
-                state[field, at, :] = state_in[field, at, :] + changes[i]
+                value = changes[i]
+                if (field, row) in added:
+                    value = value + added[field, row]
+                state[field, at, :] = state_in[field, at, :] + value
 
     half = FIELDS // 2
     copies = []
@@ -502,8 +602,12 @@
         fields = range(i * half, (i + 1) * half)
         for over_chips, changes in ((False, changes_core), (True, changes_chip)):
             left, right = sides(over_chips)
-            pl.when(left)(functools.partial(patch, changes, left_places, fields))
-            pl.when(right)(functools.partial(patch, changes, right_places, fields))
+            pl.when(left)(
+                functools.partial(patch, changes, left_places, fields, left_late if over_chips else None)
+            )
+            pl.when(right)(
+                functools.partial(patch, changes, right_places, fields, right_late if over_chips else None)
+            )
         own = pl.ds(i * half, half)
         copies.append(pltpu.make_async_copy(state.at[own], out_hbm.at[own], sems.at[i]))
         copies[i].start()
@@ -539,7 +643,6 @@
     sizes = (events, rows, depth, steps, sources)
     blocks = entries // 128
     tiles = events * rows
-    group = group_of(events)
     f32 = jnp.float32
     any_space = pl.BlockSpec(memory_space=pl.ANY)
     vmem = pl.BlockSpec(memory_space=pltpu.VMEM)
@@ -548,33 +651,48 @@
     cells = drm_cells.reshape(blocks, 128)
     force = drm_force.reshape(sources * steps, 2, blocks, 128).transpose(0, 2, 1, 3)
     force = force.reshape(sources * steps * 2 * blocks, 128)
-    message = pltpu.VMEM((HALO * events, depth), f32)
+    soon = pltpu.VMEM((SOON * events, depth), f32)
+    late = pltpu.VMEM((LATE * events, depth), f32)
     half = pltpu.VMEM((HALO // 2 * events, depth), f32)
     limits = pltpu.CompilerParams(vmem_limit_bytes=ROOM)
 
     def kept(space, *values):
         return tuple(pltpu.with_memory_space_constraint(v, space) for v in values)
 
-    table, message_first, message_second, message_chip, vel, stress = pl.pallas_call(
+    (
+        forward,
+        source_row,
+        table,
+        message_first,
+        message_second,
+        message_chip,
+        message_late,
+        vel,
+        stress,
+    ) = pl.pallas_call(
         functools.partial(edge_kernel, sizes),
         out_shape=(
+            pltpu.VMEM(forward.shape, forward.dtype),
+            pltpu.VMEM((1, events), jnp.int32),
             pltpu.VMEM(force.shape, f32),
             half,
             half,
-            message,
+            soon,
+            late,
             pltpu.VMEM(vel_coeffs.shape, f32),
             pltpu.VMEM(stress_coeffs.shape, f32),
         ),
-        in_specs=[any_space] * 6,
-        out_specs=(vmem,) * 6,
+        in_specs=[any_space] * 8,
+        out_specs=(vmem,) * 9,
         scratch_shapes=[
             pltpu.VMEM((fields * events, rows, depth), f32),
+            pltpu.VMEM((tiles, depth), f32),
             pltpu.VMEM(cells.shape, jnp.int32),
             pltpu.VMEM(force.shape, f32),
             pltpu.VMEM(force.shape, f32),
             pltpu.VMEM((tiles, depth), f32),
             pltpu.SMEM(source_id.shape, jnp.int32),
-            pltpu.SemaphoreType.DMA((7,)),
+            pltpu.SemaphoreType.DMA((10,)),
         ],
         compiler_params=limits,
         name="edges",
@@ -582,11 +700,13 @@
         *kept(
             pltpu.HBM,
             state.reshape(fields * events, rows, depth),
+            forward,
             vel_coeffs,
             stress_coeffs,
             cells,
             force,
             source_id,
+            source_id.reshape(1, events),
         )
     )
 
@@ -594,30 +714,28 @@
     got_second = swap_with(message_second, size, 1)
     got_chip = swap_over_chips(message_chip, groups, size)
 
-    state, weights, sums = pl.pallas_call(
+    state, weights, sums, message_late = pl.pallas_call(
         functools.partial(bulk_kernel, sizes),
         out_shape=(
             pltpu.VMEM(state.shape, f32),
             pltpu.VMEM(forward.shape, f32),
             pltpu.VMEM((2 * rows, depth), f32),
+            late,
         ),
-        in_specs=[any_space] * 3 + [vmem] * 3,
-        out_specs=(vmem,) * 3,
-        scratch_shapes=[
-            pltpu.VMEM(forward.shape, forward.dtype),
-            pltpu.VMEM((force.shape[0] * rows, depth), f32),
-            pltpu.SMEM(source_id.shape, jnp.int32),
-            pltpu.SemaphoreType.DMA((2, events // group + 1)),
-        ],
+        in_specs=[vmem] * 7,
+        out_specs=(vmem,) * 4,
+        input_output_aliases={6: 3},
+        scratch_shapes=[pltpu.VMEM((steps * 2 * tiles, depth), f32)],
         compiler_params=limits,
         cost_estimate=pl.CostEstimate(
             flops=steps * 80 * tiles * depth, bytes_accessed=8 * state.size, transcendentals=0
         ),
         name="bulk",
-    )(*kept(pltpu.HBM, state, forward, source_id), *kept(pltpu.VMEM, table, vel, stress))
+    )(state, *kept(pltpu.VMEM, forward, source_row, table, vel, stress, message_late))
+    got_late = swap_over_chips(message_late, groups, size)
 
     normalizer = (events * rows * size) ** (-0.5)
-    changed = pltpu.VMEM((16, events, depth), f32)
+    changed = pltpu.VMEM((17, events, depth), f32)
     changes_core, sums = pl.pallas_call(
         functools.partial(core_kernel, sizes),
         out_shape=(changed, pltpu.VMEM(sums.shape, f32)),
@@ -642,11 +760,11 @@
     changes_chip, totals = pl.pallas_call(
         functools.partial(chip_kernel, sizes, normalizer),
         out_shape=(changed, pltpu.VMEM((2, depth), f32)),
-        in_specs=[vmem] * 6,
+        in_specs=[vmem] * 7,
         out_specs=(vmem,) * 2,
         compiler_params=limits,
         name="join_chip",
-    )(*kept(pltpu.VMEM, sums, weights, message_chip, got_chip, vel, stress))
+    )(*kept(pltpu.VMEM, sums, weights, message_chip, message_late, got_chip, vel, stress))
 
     _, out, done = pl.pallas_call(
         functools.partial(finish_kernel, sizes),
@@ -655,14 +773,14 @@
             jax.ShapeDtypeStruct(state.shape, f32),
             pltpu.VMEM((2, depth), f32),
         ),
-        in_specs=[vmem] * 3,
+        in_specs=[vmem] * 6,
         out_specs=(vmem, any_space, vmem),
         input_output_aliases={0: 0},
         scratch_shapes=[pltpu.SemaphoreType.DMA((2,))],
         compiler_params=limits,
         cost_estimate=pl.CostEstimate(flops=0, bytes_accessed=2 * 4 * state.size, transcendentals=0),
         name="finish",
-    )(*kept(pltpu.VMEM, state, changes_core, changes_chip))
+    )(*kept(pltpu.VMEM, state, changes_core, changes_chip, got_late, vel, stress))
 
     mask = 1
     while mask < size:

time: 21.6 us -> 21.3 us (0.986)
  Pallas kernels: 5.64 us -> 5.21 us
  starting transfers between devices: 10.7 us -> 11 us
    ppermute x1 -> x2, starting transfers between devices: 3 us -> 4.2 us  [swap_over_chips(): return lax.ppermute(value, ('groups', 'gx'), route)]
    ppermute x6, starting transfers between devices: 7.68 us -> 6.78 us  [swap_with(): return lax.ppermute(value, 'gx', [(i, i ^ mask) for i in range(size)])]
    pallas_call x1, Pallas kernels: 2.58 us -> 1.97 us  [shards(): pl.pallas_call(functools.partial(bulk_kernel, sizes), out_shape=(pltpu.VM...]
  transfers between devices with their start and end apart: 7 -> 8, of which waited for: 4 -> 4; matrix products, arithmetic and copies ran while one was open for 0% -> 0% of each run, Pallas kernels for 19% -> 16%
where the time goes in v5:
time: 21.3 us; the launch traced here: 21.2 us
  starting transfers between devices  11 us (52%)
  Pallas kernels  5.21 us (24%)
  waiting for transfers between devices  3.7 us (17%)
  between operations  0.69 us (3%)
  other arithmetic  0.58 us (3%)
    ppermute x6, starting transfers between devices, swap_with(): return lax.ppermute(value, 'gx', [(i, i ^ mask) for i in range(size)])  6.78 us
    ppermute x2, starting transfers between devices, swap_over_chips(): return lax.ppermute(value, ('groups', 'gx'), route)  4.2 us
    ppermute x6, waiting for transfers between devices, swap_with(): return lax.ppermute(value, 'gx', [(i, i ^ mask) for i in range(size)])  3.7 us
    pallas_call x1, Pallas kernels, shards(): pl.pallas_call(functools.partial(bulk_kernel, sizes), out_shape=(pltpu.VM...  1.97 us
    pallas_call x1, Pallas kernels, shards(): pl.pallas_call(functools.partial(edge_kernel, sizes), out_shape=(pltpu.VM...  1.77 us
    pallas_call x1, Pallas kernels, shards(): pl.pallas_call(functools.partial(finish_kernel, sizes), out_shape=(pltpu....  1.22 us
    add x3, other arithmetic, shards(): totals = totals + swap_with(totals, size, mask | 1)  0.57 us
  transfers between devices with their start and end apart: 8, of which 4 were waited for; matrix products, arithmetic and copies ran while one was open for 0% of the time, Pallas kernels for 16%

profile of v5, /device:TPU:0, one launch (start us, length us, event | category | flops | bytes accessed | tf_op | source)
XLA Modules:
  0.0 21.2 jit_solution(5268551521087173089)
XLA Ops:
  0.6 0.0 copy-start
  0.6 1.8 %edges.1 = (bf16[6,384,128]{2,1,0:T(8,128)(2,1)S(1)}, s32[1,48]{1,0:T(1,128)S(1)}, f32[128,128]{1,0:T(8,128)S(1)}, f32[144,128]{1,0:T(8,128)S(1)}, f32[144,128]{...) custom-call(f32[384,8,128]{2,1,0:T(8,128)} %bitcast.11, ...), custom_call_target="tpu_custom_call" | custom-call | tf_op jit(solution)/shard_map/edges/pallas_call | solution.py:672
  2.4 3.0 %collective-permute-start.2 = (f32[240,128]{1,0:T(8,128)S(1)}, f32[240,128]{1,0:T(8,128)S(1)}, u32[]{:S(2)}, u32[]{:S(2)}) collective-permute-start(f32[240,128]{1,0:T(8,128)S(1)} %get-tuple-element.34.sent), channel_id=1, source_target_pairs={{1,2},{2,1},{3,4},{4,3},{5,6},{6,5},{7,8},{8,7},{9,10},{10,9},{11,... | collective-permute-start | bytes 368648 | tf_op jit(solution)/shard_map/ppermute | solution.py:631
  5.4 0.1 collective-permute-start
  5.6 0.4 %collective-permute-start.1 = (f32[144,128]{1,0:T(8,128)S(1)}, f32[144,128]{1,0:T(8,128)S(1)}, u32[]{:S(2)}, u32[]{:S(2)}) collective-permute-start(f32[144,128]{1,0:T(8,128)S(1)} %get-tuple-element.31.sent_b), channel_id=1, source_target_pairs={{0,1},{1,0},{2,3},{3,2},{4,5},{5,4},{6,7},{7,6},{8,9},{9,8},{10,11... | collective-permute-start | bytes 221192 | tf_op jit(solution)/shard_map/ppermute | solution.py:620
  5.9 0.0 copy-done
  5.9 2.0 %bulk.1 = (f32[8,384,128]{2,1,0:T(8,128)S(1)}, f32[6,384,128]{2,1,0:T(8,128)S(1)}, f32[16,128]{1,0:T(8,128)S(1)}, f32[144,128]{1,0:T(8,128)S(1)}) custom-call(f32[8,384,128]{2,1,0:T(8,128)S(1)} %bitcast.12, bf16[6,384,128]{2,1,0:T(8,128)(2,1)S(1)} %get-tuple-element.21.forward, ...), custom_call_target="tpu_custom_call", output_to_operand_aliasing={{3}: (6, {})} | custom-call | flops 7864320 | bytes 3145728 | tf_op jit(solution)/shard_map/bulk/pallas_call | solution.py:717
  7.9 1.2 %collective-permute-start.3 = (f32[144,128]{1,0:T(8,128)S(1)}, f32[144,128]{1,0:T(8,128)S(1)}, u32[]{:S(2)}, u32[]{:S(2)}) collective-permute-start(f32[144,128]{1,0:T(8,128)S(1)} %get-tuple-element.35.late), channel_id=1, source_target_pairs={{1,2},{2,1},{3,4},{4,3},{5,6},{6,5},{7,8},{8,7},{9,10},{10,9},{11,... | collective-permute-start | bytes 221192 | tf_op jit(solution)/shard_map/ppermute | solution.py:631
  9.1 0.0 collective-permute-done.got_a
  9.1 0.0 collective-permute-done.1.got_b
  9.1 0.2 %join_core.1 = (f32[17,48,128]{2,1,0:T(8,128)S(1)}, f32[16,128]{1,0:T(8,128)S(1)}) custom-call(f32[16,128]{1,0:T(8,128)S(1)} %get-tuple-element.28.sums_in, f32[6,384,128]{2,1,0:T(8,128)S(1)} %get-tuple-element.29.weights, f32[144,128]{1,0:T(8,128)S(1)} %get-tuple-element.30.sent_a, f32[144,128]{1,0:T(8,128)S(1)} %get-tuple-element.31.sent_b, ...), custom_call_target="tpu_custom_call" | custom-call | tf_op jit(solution)/shard_map/join_core/pallas_call | solution.py:739
  9.3 0.0 collective-permute-done.2.got
  9.4 0.5 %collective-permute-start.4 = (f32[2,128]{1,0:T(2,128)S(1)}, f32[2,128]{1,0:T(2,128)S(1)}, u32[]{:S(2)}, u32[]{:S(2)}) collective-permute-start(f32[2,128]{1,0:T(2,128)S(1)} %get-tuple-element.38), channel_id=1, source_target_pairs={{0,1},{1,0},{2,3},{3,2},{4,5},{5,4},{6,7},{7,6},{8,9},{9,8},{10,11... | collective-permute-start | bytes 3080 | tf_op jit(solution)/shard_map/ppermute | solution.py:620
  9.9 0.8 %collective-permute-done.4 = f32[2,128]{1,0:T(2,128)S(1)} collective-permute-done((f32[2,128]{1,0:T(2,128)S(1)}, f32[2,128]{1,0:T(2,128)S(1)}, u32[]{:S(2)}, u32[]{:S(2)}) %collective-permute-start.4) | collective-permute-done | bytes 1056 | tf_op jit(solution)/shard_map/ppermute | solution.py:620
  10.7 1.7 %collective-permute-start.5 = (f32[2,128]{1,0:T(2,128)S(1)}, f32[2,128]{1,0:T(2,128)S(1)}, u32[]{:S(2)}, u32[]{:S(2)}) collective-permute-start(f32[2,128]{1,0:T(2,128)S(1)} %add.15), channel_id=1, source_target_pairs={{0,3},{1,2},{2,1},{3,0},{4,7},{5,6},{6,5},{7,4},{8,11},{9,10},{10,... | collective-permute-start | bytes 3080 | tf_op jit(solution)/shard_map/ppermute | solution.py:620
  12.4 1.3 %collective-permute-done.5 = f32[2,128]{1,0:T(2,128)S(1)} collective-permute-done((f32[2,128]{1,0:T(2,128)S(1)}, f32[2,128]{1,0:T(2,128)S(1)}, u32[]{:S(2)}, u32[]{:S(2)}) %collective-permute-start.5) | collective-permute-done | bytes 1056 | tf_op jit(solution)/shard_map/ppermute | solution.py:620
  13.7 1.6 %collective-permute-start.6 = (f32[2,128]{1,0:T(2,128)S(1)}, f32[2,128]{1,0:T(2,128)S(1)}, u32[]{:S(2)}, u32[]{:S(2)}) collective-permute-start(f32[2,128]{1,0:T(2,128)S(1)} %add.16), channel_id=1, source_target_pairs={{0,5},{1,4},{2,7},{3,6},{4,1},{5,0},{6,3},{7,2},{8,13},{9,12},{10,... | collective-permute-start | bytes 3080 | tf_op jit(solution)/shard_map/ppermute | solution.py:620
  15.3 0.0 collective-permute-done.3.late
  15.3 1.2 %finish.1 = (f32[8,384,128]{2,1,0:T(8,128)S(1)}, f32[8,384,128]{2,1,0:T(8,128)}, f32[2,128]{1,0:T(2,128)S(1)}) custom-call(f32[8,384,128]{2,1,0:T(8,128)S(1)} %get-tuple-element.27.state_in, f32[17,48,128]{2,1,0:T(8,128)S(1)} %get-tuple-element.32.changes_core, f32[17,48,128]{2,1,0:T(8,128)S(1)} %get-tuple-element.36.changes_chip, ...), custom_call_target="tpu_custom_call", output_to_operand_aliasing={{0}: (0, {})} | custom-call | bytes 3145728 | tf_op jit(solution)/shard_map/finish/pallas_call | solution.py:769
  16.5 0.2 %collective-permute-done.6 = f32[2,128]{1,0:T(2,128)S(1)} collective-permute-done((f32[2,128]{1,0:T(2,128)S(1)}, f32[2,128]{1,0:T(2,128)S(1)}, u32[]{:S(2)}, u32[]{:S(2)}) %collective-permute-start.6) | collective-permute-done | bytes 1056 | tf_op jit(solution)/shard_map/ppermute | solution.py:620
  16.7 2.6 %collective-permute-start.7 = (f32[2,128]{1,0:T(2,128)S(1)}, f32[2,128]{1,0:T(2,128)S(1)}, u32[]{:S(2)}, u32[]{:S(2)}) collective-permute-start(f32[2,128]{1,0:T(2,128)S(1)} %add_add_fusion), channel_id=1, source_target_pairs={{0,9},{1,8},{2,11},{3,10},{4,13},{5,12},{6,15},{7,14},{8,1},{9,0},... | collective-permute-start | bytes 3080 | tf_op jit(solution)/shard_map/ppermute | solution.py:620
  19.3 1.3 %collective-permute-done.7 = f32[2,128]{1,0:T(2,128)S(1)} collective-permute-done((f32[2,128]{1,0:T(2,128)S(1)}, f32[2,128]{1,0:T(2,128)S(1)}, u32[]{:S(2)}, u32[]{:S(2)}) %collective-permute-start.7) | collective-permute-done | bytes 1056 | tf_op jit(solution)/shard_map/ppermute | solution.py:620
  20.6 0.6 %add.19 = f32[2,128]{1,0:T(2,128)} add(f32[2,128]{1,0:T(2,128)S(1)} %add_add_fusion, f32[2,128]{1,0:T(2,128)S(1)} %collective-permute-done.7) | non-fusion elementwise | flops 256 | bytes 3072 | tf_op jit(solution)/shard_map/add | solution.py:787
  (4 shorter events, 0.0 us)
Async XLA Ops:
  0.6 5.3 %copy-start = (f32[8,48,8,128]{3,2,1,0:T(8,128)S(1)}, f32[8,48,8,128]{3,2,1,0:T(8,128)}, u32[]{:S(2)}) copy-start(f32[8,48,8,128]{3,2,1,0:T(8,128)} %param.7) | copy-start | bytes 4718596
  2.4 6.9 %collective-permute-start.2 = (f32[240,128]{1,0:T(8,128)S(1)}, f32[240,128]{1,0:T(8,128)S(1)}, u32[]{:S(2)}, u32[]{:S(2)}) collective-permute-start(f32[240,128]{1,0:T(8,128)S(1)} %get-tuple-element.34.sent), channel_id=1, source_target_pairs={{1,2},{2,1},{3,4},{4,3},{5,6},{6,5},{7,8},{8,7},{9,10},{10,9},{11,... | collective-permute-start | bytes 368648 | tf_op jit(solution)/shard_map/ppermute | solution.py:631
  5.4 3.7 %collective-permute-start = (f32[144,128]{1,0:T(8,128)S(1)}, f32[144,128]{1,0:T(8,128)S(1)}, u32[]{:S(2)}, u32[]{:S(2)}) collective-permute-start(f32[144,128]{1,0:T(8,128)S(1)} %get-tuple-element.30.sent_a), channel_id=1, source_target_pairs={{0,1},{1,0},{2,3},{3,2},{4,5},{5,4},{6,7},{7,6},{8,9},{9,8},{10,11... | collective-permute-start | bytes 221192 | tf_op jit(solution)/shard_map/ppermute | solution.py:620
  5.6 3.5 %collective-permute-start.1 = (f32[144,128]{1,0:T(8,128)S(1)}, f32[144,128]{1,0:T(8,128)S(1)}, u32[]{:S(2)}, u32[]{:S(2)}) collective-permute-start(f32[144,128]{1,0:T(8,128)S(1)} %get-tuple-element.31.sent_b), channel_id=1, source_target_pairs={{0,1},{1,0},{2,3},{3,2},{4,5},{5,4},{6,7},{7,6},{8,9},{9,8},{10,11... | collective-permute-start | bytes 221192 | tf_op jit(solution)/shard_map/ppermute | solution.py:620
  7.9 7.3 %collective-permute-start.3 = (f32[144,128]{1,0:T(8,128)S(1)}, f32[144,128]{1,0:T(8,128)S(1)}, u32[]{:S(2)}, u32[]{:S(2)}) collective-permute-start(f32[144,128]{1,0:T(8,128)S(1)} %get-tuple-element.35.late), channel_id=1, source_target_pairs={{1,2},{2,1},{3,4},{4,3},{5,6},{6,5},{7,8},{8,7},{9,10},{10,9},{11,... | collective-permute-start | bytes 221192 | tf_op jit(solution)/shard_map/ppermute | solution.py:631
  9.4 1.3 %collective-permute-start.4 = (f32[2,128]{1,0:T(2,128)S(1)}, f32[2,128]{1,0:T(2,128)S(1)}, u32[]{:S(2)}, u32[]{:S(2)}) collective-permute-start(f32[2,128]{1,0:T(2,128)S(1)} %get-tuple-element.38), channel_id=1, source_target_pairs={{0,1},{1,0},{2,3},{3,2},{4,5},{5,4},{6,7},{7,6},{8,9},{9,8},{10,11... | collective-permute-start | bytes 3080 | tf_op jit(solution)/shard_map/ppermute | solution.py:620
  10.7 3.0 %collective-permute-start.5 = (f32[2,128]{1,0:T(2,128)S(1)}, f32[2,128]{1,0:T(2,128)S(1)}, u32[]{:S(2)}, u32[]{:S(2)}) collective-permute-start(f32[2,128]{1,0:T(2,128)S(1)} %add.15), channel_id=1, source_target_pairs={{0,3},{1,2},{2,1},{3,0},{4,7},{5,6},{6,5},{7,4},{8,11},{9,10},{10,... | collective-permute-start | bytes 3080 | tf_op jit(solution)/shard_map/ppermute | solution.py:620
  13.7 3.0 %collective-permute-start.6 = (f32[2,128]{1,0:T(2,128)S(1)}, f32[2,128]{1,0:T(2,128)S(1)}, u32[]{:S(2)}, u32[]{:S(2)}) collective-permute-start(f32[2,128]{1,0:T(2,128)S(1)} %add.16), channel_id=1, source_target_pairs={{0,5},{1,4},{2,7},{3,6},{4,1},{5,0},{6,3},{7,2},{8,13},{9,12},{10,... | collective-permute-start | bytes 3080 | tf_op jit(solution)/shard_map/ppermute | solution.py:620
  16.7 3.9 %collective-permute-start.7 = (f32[2,128]{1,0:T(2,128)S(1)}, f32[2,128]{1,0:T(2,128)S(1)}, u32[]{:S(2)}, u32[]{:S(2)}) collective-permute-start(f32[2,128]{1,0:T(2,128)S(1)} %add_add_fusion), channel_id=1, source_target_pairs={{0,9},{1,8},{2,11},{3,10},{4,13},{5,12},{6,15},{7,14},{8,1},{9,0},... | collective-permute-start | bytes 3080 | tf_op jit(solution)/shard_map/ppermute | solution.py:620

commit v6 on v5

--- a/solution.py
+++ b/solution.py
@@ -107,9 +107,8 @@
     cells_hbm,
     force_hbm,
     source_hbm,
-    row_hbm,
     forward,
-    source_row,
+    source,
     table_ref,
     message_first,
     message_second,
@@ -123,7 +122,6 @@
     force,
     near_force,
     pushes,
-    source,
     sems,
 ):
     events, rows, depth, steps, sources = sizes
@@ -140,7 +138,6 @@
                 (state_hbm.at[:, pl.ds(0, 2)], near.at[:, pl.ds(0, 2)]),
                 (state_hbm.at[:, pl.ds(rows - 2, 2)], near.at[:, pl.ds(rows - 2, 2)]),
                 (forward_hbm.at[pl.ds(final_kind, 1)], forward.at[pl.ds(final_kind, 1)]),
-                (row_hbm, source_row),
                 (forward_hbm.at[pl.ds(0, final_kind)], forward.at[pl.ds(0, final_kind)]),
             ]
         )
@@ -277,7 +274,7 @@
     sizes,
     state_in,
     forward,
-    source_row,
+    source,
     table_ref,
     vel_ref,
     stress_ref,
@@ -286,33 +283,17 @@
     weights,
     sums,
     late,
-    forcing,
+    by_source,
 ):
     events, rows, depth, steps, sources = sizes
     group = group_of(events)
     each = table_ref.shape[0] // sources
-    kinds = [(step, part) for step in range(steps) for part in range(2)]
-    table = jnp.concatenate(
-        [
-            table_ref[pl.ds(step * (each // steps) + part, sources, stride=each), :]
-            for step, part in kinds
-        ],
-        axis=1,
-    )
-    pieces = exact_pieces(table)
-    records = lax.broadcasted_iota(jnp.int32, (sources, events), 0)
-    hit = (records == source_row[...]).astype(jnp.float32)
-    by_event = lax.dot_general(
-        jnp.concatenate([hit] * len(pieces), axis=0).astype(jnp.bfloat16),
-        jnp.concatenate(pieces, axis=0),
-        (((0,), (0,)), ((), ())),
-        preferred_element_type=jnp.float32,
-    )
-    for kind in range(len(kinds)):
-        layers = by_event[:, kind * depth : (kind + 1) * depth]
-        for row in range(rows):
-            at = pl.ds(kind * events * rows + row, events, stride=rows)
-            forcing[at, :] = at_row(layers, row, depth)
+    for step in range(steps):
+        for part in range(2):
+            layers = table_ref[pl.ds(step * (each // steps) + part, sources, stride=each), :]
+            for row in range(rows):
+                at = (step * 2 + part) * sources * rows + row
+                by_source[pl.ds(at, sources, stride=rows), :] = at_row(layers, row, depth)
     vel = tuple(jnp.broadcast_to(c, (rows, depth)) for c in load_coeffs(vel_ref))
     stress = tuple(jnp.broadcast_to(c, (rows, depth)) for c in load_coeffs(stress_ref))
 
@@ -324,8 +305,8 @@
             return pl.ds(pl.multiple_of(at, count * rows), count * rows)
 
         def pushed(step, part, sub):
-            at = ((step * 2 + part) * events + i * group + sub) * rows
-            return forcing[pl.ds(pl.multiple_of(at, rows), rows), :]
+            at = ((step * 2 + part) * sources + source[i * group + sub]) * rows
+            return by_source[pl.ds(pl.multiple_of(at, rows), rows), :]
 
         fields = [[state_in[f, tile(sub), :] for f in range(FIELDS)] for sub in range(group)]
         for step in range(steps):
@@ -646,6 +627,7 @@
     f32 = jnp.float32
     any_space = pl.BlockSpec(memory_space=pl.ANY)
     vmem = pl.BlockSpec(memory_space=pltpu.VMEM)
+    smem = pl.BlockSpec(memory_space=pltpu.SMEM)
     state = adjoint_state.reshape(fields, tiles, depth)
     forward = forward_fields.reshape(steps * 3, tiles, depth)
     cells = drm_cells.reshape(blocks, 128)
@@ -661,7 +643,7 @@
 
     (
         forward,
-        source_row,
+        source,
         table,
         message_first,
         message_second,
@@ -673,7 +655,7 @@
         functools.partial(edge_kernel, sizes),
         out_shape=(
             pltpu.VMEM(forward.shape, forward.dtype),
-            pltpu.VMEM((1, events), jnp.int32),
+            pltpu.SMEM((events,), jnp.int32),
             pltpu.VMEM(force.shape, f32),
             half,
             half,
@@ -682,8 +664,8 @@
             pltpu.VMEM(vel_coeffs.shape, f32),
             pltpu.VMEM(stress_coeffs.shape, f32),
         ),
-        in_specs=[any_space] * 8,
-        out_specs=(vmem,) * 9,
+        in_specs=[any_space] * 7,
+        out_specs=(vmem, smem) + (vmem,) * 7,
         scratch_shapes=[
             pltpu.VMEM((fields * events, rows, depth), f32),
             pltpu.VMEM((tiles, depth), f32),
@@ -691,8 +673,7 @@
             pltpu.VMEM(force.shape, f32),
             pltpu.VMEM(force.shape, f32),
             pltpu.VMEM((tiles, depth), f32),
-            pltpu.SMEM(source_id.shape, jnp.int32),
-            pltpu.SemaphoreType.DMA((10,)),
+            pltpu.SemaphoreType.DMA((9,)),
         ],
         compiler_params=limits,
         name="edges",
@@ -706,7 +687,6 @@
             cells,
             force,
             source_id,
-            source_id.reshape(1, events),
         )
     )
 
@@ -722,16 +702,21 @@
             pltpu.VMEM((2 * rows, depth), f32),
             late,
         ),
-        in_specs=[vmem] * 7,
+        in_specs=[vmem] * 2 + [smem] + [vmem] * 4,
         out_specs=(vmem,) * 4,
         input_output_aliases={6: 3},
-        scratch_shapes=[pltpu.VMEM((steps * 2 * tiles, depth), f32)],
+        scratch_shapes=[pltpu.VMEM((steps * 2 * sources * rows, depth), f32)],
         compiler_params=limits,
         cost_estimate=pl.CostEstimate(
             flops=steps * 80 * tiles * depth, bytes_accessed=8 * state.size, transcendentals=0
         ),
         name="bulk",
-    )(state, *kept(pltpu.VMEM, forward, source_row, table, vel, stress, message_late))
+    )(
+        state,
+        *kept(pltpu.VMEM, forward),
+        *kept(pltpu.SMEM, source),
+        *kept(pltpu.VMEM, table, vel, stress, message_late),
+    )
     got_late = swap_over_chips(message_late, groups, size)
 
     normalizer = (events * rows * size) ** (-0.5)

time: 21.3 us -> 21.3 us (level)
  Pallas kernels: 5.21 us -> 4.89 us
    pallas_call x1, Pallas kernels: 1.97 us -> 1.65 us  [shards(): pl.pallas_call(functools.partial(bulk_kernel, sizes), out_shape=(pltpu.VM...]
  transfers between devices with their start and end apart: 8 -> 8, of which waited for: 4 -> 4; matrix products, arithmetic and copies ran while one was open for 0% -> 0% of each run, Pallas kernels for 16% -> 15%
where the time goes in v6:
time: 21.3 us; the launch traced here: 21.1 us
  starting transfers between devices  11.1 us (52%)
  Pallas kernels  4.89 us (23%)
  waiting for transfers between devices  3.87 us (18%)
  between operations  0.69 us (3%)
  other arithmetic  0.58 us (3%)
    ppermute x6, starting transfers between devices, swap_with(): return lax.ppermute(value, 'gx', [(i, i ^ mask) for i in range(size)])  6.92 us
    ppermute x2, starting transfers between devices, swap_over_chips(): return lax.ppermute(value, ('groups', 'gx'), route)  4.18 us
    ppermute x6, waiting for transfers between devices, swap_with(): return lax.ppermute(value, 'gx', [(i, i ^ mask) for i in range(size)])  3.87 us
    pallas_call x1, Pallas kernels, shards(): pl.pallas_call(functools.partial(edge_kernel, sizes), out_shape=(pltpu.VM...  1.77 us
    pallas_call x1, Pallas kernels, shards(): pl.pallas_call(functools.partial(bulk_kernel, sizes), out_shape=(pltpu.VM...  1.65 us
    pallas_call x1, Pallas kernels, shards(): pl.pallas_call(functools.partial(finish_kernel, sizes), out_shape=(pltpu....  1.22 us
    add x3, other arithmetic, shards(): totals = totals + swap_with(totals, size, mask | 1)  0.57 us
  transfers between devices with their start and end apart: 8, of which 4 were waited for; matrix products, arithmetic and copies ran while one was open for 0% of the time, Pallas kernels for 15%

profile of v6, /device:TPU:0, one launch (start us, length us, event | category | flops | bytes accessed | tf_op | source)
XLA Modules:
  0.0 21.1 jit_solution(10207676597131221043)
XLA Ops:
  0.6 0.0 copy-start
  0.6 1.8 %edges.1 = (bf16[6,384,128]{2,1,0:T(8,128)(2,1)S(1)}, s32[48]{0:T(128)S(4)}, f32[128,128]{1,0:T(8,128)S(1)}, f32[144,128]{1,0:T(8,128)S(1)}, f32[144,128]{1,0:T(...) custom-call(f32[384,8,128]{2,1,0:T(8,128)} %bitcast.10, ...), custom_call_target="tpu_custom_call" | custom-call | tf_op jit(solution)/shard_map/edges/pallas_call | solution.py:654
  2.4 3.0 %collective-permute-start.2 = (f32[240,128]{1,0:T(8,128)S(1)}, f32[240,128]{1,0:T(8,128)S(1)}, u32[]{:S(2)}, u32[]{:S(2)}) collective-permute-start(f32[240,128]{1,0:T(8,128)S(1)} %get-tuple-element.34.sent), channel_id=1, source_target_pairs={{1,2},{2,1},{3,4},{4,3},{5,6},{6,5},{7,8},{8,7},{9,10},{10,9},{11,... | collective-permute-start | bytes 368648 | tf_op jit(solution)/shard_map/ppermute | solution.py:612
  5.4 0.1 collective-permute-start
  5.6 0.4 %collective-permute-start.1 = (f32[144,128]{1,0:T(8,128)S(1)}, f32[144,128]{1,0:T(8,128)S(1)}, u32[]{:S(2)}, u32[]{:S(2)}) collective-permute-start(f32[144,128]{1,0:T(8,128)S(1)} %get-tuple-element.31.sent_b), channel_id=1, source_target_pairs={{0,1},{1,0},{2,3},{3,2},{4,5},{5,4},{6,7},{7,6},{8,9},{9,8},{10,11... | collective-permute-start | bytes 221192 | tf_op jit(solution)/shard_map/ppermute | solution.py:601
  5.9 0.0 copy-done
  5.9 1.6 %bulk.1 = (f32[8,384,128]{2,1,0:T(8,128)S(1)}, f32[6,384,128]{2,1,0:T(8,128)S(1)}, f32[16,128]{1,0:T(8,128)S(1)}, f32[144,128]{1,0:T(8,128)S(1)}) custom-call(f32[8,384,128]{2,1,0:T(8,128)S(1)} %bitcast.11, bf16[6,384,128]{2,1,0:T(8,128)(2,1)S(1)} %get-tuple-element.21.forward, s32[48]{0:T(128)S(4)} %get-tuple-element.22.source, ...), custom_call_target="tpu_custom_call", output_to_operand_aliasing={{3}: (6, {})} | custom-call | flops 7864320 | bytes 3145728 | tf_op jit(solution)/shard_map/bulk/pallas_call | solution.py:697
  7.6 1.2 %collective-permute-start.3 = (f32[144,128]{1,0:T(8,128)S(1)}, f32[144,128]{1,0:T(8,128)S(1)}, u32[]{:S(2)}, u32[]{:S(2)}) collective-permute-start(f32[144,128]{1,0:T(8,128)S(1)} %get-tuple-element.35.late), channel_id=1, source_target_pairs={{1,2},{2,1},{3,4},{4,3},{5,6},{6,5},{7,8},{8,7},{9,10},{10,9},{11,... | collective-permute-start | bytes 221192 | tf_op jit(solution)/shard_map/ppermute | solution.py:612
  8.8 0.0 collective-permute-done.got_a
  8.8 0.0 collective-permute-done.1.got_b
  8.8 0.2 %join_core.1 = (f32[17,48,128]{2,1,0:T(8,128)S(1)}, f32[16,128]{1,0:T(8,128)S(1)}) custom-call(f32[16,128]{1,0:T(8,128)S(1)} %get-tuple-element.28.sums_in, f32[6,384,128]{2,1,0:T(8,128)S(1)} %get-tuple-element.29.weights, f32[144,128]{1,0:T(8,128)S(1)} %get-tuple-element.30.sent_a, f32[144,128]{1,0:T(8,128)S(1)} %get-tuple-element.31.sent_b, ...), custom_call_target="tpu_custom_call" | custom-call | tf_op jit(solution)/shard_map/join_core/pallas_call | solution.py:724
  9.0 0.0 collective-permute-done.2.got
  9.1 0.5 %collective-permute-start.4 = (f32[2,128]{1,0:T(2,128)S(1)}, f32[2,128]{1,0:T(2,128)S(1)}, u32[]{:S(2)}, u32[]{:S(2)}) collective-permute-start(f32[2,128]{1,0:T(2,128)S(1)} %get-tuple-element.38), channel_id=1, source_target_pairs={{0,1},{1,0},{2,3},{3,2},{4,5},{5,4},{6,7},{7,6},{8,9},{9,8},{10,11... | collective-permute-start | bytes 3080 | tf_op jit(solution)/shard_map/ppermute | solution.py:601
  9.6 0.8 %collective-permute-done.4 = f32[2,128]{1,0:T(2,128)S(1)} collective-permute-done((f32[2,128]{1,0:T(2,128)S(1)}, f32[2,128]{1,0:T(2,128)S(1)}, u32[]{:S(2)}, u32[]{:S(2)}) %collective-permute-start.4) | collective-permute-done | bytes 1056 | tf_op jit(solution)/shard_map/ppermute | solution.py:601
  10.4 2.0 %collective-permute-start.5 = (f32[2,128]{1,0:T(2,128)S(1)}, f32[2,128]{1,0:T(2,128)S(1)}, u32[]{:S(2)}, u32[]{:S(2)}) collective-permute-start(f32[2,128]{1,0:T(2,128)S(1)} %add.15), channel_id=1, source_target_pairs={{0,3},{1,2},{2,1},{3,0},{4,7},{5,6},{6,5},{7,4},{8,11},{9,10},{10,... | collective-permute-start | bytes 3080 | tf_op jit(solution)/shard_map/ppermute | solution.py:601
  12.4 1.3 %collective-permute-done.5 = f32[2,128]{1,0:T(2,128)S(1)} collective-permute-done((f32[2,128]{1,0:T(2,128)S(1)}, f32[2,128]{1,0:T(2,128)S(1)}, u32[]{:S(2)}, u32[]{:S(2)}) %collective-permute-start.5) | collective-permute-done | bytes 1056 | tf_op jit(solution)/shard_map/ppermute | solution.py:601
  13.7 1.5 %collective-permute-start.6 = (f32[2,128]{1,0:T(2,128)S(1)}, f32[2,128]{1,0:T(2,128)S(1)}, u32[]{:S(2)}, u32[]{:S(2)}) collective-permute-start(f32[2,128]{1,0:T(2,128)S(1)} %add.16), channel_id=1, source_target_pairs={{0,5},{1,4},{2,7},{3,6},{4,1},{5,0},{6,3},{7,2},{8,13},{9,12},{10,... | collective-permute-start | bytes 3080 | tf_op jit(solution)/shard_map/ppermute | solution.py:601
  15.1 0.0 collective-permute-done.3.late
  15.1 1.2 %finish.1 = (f32[8,384,128]{2,1,0:T(8,128)S(1)}, f32[8,384,128]{2,1,0:T(8,128)}, f32[2,128]{1,0:T(2,128)S(1)}) custom-call(f32[8,384,128]{2,1,0:T(8,128)S(1)} %get-tuple-element.27.state_in, f32[17,48,128]{2,1,0:T(8,128)S(1)} %get-tuple-element.32.changes_core, f32[17,48,128]{2,1,0:T(8,128)S(1)} %get-tuple-element.36.changes_chip, ...), custom_call_target="tpu_custom_call", output_to_operand_aliasing={{0}: (0, {})} | custom-call | bytes 3145728 | tf_op jit(solution)/shard_map/finish/pallas_call | solution.py:754
  16.4 0.3 %collective-permute-done.6 = f32[2,128]{1,0:T(2,128)S(1)} collective-permute-done((f32[2,128]{1,0:T(2,128)S(1)}, f32[2,128]{1,0:T(2,128)S(1)}, u32[]{:S(2)}, u32[]{:S(2)}) %collective-permute-start.6) | collective-permute-done | bytes 1056 | tf_op jit(solution)/shard_map/ppermute | solution.py:601
  16.7 2.5 %collective-permute-start.7 = (f32[2,128]{1,0:T(2,128)S(1)}, f32[2,128]{1,0:T(2,128)S(1)}, u32[]{:S(2)}, u32[]{:S(2)}) collective-permute-start(f32[2,128]{1,0:T(2,128)S(1)} %add_add_fusion), channel_id=1, source_target_pairs={{0,9},{1,8},{2,11},{3,10},{4,13},{5,12},{6,15},{7,14},{8,1},{9,0},... | collective-permute-start | bytes 3080 | tf_op jit(solution)/shard_map/ppermute | solution.py:601
  19.1 1.4 %collective-permute-done.7 = f32[2,128]{1,0:T(2,128)S(1)} collective-permute-done((f32[2,128]{1,0:T(2,128)S(1)}, f32[2,128]{1,0:T(2,128)S(1)}, u32[]{:S(2)}, u32[]{:S(2)}) %collective-permute-start.7) | collective-permute-done | bytes 1056 | tf_op jit(solution)/shard_map/ppermute | solution.py:601
  20.6 0.6 %add.19 = f32[2,128]{1,0:T(2,128)} add(f32[2,128]{1,0:T(2,128)S(1)} %add_add_fusion, f32[2,128]{1,0:T(2,128)S(1)} %collective-permute-done.7) | non-fusion elementwise | flops 256 | bytes 3072 | tf_op jit(solution)/shard_map/add | solution.py:772
  (4 shorter events, 0.0 us)
Async XLA Ops:
  0.6 5.3 %copy-start = (f32[8,48,8,128]{3,2,1,0:T(8,128)S(1)}, f32[8,48,8,128]{3,2,1,0:T(8,128)}, u32[]{:S(2)}) copy-start(f32[8,48,8,128]{3,2,1,0:T(8,128)} %param.7) | copy-start | bytes 4718596
  2.4 6.6 %collective-permute-start.2 = (f32[240,128]{1,0:T(8,128)S(1)}, f32[240,128]{1,0:T(8,128)S(1)}, u32[]{:S(2)}, u32[]{:S(2)}) collective-permute-start(f32[240,128]{1,0:T(8,128)S(1)} %get-tuple-element.34.sent), channel_id=1, source_target_pairs={{1,2},{2,1},{3,4},{4,3},{5,6},{6,5},{7,8},{8,7},{9,10},{10,9},{11,... | collective-permute-start | bytes 368648 | tf_op jit(solution)/shard_map/ppermute | solution.py:612
  5.4 3.4 %collective-permute-start = (f32[144,128]{1,0:T(8,128)S(1)}, f32[144,128]{1,0:T(8,128)S(1)}, u32[]{:S(2)}, u32[]{:S(2)}) collective-permute-start(f32[144,128]{1,0:T(8,128)S(1)} %get-tuple-element.30.sent_a), channel_id=1, source_target_pairs={{0,1},{1,0},{2,3},{3,2},{4,5},{5,4},{6,7},{7,6},{8,9},{9,8},{10,11... | collective-permute-start | bytes 221192 | tf_op jit(solution)/shard_map/ppermute | solution.py:601
  5.6 3.2 %collective-permute-start.1 = (f32[144,128]{1,0:T(8,128)S(1)}, f32[144,128]{1,0:T(8,128)S(1)}, u32[]{:S(2)}, u32[]{:S(2)}) collective-permute-start(f32[144,128]{1,0:T(8,128)S(1)} %get-tuple-element.31.sent_b), channel_id=1, source_target_pairs={{0,1},{1,0},{2,3},{3,2},{4,5},{5,4},{6,7},{7,6},{8,9},{9,8},{10,11... | collective-permute-start | bytes 221192 | tf_op jit(solution)/shard_map/ppermute | solution.py:601
  7.6 7.5 %collective-permute-start.3 = (f32[144,128]{1,0:T(8,128)S(1)}, f32[144,128]{1,0:T(8,128)S(1)}, u32[]{:S(2)}, u32[]{:S(2)}) collective-permute-start(f32[144,128]{1,0:T(8,128)S(1)} %get-tuple-element.35.late), channel_id=1, source_target_pairs={{1,2},{2,1},{3,4},{4,3},{5,6},{6,5},{7,8},{8,7},{9,10},{10,9},{11,... | collective-permute-start | bytes 221192 | tf_op jit(solution)/shard_map/ppermute | solution.py:612
  9.1 1.3 %collective-permute-start.4 = (f32[2,128]{1,0:T(2,128)S(1)}, f32[2,128]{1,0:T(2,128)S(1)}, u32[]{:S(2)}, u32[]{:S(2)}) collective-permute-start(f32[2,128]{1,0:T(2,128)S(1)} %get-tuple-element.38), channel_id=1, source_target_pairs={{0,1},{1,0},{2,3},{3,2},{4,5},{5,4},{6,7},{7,6},{8,9},{9,8},{10,11... | collective-permute-start | bytes 3080 | tf_op jit(solution)/shard_map/ppermute | solution.py:601
  10.4 3.3 %collective-permute-start.5 = (f32[2,128]{1,0:T(2,128)S(1)}, f32[2,128]{1,0:T(2,128)S(1)}, u32[]{:S(2)}, u32[]{:S(2)}) collective-permute-start(f32[2,128]{1,0:T(2,128)S(1)} %add.15), channel_id=1, source_target_pairs={{0,3},{1,2},{2,1},{3,0},{4,7},{5,6},{6,5},{7,4},{8,11},{9,10},{10,... | collective-permute-start | bytes 3080 | tf_op jit(solution)/shard_map/ppermute | solution.py:601
  13.7 3.0 %collective-permute-start.6 = (f32[2,128]{1,0:T(2,128)S(1)}, f32[2,128]{1,0:T(2,128)S(1)}, u32[]{:S(2)}, u32[]{:S(2)}) collective-permute-start(f32[2,128]{1,0:T(2,128)S(1)} %add.16), channel_id=1, source_target_pairs={{0,5},{1,4},{2,7},{3,6},{4,1},{5,0},{6,3},{7,2},{8,13},{9,12},{10,... | collective-permute-start | bytes 3080 | tf_op jit(solution)/shard_map/ppermute | solution.py:601
  16.7 3.9 %collective-permute-start.7 = (f32[2,128]{1,0:T(2,128)S(1)}, f32[2,128]{1,0:T(2,128)S(1)}, u32[]{:S(2)}, u32[]{:S(2)}) collective-permute-start(f32[2,128]{1,0:T(2,128)S(1)} %add_add_fusion), channel_id=1, source_target_pairs={{0,9},{1,8},{2,11},{3,10},{4,13},{5,12},{6,15},{7,14},{8,1},{9,0},... | collective-permute-start | bytes 3080 | tf_op jit(solution)/shard_map/ppermute | solution.py:601

commit v7 on v6

--- a/solution.py
+++ b/solution.py
@@ -107,6 +107,7 @@
     cells_hbm,
     force_hbm,
     source_hbm,
+    near,
     forward,
     source,
     table_ref,
@@ -116,7 +117,6 @@
     message_late,
     vel_ref,
     stress_ref,
-    near,
     weights,
     cells,
     force,
@@ -138,6 +138,7 @@
                 (state_hbm.at[:, pl.ds(0, 2)], near.at[:, pl.ds(0, 2)]),
                 (state_hbm.at[:, pl.ds(rows - 2, 2)], near.at[:, pl.ds(rows - 2, 2)]),
                 (forward_hbm.at[pl.ds(final_kind, 1)], forward.at[pl.ds(final_kind, 1)]),
+                (state_hbm.at[:, pl.ds(2, rows - 4)], near.at[:, pl.ds(2, rows - 4)]),
                 (forward_hbm.at[pl.ds(0, final_kind)], forward.at[pl.ds(0, final_kind)]),
             ]
         )
@@ -178,7 +179,7 @@
     for event in range(events):
         record = pl.multiple_of(source[event] * rows, rows)
         pushes[pl.ds(event * rows, rows), :] = near_force[pl.ds(record, rows), :]
-    for copy in copies[3:-1]:
+    for copy in copies[3:-2]:
         copy.wait()
     weights[...] = forward[final_kind].astype(jnp.float32)
     vel = load_coeffs(vel_ref)
@@ -263,7 +264,8 @@
             message_chip[pl.ds(i * events + chunk, 8), :] = jnp.where(odd, right_soon[i], left_soon[i])
         for i in range(LATE):
             message_late[pl.ds(i * events + chunk, 8), :] = jnp.where(odd, right_late[i], left[3 + i])
-    copies[-1].wait()
+    for copy in copies[-2:]:
+        copy.wait()
 
 
 def group_of(events):
@@ -272,14 +274,14 @@
 
 def bulk_kernel(
     sizes,
-    state_in,
+    given,
     forward,
     source,
     table_ref,
     vel_ref,
     stress_ref,
     late_in,
-    state,
+    changed,
     weights,
     sums,
     late,
@@ -287,6 +289,8 @@
 ):
     events, rows, depth, steps, sources = sizes
     group = group_of(events)
+    state_in = given.reshape(FIELDS, events * rows, depth)
+    state = changed.reshape(FIELDS, events * rows, depth)
     each = table_ref.shape[0] // sources
     for step in range(steps):
         for part in range(2):
@@ -547,9 +551,11 @@
 
 
 def finish_kernel(
-    sizes, state_in, changes_core, changes_chip, late, vel_ref, stress_ref, state, out_hbm, done, sems
+    sizes, given, changes_core, changes_chip, late, vel_ref, stress_ref, changed, out_hbm, done, sems
 ):
-    events, rows, _, _, _ = sizes
+    events, rows, depth, _, _ = sizes
+    state_in = given.reshape(FIELDS, events * rows, depth)
+    state = changed.reshape(FIELDS, events * rows, depth)
     vel = load_coeffs(vel_ref)
     stress = load_coeffs(stress_ref)
     last = rows - 1
@@ -589,8 +595,8 @@
             pl.when(right)(
                 functools.partial(patch, changes, right_places, fields, right_late if over_chips else None)
             )
-        own = pl.ds(i * half, half)
-        copies.append(pltpu.make_async_copy(state.at[own], out_hbm.at[own], sems.at[i]))
+        own = pl.ds(i * half * events, half * events)
+        copies.append(pltpu.make_async_copy(changed.at[own], out_hbm.at[own], sems.at[i]))
         copies[i].start()
     done[...] = jnp.zeros_like(done)
     for copy in copies:
@@ -628,7 +634,7 @@
     any_space = pl.BlockSpec(memory_space=pl.ANY)
     vmem = pl.BlockSpec(memory_space=pltpu.VMEM)
     smem = pl.BlockSpec(memory_space=pltpu.SMEM)
-    state = adjoint_state.reshape(fields, tiles, depth)
+    state = adjoint_state.reshape(fields * events, rows, depth)
     forward = forward_fields.reshape(steps * 3, tiles, depth)
     cells = drm_cells.reshape(blocks, 128)
     force = drm_force.reshape(sources * steps, 2, blocks, 128).transpose(0, 2, 1, 3)
@@ -642,6 +648,7 @@
         return tuple(pltpu.with_memory_space_constraint(v, space) for v in values)
 
     (
+        state,
         forward,
         source,
         table,
@@ -654,6 +661,7 @@
     ) = pl.pallas_call(
         functools.partial(edge_kernel, sizes),
         out_shape=(
+            pltpu.VMEM(state.shape, f32),
             pltpu.VMEM(forward.shape, forward.dtype),
             pltpu.SMEM((events,), jnp.int32),
             pltpu.VMEM(force.shape, f32),
@@ -665,22 +673,21 @@
             pltpu.VMEM(stress_coeffs.shape, f32),
         ),
         in_specs=[any_space] * 7,
-        out_specs=(vmem, smem) + (vmem,) * 7,
+        out_specs=(vmem, vmem, smem) + (vmem,) * 7,
         scratch_shapes=[
-            pltpu.VMEM((fields * events, rows, depth), f32),
             pltpu.VMEM((tiles, depth), f32),
             pltpu.VMEM(cells.shape, jnp.int32),
             pltpu.VMEM(force.shape, f32),
             pltpu.VMEM(force.shape, f32),
             pltpu.VMEM((tiles, depth), f32),
-            pltpu.SemaphoreType.DMA((9,)),
+            pltpu.SemaphoreType.DMA((10,)),
         ],
         compiler_params=limits,
         name="edges",
     )(
         *kept(
             pltpu.HBM,
-            state.reshape(fields * events, rows, depth),
+            state,
             forward,
             vel_coeffs,
             stress_coeffs,
@@ -704,7 +711,7 @@
         ),
         in_specs=[vmem] * 2 + [smem] + [vmem] * 4,
         out_specs=(vmem,) * 4,
-        input_output_aliases={6: 3},
+        input_output_aliases={0: 0, 6: 3},
         scratch_shapes=[pltpu.VMEM((steps * 2 * sources * rows, depth), f32)],
         compiler_params=limits,
         cost_estimate=pl.CostEstimate(
@@ -712,8 +719,7 @@
         ),
         name="bulk",
     )(
-        state,
-        *kept(pltpu.VMEM, forward),
+        *kept(pltpu.VMEM, state, forward),
         *kept(pltpu.SMEM, source),
         *kept(pltpu.VMEM, table, vel, stress, message_late),
     )

time: 21.3 us -> 21.2 us (level)
  no operation moved by 1% of the time
where the time goes in v7:
time: 21.2 us; the launch traced here: 21.1 us
  starting transfers between devices  11.1 us (52%)
  Pallas kernels  4.82 us (23%)
  waiting for transfers between devices  3.87 us (18%)
  between operations  0.68 us (3%)
  other arithmetic  0.58 us (3%)
    ppermute x6, starting transfers between devices, swap_with(): return lax.ppermute(value, 'gx', [(i, i ^ mask) for i in range(size)])  6.92 us
    ppermute x2, starting transfers between devices, swap_over_chips(): return lax.ppermute(value, ('groups', 'gx'), route)  4.2 us
    ppermute x6, waiting for transfers between devices, swap_with(): return lax.ppermute(value, 'gx', [(i, i ^ mask) for i in range(size)])  3.86 us
    pallas_call x1, Pallas kernels, shards(): pl.pallas_call(functools.partial(edge_kernel, sizes), out_shape=(pltpu.VM...  1.71 us
    pallas_call x1, Pallas kernels, shards(): pl.pallas_call(functools.partial(bulk_kernel, sizes), out_shape=(pltpu.VM...  1.64 us
    pallas_call x1, Pallas kernels, shards(): pl.pallas_call(functools.partial(finish_kernel, sizes), out_shape=(pltpu....  1.22 us
    add x3, other arithmetic, shards(): totals = totals + swap_with(totals, size, mask | 1)  0.57 us
  transfers between devices with their start and end apart: 8, of which 4 were waited for; matrix products, arithmetic and copies ran while one was open for 0% of the time, Pallas kernels for 15%

profile of v7, /device:TPU:0, one launch (start us, length us, event | category | flops | bytes accessed | tf_op | source)
XLA Modules:
  0.0 21.1 jit_solution(9499681046634424283)
XLA Ops:
  0.6 1.7 %edges.1 = (f32[384,8,128]{2,1,0:T(8,128)S(1)}, bf16[6,384,128]{2,1,0:T(8,128)(2,1)S(1)}, s32[48]{0:T(128)S(4)}, f32[128,128]{1,0:T(8,128)S(1)}, f32[144,128]{1,...) custom-call(f32[384,8,128]{2,1,0:T(8,128)} %bitcast.9, ...), custom_call_target="tpu_custom_call" | custom-call | tf_op jit(solution)/shard_map/edges/pallas_call | solution.py:661
  2.4 3.0 %collective-permute-start.2 = (f32[240,128]{1,0:T(8,128)S(1)}, f32[240,128]{1,0:T(8,128)S(1)}, u32[]{:S(2)}, u32[]{:S(2)}) collective-permute-start(f32[240,128]{1,0:T(8,128)S(1)} %get-tuple-element.36.sent), channel_id=1, source_target_pairs={{1,2},{2,1},{3,4},{4,3},{5,6},{6,5},{7,8},{8,7},{9,10},{10,9},{11,... | collective-permute-start | bytes 368648 | tf_op jit(solution)/shard_map/ppermute | solution.py:618
  5.4 0.1 collective-permute-start
  5.5 0.4 %collective-permute-start.1 = (f32[144,128]{1,0:T(8,128)S(1)}, f32[144,128]{1,0:T(8,128)S(1)}, u32[]{:S(2)}, u32[]{:S(2)}) collective-permute-start(f32[144,128]{1,0:T(8,128)S(1)} %get-tuple-element.33.sent_b), channel_id=1, source_target_pairs={{0,1},{1,0},{2,3},{3,2},{4,5},{5,4},{6,7},{7,6},{8,9},{9,8},{10,11... | collective-permute-start | bytes 221192 | tf_op jit(solution)/shard_map/ppermute | solution.py:607
  5.9 1.6 %bulk.1 = (f32[384,8,128]{2,1,0:T(8,128)S(1)}, f32[6,384,128]{2,1,0:T(8,128)S(1)}, f32[16,128]{1,0:T(8,128)S(1)}, f32[144,128]{1,0:T(8,128)S(1)}) custom-call(f32[384,8,128]{2,1,0:T(8,128)S(1)} %get-tuple-element.22.given, bf16[6,384,128]{2,1,0:T(8,128)(2,1)S(1)} %get-tuple-element.23.forward, ...), custom_call_target="tpu_custom_call", output_to_operand_aliasing={{0}: (0, {}), {3}: (6, {})} | custom-call | flops 7864320 | bytes 3145728 | tf_op jit(solution)/shard_map/bulk/pallas_call | solution.py:704
  7.5 1.2 %collective-permute-start.3 = (f32[144,128]{1,0:T(8,128)S(1)}, f32[144,128]{1,0:T(8,128)S(1)}, u32[]{:S(2)}, u32[]{:S(2)}) collective-permute-start(f32[144,128]{1,0:T(8,128)S(1)} %get-tuple-element.37.late), channel_id=1, source_target_pairs={{1,2},{2,1},{3,4},{4,3},{5,6},{6,5},{7,8},{8,7},{9,10},{10,9},{11,... | collective-permute-start | bytes 221192 | tf_op jit(solution)/shard_map/ppermute | solution.py:618
  8.7 0.0 collective-permute-done.got_a
  8.7 0.0 collective-permute-done.1.got_b
  8.7 0.2 %join_core.1 = (f32[17,48,128]{2,1,0:T(8,128)S(1)}, f32[16,128]{1,0:T(8,128)S(1)}) custom-call(f32[16,128]{1,0:T(8,128)S(1)} %get-tuple-element.30.sums_in, f32[6,384,128]{2,1,0:T(8,128)S(1)} %get-tuple-element.31.weights, f32[144,128]{1,0:T(8,128)S(1)} %get-tuple-element.32.sent_a, f32[144,128]{1,0:T(8,128)S(1)} %get-tuple-element.33.sent_b, ...), custom_call_target="tpu_custom_call" | custom-call | tf_op jit(solution)/shard_map/join_core/pallas_call | solution.py:730
  8.9 0.0 collective-permute-done.2.got
  9.0 0.5 %collective-permute-start.4 = (f32[2,128]{1,0:T(2,128)S(1)}, f32[2,128]{1,0:T(2,128)S(1)}, u32[]{:S(2)}, u32[]{:S(2)}) collective-permute-start(f32[2,128]{1,0:T(2,128)S(1)} %get-tuple-element.40), channel_id=1, source_target_pairs={{0,1},{1,0},{2,3},{3,2},{4,5},{5,4},{6,7},{7,6},{8,9},{9,8},{10,11... | collective-permute-start | bytes 3080 | tf_op jit(solution)/shard_map/ppermute | solution.py:607
  9.5 0.8 %collective-permute-done.4 = f32[2,128]{1,0:T(2,128)S(1)} collective-permute-done((f32[2,128]{1,0:T(2,128)S(1)}, f32[2,128]{1,0:T(2,128)S(1)}, u32[]{:S(2)}, u32[]{:S(2)}) %collective-permute-start.4) | collective-permute-done | bytes 1056 | tf_op jit(solution)/shard_map/ppermute | solution.py:607
  10.3 2.0 %collective-permute-start.5 = (f32[2,128]{1,0:T(2,128)S(1)}, f32[2,128]{1,0:T(2,128)S(1)}, u32[]{:S(2)}, u32[]{:S(2)}) collective-permute-start(f32[2,128]{1,0:T(2,128)S(1)} %add.15), channel_id=1, source_target_pairs={{0,3},{1,2},{2,1},{3,0},{4,7},{5,6},{6,5},{7,4},{8,11},{9,10},{10,... | collective-permute-start | bytes 3080 | tf_op jit(solution)/shard_map/ppermute | solution.py:607
  12.3 1.3 %collective-permute-done.5 = f32[2,128]{1,0:T(2,128)S(1)} collective-permute-done((f32[2,128]{1,0:T(2,128)S(1)}, f32[2,128]{1,0:T(2,128)S(1)}, u32[]{:S(2)}, u32[]{:S(2)}) %collective-permute-start.5) | collective-permute-done | bytes 1056 | tf_op jit(solution)/shard_map/ppermute | solution.py:607
  13.6 1.5 %collective-permute-start.6 = (f32[2,128]{1,0:T(2,128)S(1)}, f32[2,128]{1,0:T(2,128)S(1)}, u32[]{:S(2)}, u32[]{:S(2)}) collective-permute-start(f32[2,128]{1,0:T(2,128)S(1)} %add.16), channel_id=1, source_target_pairs={{0,5},{1,4},{2,7},{3,6},{4,1},{5,0},{6,3},{7,2},{8,13},{9,12},{10,... | collective-permute-start | bytes 3080 | tf_op jit(solution)/shard_map/ppermute | solution.py:607
  15.1 0.0 collective-permute-done.3.late
  15.1 1.2 %finish.1 = (f32[384,8,128]{2,1,0:T(8,128)S(1)}, f32[384,8,128]{2,1,0:T(8,128)}, f32[2,128]{1,0:T(2,128)S(1)}) custom-call(f32[384,8,128]{2,1,0:T(8,128)S(1)} %get-tuple-element.29.given, f32[17,48,128]{2,1,0:T(8,128)S(1)} %get-tuple-element.34.changes_core, f32[17,48,128]{2,1,0:T(8,128)S(1)} %get-tuple-element.38.changes_chip, ...), custom_call_target="tpu_custom_call", output_to_operand_aliasing={{0}: (0, {})} | custom-call | bytes 3145728 | tf_op jit(solution)/shard_map/finish/pallas_call | solution.py:760
  16.3 0.3 %collective-permute-done.6 = f32[2,128]{1,0:T(2,128)S(1)} collective-permute-done((f32[2,128]{1,0:T(2,128)S(1)}, f32[2,128]{1,0:T(2,128)S(1)}, u32[]{:S(2)}, u32[]{:S(2)}) %collective-permute-start.6) | collective-permute-done | bytes 1056 | tf_op jit(solution)/shard_map/ppermute | solution.py:607
  16.6 2.5 %collective-permute-start.7 = (f32[2,128]{1,0:T(2,128)S(1)}, f32[2,128]{1,0:T(2,128)S(1)}, u32[]{:S(2)}, u32[]{:S(2)}) collective-permute-start(f32[2,128]{1,0:T(2,128)S(1)} %add_add_fusion), channel_id=1, source_target_pairs={{0,9},{1,8},{2,11},{3,10},{4,13},{5,12},{6,15},{7,14},{8,1},{9,0},... | collective-permute-start | bytes 3080 | tf_op jit(solution)/shard_map/ppermute | solution.py:607
  19.1 1.4 %collective-permute-done.7 = f32[2,128]{1,0:T(2,128)S(1)} collective-permute-done((f32[2,128]{1,0:T(2,128)S(1)}, f32[2,128]{1,0:T(2,128)S(1)}, u32[]{:S(2)}, u32[]{:S(2)}) %collective-permute-start.7) | collective-permute-done | bytes 1056 | tf_op jit(solution)/shard_map/ppermute | solution.py:607
  20.5 0.6 %add.19 = f32[2,128]{1,0:T(2,128)} add(f32[2,128]{1,0:T(2,128)S(1)} %add_add_fusion, f32[2,128]{1,0:T(2,128)S(1)} %collective-permute-done.7) | non-fusion elementwise | flops 256 | bytes 3072 | tf_op jit(solution)/shard_map/add | solution.py:778
  (4 shorter events, 0.0 us)
Async XLA Ops:
  2.4 6.6 %collective-permute-start.2 = (f32[240,128]{1,0:T(8,128)S(1)}, f32[240,128]{1,0:T(8,128)S(1)}, u32[]{:S(2)}, u32[]{:S(2)}) collective-permute-start(f32[240,128]{1,0:T(8,128)S(1)} %get-tuple-element.36.sent), channel_id=1, source_target_pairs={{1,2},{2,1},{3,4},{4,3},{5,6},{6,5},{7,8},{8,7},{9,10},{10,9},{11,... | collective-permute-start | bytes 368648 | tf_op jit(solution)/shard_map/ppermute | solution.py:618
  5.4 3.4 %collective-permute-start = (f32[144,128]{1,0:T(8,128)S(1)}, f32[144,128]{1,0:T(8,128)S(1)}, u32[]{:S(2)}, u32[]{:S(2)}) collective-permute-start(f32[144,128]{1,0:T(8,128)S(1)} %get-tuple-element.32.sent_a), channel_id=1, source_target_pairs={{0,1},{1,0},{2,3},{3,2},{4,5},{5,4},{6,7},{7,6},{8,9},{9,8},{10,11... | collective-permute-start | bytes 221192 | tf_op jit(solution)/shard_map/ppermute | solution.py:607
  5.5 3.2 %collective-permute-start.1 = (f32[144,128]{1,0:T(8,128)S(1)}, f32[144,128]{1,0:T(8,128)S(1)}, u32[]{:S(2)}, u32[]{:S(2)}) collective-permute-start(f32[144,128]{1,0:T(8,128)S(1)} %get-tuple-element.33.sent_b), channel_id=1, source_target_pairs={{0,1},{1,0},{2,3},{3,2},{4,5},{5,4},{6,7},{7,6},{8,9},{9,8},{10,11... | collective-permute-start | bytes 221192 | tf_op jit(solution)/shard_map/ppermute | solution.py:607
  7.5 7.5 %collective-permute-start.3 = (f32[144,128]{1,0:T(8,128)S(1)}, f32[144,128]{1,0:T(8,128)S(1)}, u32[]{:S(2)}, u32[]{:S(2)}) collective-permute-start(f32[144,128]{1,0:T(8,128)S(1)} %get-tuple-element.37.late), channel_id=1, source_target_pairs={{1,2},{2,1},{3,4},{4,3},{5,6},{6,5},{7,8},{8,7},{9,10},{10,9},{11,... | collective-permute-start | bytes 221192 | tf_op jit(solution)/shard_map/ppermute | solution.py:618
  9.0 1.3 %collective-permute-start.4 = (f32[2,128]{1,0:T(2,128)S(1)}, f32[2,128]{1,0:T(2,128)S(1)}, u32[]{:S(2)}, u32[]{:S(2)}) collective-permute-start(f32[2,128]{1,0:T(2,128)S(1)} %get-tuple-element.40), channel_id=1, source_target_pairs={{0,1},{1,0},{2,3},{3,2},{4,5},{5,4},{6,7},{7,6},{8,9},{9,8},{10,11... | collective-permute-start | bytes 3080 | tf_op jit(solution)/shard_map/ppermute | solution.py:607
  10.3 3.3 %collective-permute-start.5 = (f32[2,128]{1,0:T(2,128)S(1)}, f32[2,128]{1,0:T(2,128)S(1)}, u32[]{:S(2)}, u32[]{:S(2)}) collective-permute-start(f32[2,128]{1,0:T(2,128)S(1)} %add.15), channel_id=1, source_target_pairs={{0,3},{1,2},{2,1},{3,0},{4,7},{5,6},{6,5},{7,4},{8,11},{9,10},{10,... | collective-permute-start | bytes 3080 | tf_op jit(solution)/shard_map/ppermute | solution.py:607
  13.6 3.0 %collective-permute-start.6 = (f32[2,128]{1,0:T(2,128)S(1)}, f32[2,128]{1,0:T(2,128)S(1)}, u32[]{:S(2)}, u32[]{:S(2)}) collective-permute-start(f32[2,128]{1,0:T(2,128)S(1)} %add.16), channel_id=1, source_target_pairs={{0,5},{1,4},{2,7},{3,6},{4,1},{5,0},{6,3},{7,2},{8,13},{9,12},{10,... | collective-permute-start | bytes 3080 | tf_op jit(solution)/shard_map/ppermute | solution.py:607
  16.6 3.9 %collective-permute-start.7 = (f32[2,128]{1,0:T(2,128)S(1)}, f32[2,128]{1,0:T(2,128)S(1)}, u32[]{:S(2)}, u32[]{:S(2)}) collective-permute-start(f32[2,128]{1,0:T(2,128)S(1)} %add_add_fusion), channel_id=1, source_target_pairs={{0,9},{1,8},{2,11},{3,10},{4,13},{5,12},{6,15},{7,14},{8,1},{9,0},... | collective-permute-start | bytes 3080 | tf_op jit(solution)/shard_map/ppermute | solution.py:607

commit v8 on v7

--- a/solution.py
+++ b/solution.py
@@ -127,7 +127,7 @@
     events, rows, depth, steps, sources = sizes
     final_kind = steps * 3 - 1
     copies = [
-        pltpu.make_async_copy(src, dst, sems.at[i])
+        pltpu.make_async_copy(src, dst, sems.at[min(i, 3) if i < 8 else 4])
         for i, (src, dst) in enumerate(
             [
                 (cells_hbm, cells),
@@ -179,8 +179,13 @@
     for event in range(events):
         record = pl.multiple_of(source[event] * rows, rows)
         pushes[pl.ds(event * rows, rows), :] = near_force[pl.ds(record, rows), :]
-    for copy in copies[3:-2]:
-        copy.wait()
+    def wait_tiles(index, count):
+        own = near.at[pl.ds(0, count)]
+        pltpu.make_async_copy(own, own, sems.at[index]).wait()
+
+    kind_tiles = events // 2
+    coeff_tiles = 2 * vel_ref.shape[0] // rows
+    wait_tiles(3, FIELDS * events * 4 // rows + kind_tiles + coeff_tiles)
     weights[...] = forward[final_kind].astype(jnp.float32)
     vel = load_coeffs(vel_ref)
     stress = load_coeffs(stress_ref)
@@ -264,8 +269,7 @@
             message_chip[pl.ds(i * events + chunk, 8), :] = jnp.where(odd, right_soon[i], left_soon[i])
         for i in range(LATE):
             message_late[pl.ds(i * events + chunk, 8), :] = jnp.where(odd, right_late[i], left[3 + i])
-    for copy in copies[-2:]:
-        copy.wait()
+    wait_tiles(4, FIELDS * events * (rows - 4) // rows + final_kind * kind_tiles)
 
 
 def group_of(events):
@@ -680,7 +684,7 @@
             pltpu.VMEM(force.shape, f32),
             pltpu.VMEM(force.shape, f32),
             pltpu.VMEM((tiles, depth), f32),
-            pltpu.SemaphoreType.DMA((10,)),
+            pltpu.SemaphoreType.DMA((5,)),
         ],
         compiler_params=limits,
         name="edges",

time: 21.2 us -> 21.2 us (level)
  no operation moved by 1% of the time
where the time goes in v8:
time: 21.2 us; the launch traced here: 21 us
  starting transfers between devices  11.1 us (52%)
  Pallas kernels  4.78 us (23%)
  waiting for transfers between devices  3.87 us (18%)
  between operations  0.68 us (3%)
  other arithmetic  0.58 us (3%)
    ppermute x6, starting transfers between devices, swap_with(): return lax.ppermute(value, 'gx', [(i, i ^ mask) for i in range(size)])  6.91 us
    ppermute x2, starting transfers between devices, swap_over_chips(): return lax.ppermute(value, ('groups', 'gx'), route)  4.2 us
    ppermute x6, waiting for transfers between devices, swap_with(): return lax.ppermute(value, 'gx', [(i, i ^ mask) for i in range(size)])  3.86 us
    pallas_call x1, Pallas kernels, shards(): pl.pallas_call(functools.partial(edge_kernel, sizes), out_shape=(pltpu.VM...  1.67 us
    pallas_call x1, Pallas kernels, shards(): pl.pallas_call(functools.partial(bulk_kernel, sizes), out_shape=(pltpu.VM...  1.64 us
    pallas_call x1, Pallas kernels, shards(): pl.pallas_call(functools.partial(finish_kernel, sizes), out_shape=(pltpu....  1.22 us
    add x3, other arithmetic, shards(): totals = totals + swap_with(totals, size, mask | 1)  0.57 us
  transfers between devices with their start and end apart: 8, of which 4 were waited for; matrix products, arithmetic and copies ran while one was open for 0% of the time, Pallas kernels for 15%

profile of v8, /device:TPU:0, one launch (start us, length us, event | category | flops | bytes accessed | tf_op | source)
XLA Modules:
  0.0 21.0 jit_solution(10160746610808841200)
XLA Ops:
  0.6 1.7 %edges.1 = (f32[384,8,128]{2,1,0:T(8,128)S(1)}, bf16[6,384,128]{2,1,0:T(8,128)(2,1)S(1)}, s32[48]{0:T(128)S(4)}, f32[128,128]{1,0:T(8,128)S(1)}, f32[144,128]{1,...) custom-call(f32[384,8,128]{2,1,0:T(8,128)} %bitcast.9, ...), custom_call_target="tpu_custom_call" | custom-call | tf_op jit(solution)/shard_map/edges/pallas_call | solution.py:665
  2.3 3.0 %collective-permute-start.2 = (f32[240,128]{1,0:T(8,128)S(1)}, f32[240,128]{1,0:T(8,128)S(1)}, u32[]{:S(2)}, u32[]{:S(2)}) collective-permute-start(f32[240,128]{1,0:T(8,128)S(1)} %get-tuple-element.36.sent), channel_id=1, source_target_pairs={{1,2},{2,1},{3,4},{4,3},{5,6},{6,5},{7,8},{8,7},{9,10},{10,9},{11,... | collective-permute-start | bytes 368648 | tf_op jit(solution)/shard_map/ppermute | solution.py:622
  5.3 0.1 collective-permute-start
  5.5 0.4 %collective-permute-start.1 = (f32[144,128]{1,0:T(8,128)S(1)}, f32[144,128]{1,0:T(8,128)S(1)}, u32[]{:S(2)}, u32[]{:S(2)}) collective-permute-start(f32[144,128]{1,0:T(8,128)S(1)} %get-tuple-element.33.sent_b), channel_id=1, source_target_pairs={{0,1},{1,0},{2,3},{3,2},{4,5},{5,4},{6,7},{7,6},{8,9},{9,8},{10,11... | collective-permute-start | bytes 221192 | tf_op jit(solution)/shard_map/ppermute | solution.py:611
  5.8 1.6 %bulk.1 = (f32[384,8,128]{2,1,0:T(8,128)S(1)}, f32[6,384,128]{2,1,0:T(8,128)S(1)}, f32[16,128]{1,0:T(8,128)S(1)}, f32[144,128]{1,0:T(8,128)S(1)}) custom-call(f32[384,8,128]{2,1,0:T(8,128)S(1)} %get-tuple-element.22.given, bf16[6,384,128]{2,1,0:T(8,128)(2,1)S(1)} %get-tuple-element.23.forward, ...), custom_call_target="tpu_custom_call", output_to_operand_aliasing={{0}: (0, {}), {3}: (6, {})} | custom-call | flops 7864320 | bytes 3145728 | tf_op jit(solution)/shard_map/bulk/pallas_call | solution.py:708
  7.5 1.2 %collective-permute-start.3 = (f32[144,128]{1,0:T(8,128)S(1)}, f32[144,128]{1,0:T(8,128)S(1)}, u32[]{:S(2)}, u32[]{:S(2)}) collective-permute-start(f32[144,128]{1,0:T(8,128)S(1)} %get-tuple-element.37.late), channel_id=1, source_target_pairs={{1,2},{2,1},{3,4},{4,3},{5,6},{6,5},{7,8},{8,7},{9,10},{10,9},{11,... | collective-permute-start | bytes 221192 | tf_op jit(solution)/shard_map/ppermute | solution.py:622
  8.7 0.0 collective-permute-done.got_a
  8.7 0.0 collective-permute-done.1.got_b
  8.7 0.2 %join_core.1 = (f32[17,48,128]{2,1,0:T(8,128)S(1)}, f32[16,128]{1,0:T(8,128)S(1)}) custom-call(f32[16,128]{1,0:T(8,128)S(1)} %get-tuple-element.30.sums_in, f32[6,384,128]{2,1,0:T(8,128)S(1)} %get-tuple-element.31.weights, f32[144,128]{1,0:T(8,128)S(1)} %get-tuple-element.32.sent_a, f32[144,128]{1,0:T(8,128)S(1)} %get-tuple-element.33.sent_b, ...), custom_call_target="tpu_custom_call" | custom-call | tf_op jit(solution)/shard_map/join_core/pallas_call | solution.py:734
  8.9 0.0 collective-permute-done.2.got
  8.9 0.5 %collective-permute-start.4 = (f32[2,128]{1,0:T(2,128)S(1)}, f32[2,128]{1,0:T(2,128)S(1)}, u32[]{:S(2)}, u32[]{:S(2)}) collective-permute-start(f32[2,128]{1,0:T(2,128)S(1)} %get-tuple-element.40), channel_id=1, source_target_pairs={{0,1},{1,0},{2,3},{3,2},{4,5},{5,4},{6,7},{7,6},{8,9},{9,8},{10,11... | collective-permute-start | bytes 3080 | tf_op jit(solution)/shard_map/ppermute | solution.py:611
  9.4 0.8 %collective-permute-done.4 = f32[2,128]{1,0:T(2,128)S(1)} collective-permute-done((f32[2,128]{1,0:T(2,128)S(1)}, f32[2,128]{1,0:T(2,128)S(1)}, u32[]{:S(2)}, u32[]{:S(2)}) %collective-permute-start.4) | collective-permute-done | bytes 1056 | tf_op jit(solution)/shard_map/ppermute | solution.py:611
  10.3 2.0 %collective-permute-start.5 = (f32[2,128]{1,0:T(2,128)S(1)}, f32[2,128]{1,0:T(2,128)S(1)}, u32[]{:S(2)}, u32[]{:S(2)}) collective-permute-start(f32[2,128]{1,0:T(2,128)S(1)} %add.15), channel_id=1, source_target_pairs={{0,3},{1,2},{2,1},{3,0},{4,7},{5,6},{6,5},{7,4},{8,11},{9,10},{10,... | collective-permute-start | bytes 3080 | tf_op jit(solution)/shard_map/ppermute | solution.py:611
  12.3 1.3 %collective-permute-done.5 = f32[2,128]{1,0:T(2,128)S(1)} collective-permute-done((f32[2,128]{1,0:T(2,128)S(1)}, f32[2,128]{1,0:T(2,128)S(1)}, u32[]{:S(2)}, u32[]{:S(2)}) %collective-permute-start.5) | collective-permute-done | bytes 1056 | tf_op jit(solution)/shard_map/ppermute | solution.py:611
  13.6 1.5 %collective-permute-start.6 = (f32[2,128]{1,0:T(2,128)S(1)}, f32[2,128]{1,0:T(2,128)S(1)}, u32[]{:S(2)}, u32[]{:S(2)}) collective-permute-start(f32[2,128]{1,0:T(2,128)S(1)} %add.16), channel_id=1, source_target_pairs={{0,5},{1,4},{2,7},{3,6},{4,1},{5,0},{6,3},{7,2},{8,13},{9,12},{10,... | collective-permute-start | bytes 3080 | tf_op jit(solution)/shard_map/ppermute | solution.py:611
  15.0 0.0 collective-permute-done.3.late
  15.0 1.2 %finish.1 = (f32[384,8,128]{2,1,0:T(8,128)S(1)}, f32[384,8,128]{2,1,0:T(8,128)}, f32[2,128]{1,0:T(2,128)S(1)}) custom-call(f32[384,8,128]{2,1,0:T(8,128)S(1)} %get-tuple-element.29.given, f32[17,48,128]{2,1,0:T(8,128)S(1)} %get-tuple-element.34.changes_core, f32[17,48,128]{2,1,0:T(8,128)S(1)} %get-tuple-element.38.changes_chip, ...), custom_call_target="tpu_custom_call", output_to_operand_aliasing={{0}: (0, {})} | custom-call | bytes 3145728 | tf_op jit(solution)/shard_map/finish/pallas_call | solution.py:764
  16.2 0.3 %collective-permute-done.6 = f32[2,128]{1,0:T(2,128)S(1)} collective-permute-done((f32[2,128]{1,0:T(2,128)S(1)}, f32[2,128]{1,0:T(2,128)S(1)}, u32[]{:S(2)}, u32[]{:S(2)}) %collective-permute-start.6) | collective-permute-done | bytes 1056 | tf_op jit(solution)/shard_map/ppermute | solution.py:611
  16.6 2.5 %collective-permute-start.7 = (f32[2,128]{1,0:T(2,128)S(1)}, f32[2,128]{1,0:T(2,128)S(1)}, u32[]{:S(2)}, u32[]{:S(2)}) collective-permute-start(f32[2,128]{1,0:T(2,128)S(1)} %add_add_fusion), channel_id=1, source_target_pairs={{0,9},{1,8},{2,11},{3,10},{4,13},{5,12},{6,15},{7,14},{8,1},{9,0},... | collective-permute-start | bytes 3080 | tf_op jit(solution)/shard_map/ppermute | solution.py:611
  19.0 1.4 %collective-permute-done.7 = f32[2,128]{1,0:T(2,128)S(1)} collective-permute-done((f32[2,128]{1,0:T(2,128)S(1)}, f32[2,128]{1,0:T(2,128)S(1)}, u32[]{:S(2)}, u32[]{:S(2)}) %collective-permute-start.7) | collective-permute-done | bytes 1056 | tf_op jit(solution)/shard_map/ppermute | solution.py:611
  20.5 0.6 %add.19 = f32[2,128]{1,0:T(2,128)} add(f32[2,128]{1,0:T(2,128)S(1)} %add_add_fusion, f32[2,128]{1,0:T(2,128)S(1)} %collective-permute-done.7) | non-fusion elementwise | flops 256 | bytes 3072 | tf_op jit(solution)/shard_map/add | solution.py:782
  (4 shorter events, 0.0 us)
Async XLA Ops:
  2.3 6.6 %collective-permute-start.2 = (f32[240,128]{1,0:T(8,128)S(1)}, f32[240,128]{1,0:T(8,128)S(1)}, u32[]{:S(2)}, u32[]{:S(2)}) collective-permute-start(f32[240,128]{1,0:T(8,128)S(1)} %get-tuple-element.36.sent), channel_id=1, source_target_pairs={{1,2},{2,1},{3,4},{4,3},{5,6},{6,5},{7,8},{8,7},{9,10},{10,9},{11,... | collective-permute-start | bytes 368648 | tf_op jit(solution)/shard_map/ppermute | solution.py:622
  5.3 3.4 %collective-permute-start = (f32[144,128]{1,0:T(8,128)S(1)}, f32[144,128]{1,0:T(8,128)S(1)}, u32[]{:S(2)}, u32[]{:S(2)}) collective-permute-start(f32[144,128]{1,0:T(8,128)S(1)} %get-tuple-element.32.sent_a), channel_id=1, source_target_pairs={{0,1},{1,0},{2,3},{3,2},{4,5},{5,4},{6,7},{7,6},{8,9},{9,8},{10,11... | collective-permute-start | bytes 221192 | tf_op jit(solution)/shard_map/ppermute | solution.py:611
  5.5 3.2 %collective-permute-start.1 = (f32[144,128]{1,0:T(8,128)S(1)}, f32[144,128]{1,0:T(8,128)S(1)}, u32[]{:S(2)}, u32[]{:S(2)}) collective-permute-start(f32[144,128]{1,0:T(8,128)S(1)} %get-tuple-element.33.sent_b), channel_id=1, source_target_pairs={{0,1},{1,0},{2,3},{3,2},{4,5},{5,4},{6,7},{7,6},{8,9},{9,8},{10,11... | collective-permute-start | bytes 221192 | tf_op jit(solution)/shard_map/ppermute | solution.py:611
  7.5 7.5 %collective-permute-start.3 = (f32[144,128]{1,0:T(8,128)S(1)}, f32[144,128]{1,0:T(8,128)S(1)}, u32[]{:S(2)}, u32[]{:S(2)}) collective-permute-start(f32[144,128]{1,0:T(8,128)S(1)} %get-tuple-element.37.late), channel_id=1, source_target_pairs={{1,2},{2,1},{3,4},{4,3},{5,6},{6,5},{7,8},{8,7},{9,10},{10,9},{11,... | collective-permute-start | bytes 221192 | tf_op jit(solution)/shard_map/ppermute | solution.py:622
  8.9 1.3 %collective-permute-start.4 = (f32[2,128]{1,0:T(2,128)S(1)}, f32[2,128]{1,0:T(2,128)S(1)}, u32[]{:S(2)}, u32[]{:S(2)}) collective-permute-start(f32[2,128]{1,0:T(2,128)S(1)} %get-tuple-element.40), channel_id=1, source_target_pairs={{0,1},{1,0},{2,3},{3,2},{4,5},{5,4},{6,7},{7,6},{8,9},{9,8},{10,11... | collective-permute-start | bytes 3080 | tf_op jit(solution)/shard_map/ppermute | solution.py:611
  10.3 3.3 %collective-permute-start.5 = (f32[2,128]{1,0:T(2,128)S(1)}, f32[2,128]{1,0:T(2,128)S(1)}, u32[]{:S(2)}, u32[]{:S(2)}) collective-permute-start(f32[2,128]{1,0:T(2,128)S(1)} %add.15), channel_id=1, source_target_pairs={{0,3},{1,2},{2,1},{3,0},{4,7},{5,6},{6,5},{7,4},{8,11},{9,10},{10,... | collective-permute-start | bytes 3080 | tf_op jit(solution)/shard_map/ppermute | solution.py:611
  13.6 3.0 %collective-permute-start.6 = (f32[2,128]{1,0:T(2,128)S(1)}, f32[2,128]{1,0:T(2,128)S(1)}, u32[]{:S(2)}, u32[]{:S(2)}) collective-permute-start(f32[2,128]{1,0:T(2,128)S(1)} %add.16), channel_id=1, source_target_pairs={{0,5},{1,4},{2,7},{3,6},{4,1},{5,0},{6,3},{7,2},{8,13},{9,12},{10,... | collective-permute-start | bytes 3080 | tf_op jit(solution)/shard_map/ppermute | solution.py:611
  16.6 3.9 %collective-permute-start.7 = (f32[2,128]{1,0:T(2,128)S(1)}, f32[2,128]{1,0:T(2,128)S(1)}, u32[]{:S(2)}, u32[]{:S(2)}) collective-permute-start(f32[2,128]{1,0:T(2,128)S(1)} %add_add_fusion), channel_id=1, source_target_pairs={{0,9},{1,8},{2,11},{3,10},{4,13},{5,12},{6,15},{7,14},{8,1},{9,0},... | collective-permute-start | bytes 3080 | tf_op jit(solution)/shard_map/ppermute | solution.py:611

commit v9 on v8

--- a/solution.py
+++ b/solution.py
@@ -12,7 +12,7 @@
 VX, VZ, QX, QZ, SXX, SZZ, SXZ, PR = range(FIELDS)
 HALO = 6
 SOON = 5
-LATE = 3
+LATE = 2
 PUSHED = ((0, 0), (0, 1), (1, 0), (0, -1))
 GROUPS = (16, 8, 4, 2)
 ROOM = 16 << 20
@@ -264,7 +264,7 @@
         weight = weights[pl.ds(chunk * rows, 8, stride=rows), :]
         right_soon = right[:3] + [flow, stress_final[2]]
         left_soon = left[:3] + [drain, weight]
-        right_late = [stress_final[0], stress_final[3], stress_final[3]]
+        right_late = [stress_final[0], stress_final[3]]
         for i in range(SOON):
             message_chip[pl.ds(i * events + chunk, 8), :] = jnp.where(odd, right_soon[i], left_soon[i])
         for i in range(LATE):
@@ -555,7 +555,7 @@
 
 
 def finish_kernel(
-    sizes, given, changes_core, changes_chip, late, vel_ref, stress_ref, changed, out_hbm, done, sems
+    sizes, given, changes_core, changes_chip, soon, late, vel_ref, stress_ref, changed, out_hbm, done, sems
 ):
     events, rows, depth, _, _ = sizes
     state_in = given.reshape(FIELDS, events * rows, depth)
@@ -573,7 +573,9 @@
         return {(VX, 0): -push} | {(SXX + f, 0): stresses[f] for f in range(4)}
 
     def right_late():
-        again = [got[i] + changes_chip[len(right_places) + i] for i in range(LATE)]
+        drain = soon[pl.ds(3 * events, events), :]
+        flow = (drain - stress[2] * got[0]) / stress[3]
+        again = [value + changes_chip[len(right_places) + i] for i, value in enumerate((*got, flow))]
         stresses = beyond_gain(stress, *again)
         return {(SXX + f, last): stresses[f] for f in range(4)}
 
@@ -768,14 +770,14 @@
             jax.ShapeDtypeStruct(state.shape, f32),
             pltpu.VMEM((2, depth), f32),
         ),
-        in_specs=[vmem] * 6,
+        in_specs=[vmem] * 7,
         out_specs=(vmem, any_space, vmem),
         input_output_aliases={0: 0},
         scratch_shapes=[pltpu.SemaphoreType.DMA((2,))],
         compiler_params=limits,
         cost_estimate=pl.CostEstimate(flops=0, bytes_accessed=2 * 4 * state.size, transcendentals=0),
         name="finish",
-    )(*kept(pltpu.VMEM, state, changes_core, changes_chip, got_late, vel, stress))
+    )(*kept(pltpu.VMEM, state, changes_core, changes_chip, got_chip, got_late, vel, stress))
 
     mask = 1
     while mask < size:

time: 21.2 us -> 21.2 us (level)
  no operation moved by 1% of the time
where the time goes in v9:
time: 21.2 us; the launch traced here: 21 us
  starting transfers between devices  11.1 us (52%)
  Pallas kernels  4.75 us (22%)
  waiting for transfers between devices  3.87 us (18%)
  between operations  0.68 us (3%)
  other arithmetic  0.58 us (3%)
    ppermute x6, starting transfers between devices, swap_with(): return lax.ppermute(value, 'gx', [(i, i ^ mask) for i in range(size)])  6.95 us
    ppermute x2, starting transfers between devices, swap_over_chips(): return lax.ppermute(value, ('groups', 'gx'), route)  4.19 us
    ppermute x6, waiting for transfers between devices, swap_with(): return lax.ppermute(value, 'gx', [(i, i ^ mask) for i in range(size)])  3.86 us
    pallas_call x1, Pallas kernels, shards(): pl.pallas_call(functools.partial(edge_kernel, sizes), out_shape=(pltpu.VM...  1.67 us
    pallas_call x1, Pallas kernels, shards(): pl.pallas_call(functools.partial(bulk_kernel, sizes), out_shape=(pltpu.VM...  1.61 us
    pallas_call x1, Pallas kernels, shards(): pl.pallas_call(functools.partial(finish_kernel, sizes), out_shape=(pltpu....  1.22 us
    add x3, other arithmetic, shards(): totals = totals + swap_with(totals, size, mask | 1)  0.57 us
  transfers between devices with their start and end apart: 8, of which 4 were waited for; matrix products, arithmetic and copies ran while one was open for 0% of the time, Pallas kernels for 15%

profile of v9, /device:TPU:0, one launch (start us, length us, event | category | flops | bytes accessed | tf_op | source)
XLA Modules:
  0.0 21.0 jit_solution(106199032293709820)
XLA Ops:
  0.6 1.7 %edges.1 = (f32[384,8,128]{2,1,0:T(8,128)S(1)}, bf16[6,384,128]{2,1,0:T(8,128)(2,1)S(1)}, s32[48]{0:T(128)S(4)}, f32[128,128]{1,0:T(8,128)S(1)}, f32[144,128]{1,...) custom-call(f32[384,8,128]{2,1,0:T(8,128)} %bitcast.9, ...), custom_call_target="tpu_custom_call" | custom-call | tf_op jit(solution)/shard_map/edges/pallas_call | solution.py:667
  2.3 3.0 %collective-permute-start.2 = (f32[240,128]{1,0:T(8,128)S(1)}, f32[240,128]{1,0:T(8,128)S(1)}, u32[]{:S(2)}, u32[]{:S(2)}) collective-permute-start(f32[240,128]{1,0:T(8,128)S(1)} %get-tuple-element.36.sent), channel_id=1, source_target_pairs={{1,2},{2,1},{3,4},{4,3},{5,6},{6,5},{7,8},{8,7},{9,10},{10,9},{11,... | collective-permute-start | bytes 368648 | tf_op jit(solution)/shard_map/ppermute | solution.py:624
  5.3 0.1 collective-permute-start
  5.5 0.4 %collective-permute-start.1 = (f32[144,128]{1,0:T(8,128)S(1)}, f32[144,128]{1,0:T(8,128)S(1)}, u32[]{:S(2)}, u32[]{:S(2)}) collective-permute-start(f32[144,128]{1,0:T(8,128)S(1)} %get-tuple-element.33.sent_b), channel_id=1, source_target_pairs={{0,1},{1,0},{2,3},{3,2},{4,5},{5,4},{6,7},{7,6},{8,9},{9,8},{10,11... | collective-permute-start | bytes 221192 | tf_op jit(solution)/shard_map/ppermute | solution.py:613
  5.8 1.6 %bulk.1 = (f32[384,8,128]{2,1,0:T(8,128)S(1)}, f32[6,384,128]{2,1,0:T(8,128)S(1)}, f32[16,128]{1,0:T(8,128)S(1)}, f32[96,128]{1,0:T(8,128)S(1)}) custom-call(f32[384,8,128]{2,1,0:T(8,128)S(1)} %get-tuple-element.22.given, bf16[6,384,128]{2,1,0:T(8,128)(2,1)S(1)} %get-tuple-element.23.forward, ...), custom_call_target="tpu_custom_call", output_to_operand_aliasing={{0}: (0, {}), {3}: (6, {})} | custom-call | flops 7864320 | bytes 3145728 | tf_op jit(solution)/shard_map/bulk/pallas_call | solution.py:710
  7.4 1.2 %collective-permute-start.3 = (f32[96,128]{1,0:T(8,128)S(1)}, f32[96,128]{1,0:T(8,128)S(1)}, u32[]{:S(2)}, u32[]{:S(2)}) collective-permute-start(f32[96,128]{1,0:T(8,128)S(1)} %get-tuple-element.37.late), channel_id=1, source_target_pairs={{1,2},{2,1},{3,4},{4,3},{5,6},{6,5},{7,8},{8,7},{9,10},{10,9},{11,... | collective-permute-start | bytes 147464 | tf_op jit(solution)/shard_map/ppermute | solution.py:624
  8.6 0.0 collective-permute-done.got_a
  8.6 0.0 collective-permute-done.1.got_b
  8.6 0.2 %join_core.1 = (f32[17,48,128]{2,1,0:T(8,128)S(1)}, f32[16,128]{1,0:T(8,128)S(1)}) custom-call(f32[16,128]{1,0:T(8,128)S(1)} %get-tuple-element.30.sums_in, f32[6,384,128]{2,1,0:T(8,128)S(1)} %get-tuple-element.31.weights, f32[144,128]{1,0:T(8,128)S(1)} %get-tuple-element.32.sent_a, f32[144,128]{1,0:T(8,128)S(1)} %get-tuple-element.33.sent_b, ...), custom_call_target="tpu_custom_call" | custom-call | tf_op jit(solution)/shard_map/join_core/pallas_call | solution.py:736
  8.9 0.0 collective-permute-done.2.got.soon
  8.9 0.5 %collective-permute-start.4 = (f32[2,128]{1,0:T(2,128)S(1)}, f32[2,128]{1,0:T(2,128)S(1)}, u32[]{:S(2)}, u32[]{:S(2)}) collective-permute-start(f32[2,128]{1,0:T(2,128)S(1)} %get-tuple-element.40), channel_id=1, source_target_pairs={{0,1},{1,0},{2,3},{3,2},{4,5},{5,4},{6,7},{7,6},{8,9},{9,8},{10,11... | collective-permute-start | bytes 3080 | tf_op jit(solution)/shard_map/ppermute | solution.py:613
  9.4 0.8 %collective-permute-done.4 = f32[2,128]{1,0:T(2,128)S(1)} collective-permute-done((f32[2,128]{1,0:T(2,128)S(1)}, f32[2,128]{1,0:T(2,128)S(1)}, u32[]{:S(2)}, u32[]{:S(2)}) %collective-permute-start.4) | collective-permute-done | bytes 1056 | tf_op jit(solution)/shard_map/ppermute | solution.py:613
  10.2 2.0 %collective-permute-start.5 = (f32[2,128]{1,0:T(2,128)S(1)}, f32[2,128]{1,0:T(2,128)S(1)}, u32[]{:S(2)}, u32[]{:S(2)}) collective-permute-start(f32[2,128]{1,0:T(2,128)S(1)} %add.15), channel_id=1, source_target_pairs={{0,3},{1,2},{2,1},{3,0},{4,7},{5,6},{6,5},{7,4},{8,11},{9,10},{10,... | collective-permute-start | bytes 3080 | tf_op jit(solution)/shard_map/ppermute | solution.py:613
  12.3 1.3 %collective-permute-done.5 = f32[2,128]{1,0:T(2,128)S(1)} collective-permute-done((f32[2,128]{1,0:T(2,128)S(1)}, f32[2,128]{1,0:T(2,128)S(1)}, u32[]{:S(2)}, u32[]{:S(2)}) %collective-permute-start.5) | collective-permute-done | bytes 1056 | tf_op jit(solution)/shard_map/ppermute | solution.py:613
  13.6 1.5 %collective-permute-start.6 = (f32[2,128]{1,0:T(2,128)S(1)}, f32[2,128]{1,0:T(2,128)S(1)}, u32[]{:S(2)}, u32[]{:S(2)}) collective-permute-start(f32[2,128]{1,0:T(2,128)S(1)} %add.16), channel_id=1, source_target_pairs={{0,5},{1,4},{2,7},{3,6},{4,1},{5,0},{6,3},{7,2},{8,13},{9,12},{10,... | collective-permute-start | bytes 3080 | tf_op jit(solution)/shard_map/ppermute | solution.py:613
  15.0 0.0 collective-permute-done.3.late
  15.0 1.2 %finish.1 = (f32[384,8,128]{2,1,0:T(8,128)S(1)}, f32[384,8,128]{2,1,0:T(8,128)}, f32[2,128]{1,0:T(2,128)S(1)}) custom-call(f32[384,8,128]{2,1,0:T(8,128)S(1)} %get-tuple-element.29.given, f32[17,48,128]{2,1,0:T(8,128)S(1)} %get-tuple-element.34.changes_core, f32[17,48,128]{2,1,0:T(8,128)S(1)} %get-tuple-element.38.changes_chip, ...), custom_call_target="tpu_custom_call", output_to_operand_aliasing={{0}: (0, {})} | custom-call | bytes 3145728 | tf_op jit(solution)/shard_map/finish/pallas_call | solution.py:766
  16.2 0.3 %collective-permute-done.6 = f32[2,128]{1,0:T(2,128)S(1)} collective-permute-done((f32[2,128]{1,0:T(2,128)S(1)}, f32[2,128]{1,0:T(2,128)S(1)}, u32[]{:S(2)}, u32[]{:S(2)}) %collective-permute-start.6) | collective-permute-done | bytes 1056 | tf_op jit(solution)/shard_map/ppermute | solution.py:613
  16.6 2.5 %collective-permute-start.7 = (f32[2,128]{1,0:T(2,128)S(1)}, f32[2,128]{1,0:T(2,128)S(1)}, u32[]{:S(2)}, u32[]{:S(2)}) collective-permute-start(f32[2,128]{1,0:T(2,128)S(1)} %add_add_fusion), channel_id=1, source_target_pairs={{0,9},{1,8},{2,11},{3,10},{4,13},{5,12},{6,15},{7,14},{8,1},{9,0},... | collective-permute-start | bytes 3080 | tf_op jit(solution)/shard_map/ppermute | solution.py:613
  19.0 1.4 %collective-permute-done.7 = f32[2,128]{1,0:T(2,128)S(1)} collective-permute-done((f32[2,128]{1,0:T(2,128)S(1)}, f32[2,128]{1,0:T(2,128)S(1)}, u32[]{:S(2)}, u32[]{:S(2)}) %collective-permute-start.7) | collective-permute-done | bytes 1056 | tf_op jit(solution)/shard_map/ppermute | solution.py:613
  20.5 0.6 %add.19 = f32[2,128]{1,0:T(2,128)} add(f32[2,128]{1,0:T(2,128)S(1)} %add_add_fusion, f32[2,128]{1,0:T(2,128)S(1)} %collective-permute-done.7) | non-fusion elementwise | flops 256 | bytes 3072 | tf_op jit(solution)/shard_map/add | solution.py:784
  (4 shorter events, 0.0 us)
Async XLA Ops:
  2.3 6.6 %collective-permute-start.2 = (f32[240,128]{1,0:T(8,128)S(1)}, f32[240,128]{1,0:T(8,128)S(1)}, u32[]{:S(2)}, u32[]{:S(2)}) collective-permute-start(f32[240,128]{1,0:T(8,128)S(1)} %get-tuple-element.36.sent), channel_id=1, source_target_pairs={{1,2},{2,1},{3,4},{4,3},{5,6},{6,5},{7,8},{8,7},{9,10},{10,9},{11,... | collective-permute-start | bytes 368648 | tf_op jit(solution)/shard_map/ppermute | solution.py:624
  5.3 3.3 %collective-permute-start = (f32[144,128]{1,0:T(8,128)S(1)}, f32[144,128]{1,0:T(8,128)S(1)}, u32[]{:S(2)}, u32[]{:S(2)}) collective-permute-start(f32[144,128]{1,0:T(8,128)S(1)} %get-tuple-element.32.sent_a), channel_id=1, source_target_pairs={{0,1},{1,0},{2,3},{3,2},{4,5},{5,4},{6,7},{7,6},{8,9},{9,8},{10,11... | collective-permute-start | bytes 221192 | tf_op jit(solution)/shard_map/ppermute | solution.py:613
  5.5 3.2 %collective-permute-start.1 = (f32[144,128]{1,0:T(8,128)S(1)}, f32[144,128]{1,0:T(8,128)S(1)}, u32[]{:S(2)}, u32[]{:S(2)}) collective-permute-start(f32[144,128]{1,0:T(8,128)S(1)} %get-tuple-element.33.sent_b), channel_id=1, source_target_pairs={{0,1},{1,0},{2,3},{3,2},{4,5},{5,4},{6,7},{7,6},{8,9},{9,8},{10,11... | collective-permute-start | bytes 221192 | tf_op jit(solution)/shard_map/ppermute | solution.py:613
  7.4 7.6 %collective-permute-start.3 = (f32[96,128]{1,0:T(8,128)S(1)}, f32[96,128]{1,0:T(8,128)S(1)}, u32[]{:S(2)}, u32[]{:S(2)}) collective-permute-start(f32[96,128]{1,0:T(8,128)S(1)} %get-tuple-element.37.late), channel_id=1, source_target_pairs={{1,2},{2,1},{3,4},{4,3},{5,6},{6,5},{7,8},{8,7},{9,10},{10,9},{11,... | collective-permute-start | bytes 147464 | tf_op jit(solution)/shard_map/ppermute | solution.py:624
  8.9 1.3 %collective-permute-start.4 = (f32[2,128]{1,0:T(2,128)S(1)}, f32[2,128]{1,0:T(2,128)S(1)}, u32[]{:S(2)}, u32[]{:S(2)}) collective-permute-start(f32[2,128]{1,0:T(2,128)S(1)} %get-tuple-element.40), channel_id=1, source_target_pairs={{0,1},{1,0},{2,3},{3,2},{4,5},{5,4},{6,7},{7,6},{8,9},{9,8},{10,11... | collective-permute-start | bytes 3080 | tf_op jit(solution)/shard_map/ppermute | solution.py:613
  10.2 3.3 %collective-permute-start.5 = (f32[2,128]{1,0:T(2,128)S(1)}, f32[2,128]{1,0:T(2,128)S(1)}, u32[]{:S(2)}, u32[]{:S(2)}) collective-permute-start(f32[2,128]{1,0:T(2,128)S(1)} %add.15), channel_id=1, source_target_pairs={{0,3},{1,2},{2,1},{3,0},{4,7},{5,6},{6,5},{7,4},{8,11},{9,10},{10,... | collective-permute-start | bytes 3080 | tf_op jit(solution)/shard_map/ppermute | solution.py:613
  13.6 3.0 %collective-permute-start.6 = (f32[2,128]{1,0:T(2,128)S(1)}, f32[2,128]{1,0:T(2,128)S(1)}, u32[]{:S(2)}, u32[]{:S(2)}) collective-permute-start(f32[2,128]{1,0:T(2,128)S(1)} %add.16), channel_id=1, source_target_pairs={{0,5},{1,4},{2,7},{3,6},{4,1},{5,0},{6,3},{7,2},{8,13},{9,12},{10,... | collective-permute-start | bytes 3080 | tf_op jit(solution)/shard_map/ppermute | solution.py:613
  16.6 3.9 %collective-permute-start.7 = (f32[2,128]{1,0:T(2,128)S(1)}, f32[2,128]{1,0:T(2,128)S(1)}, u32[]{:S(2)}, u32[]{:S(2)}) collective-permute-start(f32[2,128]{1,0:T(2,128)S(1)} %add_add_fusion), channel_id=1, source_target_pairs={{0,9},{1,8},{2,11},{3,10},{4,13},{5,12},{6,15},{7,14},{8,1},{9,0},... | collective-permute-start | bytes 3080 | tf_op jit(solution)/shard_map/ppermute | solution.py:613

commit v10 on v8

--- a/solution.py
+++ b/solution.py
@@ -14,7 +14,7 @@
 SOON = 5
 LATE = 3
 PUSHED = ((0, 0), (0, 1), (1, 0), (0, -1))
-GROUPS = (16, 8, 4, 2)
+GROUPS = (24, 16, 8, 4, 2)
 ROOM = 16 << 20
 
 

time: 21.2 us -> 21.2 us (level)
  starting transfers between devices: 11.1 us -> 11.4 us
  Pallas kernels: 4.78 us -> 4.51 us
    ppermute x6, starting transfers between devices: 6.91 us -> 7.19 us  [swap_with(): return lax.ppermute(value, 'gx', [(i, i ^ mask) for i in range(size)])]
    pallas_call x1, Pallas kernels: 1.64 us -> 1.37 us  [shards(): pl.pallas_call(functools.partial(bulk_kernel, sizes), out_shape=(pltpu.VM...]
  transfers between devices with their start and end apart: 8 -> 8, of which waited for: 4 -> 4; matrix products, arithmetic and copies ran while one was open for 0% -> 0% of each run, Pallas kernels for 15% -> 14%
where the time goes in v10:
time: 21.2 us; the launch traced here: 21 us
  starting transfers between devices  11.4 us (54%)
  Pallas kernels  4.51 us (21%)
  waiting for transfers between devices  3.87 us (18%)
  between operations  0.68 us (3%)
  other arithmetic  0.58 us (3%)
    ppermute x6, starting transfers between devices, swap_with(): return lax.ppermute(value, 'gx', [(i, i ^ mask) for i in range(size)])  7.19 us
    ppermute x2, starting transfers between devices, swap_over_chips(): return lax.ppermute(value, ('groups', 'gx'), route)  4.2 us
    ppermute x6, waiting for transfers between devices, swap_with(): return lax.ppermute(value, 'gx', [(i, i ^ mask) for i in range(size)])  3.86 us
    pallas_call x1, Pallas kernels, shards(): pl.pallas_call(functools.partial(edge_kernel, sizes), out_shape=(pltpu.VM...  1.67 us
    pallas_call x1, Pallas kernels, shards(): pl.pallas_call(functools.partial(bulk_kernel, sizes), out_shape=(pltpu.VM...  1.37 us
    pallas_call x1, Pallas kernels, shards(): pl.pallas_call(functools.partial(finish_kernel, sizes), out_shape=(pltpu....  1.22 us
    add x3, other arithmetic, shards(): totals = totals + swap_with(totals, size, mask | 1)  0.57 us
  transfers between devices with their start and end apart: 8, of which 4 were waited for; matrix products, arithmetic and copies ran while one was open for 0% of the time, Pallas kernels for 14%

profile of v10, /device:TPU:0, one launch (start us, length us, event | category | flops | bytes accessed | tf_op | source)
XLA Modules:
  0.0 21.0 jit_solution(7787207848937334101)
XLA Ops:
  0.6 1.7 %edges.1 = (f32[384,8,128]{2,1,0:T(8,128)S(1)}, bf16[6,384,128]{2,1,0:T(8,128)(2,1)S(1)}, s32[48]{0:T(128)S(4)}, f32[128,128]{1,0:T(8,128)S(1)}, f32[144,128]{1,...) custom-call(f32[384,8,128]{2,1,0:T(8,128)} %bitcast.9, ...), custom_call_target="tpu_custom_call" | custom-call | tf_op jit(solution)/shard_map/edges/pallas_call | solution.py:665
  2.3 3.0 %collective-permute-start.2 = (f32[240,128]{1,0:T(8,128)S(1)}, f32[240,128]{1,0:T(8,128)S(1)}, u32[]{:S(2)}, u32[]{:S(2)}) collective-permute-start(f32[240,128]{1,0:T(8,128)S(1)} %get-tuple-element.36.sent), channel_id=1, source_target_pairs={{1,2},{2,1},{3,4},{4,3},{5,6},{6,5},{7,8},{8,7},{9,10},{10,9},{11,... | collective-permute-start | bytes 368648 | tf_op jit(solution)/shard_map/ppermute | solution.py:622
  5.3 0.1 collective-permute-start
  5.5 0.4 %collective-permute-start.1 = (f32[144,128]{1,0:T(8,128)S(1)}, f32[144,128]{1,0:T(8,128)S(1)}, u32[]{:S(2)}, u32[]{:S(2)}) collective-permute-start(f32[144,128]{1,0:T(8,128)S(1)} %get-tuple-element.33.sent_b), channel_id=1, source_target_pairs={{0,1},{1,0},{2,3},{3,2},{4,5},{5,4},{6,7},{7,6},{8,9},{9,8},{10,11... | collective-permute-start | bytes 221192 | tf_op jit(solution)/shard_map/ppermute | solution.py:611
  5.8 1.4 %bulk.1 = (f32[384,8,128]{2,1,0:T(8,128)S(1)}, f32[6,384,128]{2,1,0:T(8,128)S(1)}, f32[16,128]{1,0:T(8,128)S(1)}, f32[144,128]{1,0:T(8,128)S(1)}) custom-call(f32[384,8,128]{2,1,0:T(8,128)S(1)} %get-tuple-element.22.given, bf16[6,384,128]{2,1,0:T(8,128)(2,1)S(1)} %get-tuple-element.23.forward, ...), custom_call_target="tpu_custom_call", output_to_operand_aliasing={{0}: (0, {}), {3}: (6, {})} | custom-call | flops 7864320 | bytes 3145728 | tf_op jit(solution)/shard_map/bulk/pallas_call | solution.py:708
  7.2 1.2 %collective-permute-start.3 = (f32[144,128]{1,0:T(8,128)S(1)}, f32[144,128]{1,0:T(8,128)S(1)}, u32[]{:S(2)}, u32[]{:S(2)}) collective-permute-start(f32[144,128]{1,0:T(8,128)S(1)} %get-tuple-element.37.late), channel_id=1, source_target_pairs={{1,2},{2,1},{3,4},{4,3},{5,6},{6,5},{7,8},{8,7},{9,10},{10,9},{11,... | collective-permute-start | bytes 221192 | tf_op jit(solution)/shard_map/ppermute | solution.py:622
  8.4 0.0 collective-permute-done.got_a
  8.4 0.0 collective-permute-done.1.got_b
  8.4 0.2 %join_core.1 = (f32[17,48,128]{2,1,0:T(8,128)S(1)}, f32[16,128]{1,0:T(8,128)S(1)}) custom-call(f32[16,128]{1,0:T(8,128)S(1)} %get-tuple-element.30.sums_in, f32[6,384,128]{2,1,0:T(8,128)S(1)} %get-tuple-element.31.weights, f32[144,128]{1,0:T(8,128)S(1)} %get-tuple-element.32.sent_a, f32[144,128]{1,0:T(8,128)S(1)} %get-tuple-element.33.sent_b, ...), custom_call_target="tpu_custom_call" | custom-call | tf_op jit(solution)/shard_map/join_core/pallas_call | solution.py:734
  8.6 0.0 collective-permute-done.2.got
  8.7 0.5 %collective-permute-start.4 = (f32[2,128]{1,0:T(2,128)S(1)}, f32[2,128]{1,0:T(2,128)S(1)}, u32[]{:S(2)}, u32[]{:S(2)}) collective-permute-start(f32[2,128]{1,0:T(2,128)S(1)} %get-tuple-element.40), channel_id=1, source_target_pairs={{0,1},{1,0},{2,3},{3,2},{4,5},{5,4},{6,7},{7,6},{8,9},{9,8},{10,11... | collective-permute-start | bytes 3080 | tf_op jit(solution)/shard_map/ppermute | solution.py:611
  9.2 0.8 %collective-permute-done.4 = f32[2,128]{1,0:T(2,128)S(1)} collective-permute-done((f32[2,128]{1,0:T(2,128)S(1)}, f32[2,128]{1,0:T(2,128)S(1)}, u32[]{:S(2)}, u32[]{:S(2)}) %collective-permute-start.4) | collective-permute-done | bytes 1056 | tf_op jit(solution)/shard_map/ppermute | solution.py:611
  10.0 2.3 %collective-permute-start.5 = (f32[2,128]{1,0:T(2,128)S(1)}, f32[2,128]{1,0:T(2,128)S(1)}, u32[]{:S(2)}, u32[]{:S(2)}) collective-permute-start(f32[2,128]{1,0:T(2,128)S(1)} %add.15), channel_id=1, source_target_pairs={{0,3},{1,2},{2,1},{3,0},{4,7},{5,6},{6,5},{7,4},{8,11},{9,10},{10,... | collective-permute-start | bytes 3080 | tf_op jit(solution)/shard_map/ppermute | solution.py:611
  12.3 1.3 %collective-permute-done.5 = f32[2,128]{1,0:T(2,128)S(1)} collective-permute-done((f32[2,128]{1,0:T(2,128)S(1)}, f32[2,128]{1,0:T(2,128)S(1)}, u32[]{:S(2)}, u32[]{:S(2)}) %collective-permute-start.5) | collective-permute-done | bytes 1056 | tf_op jit(solution)/shard_map/ppermute | solution.py:611
  13.6 1.5 %collective-permute-start.6 = (f32[2,128]{1,0:T(2,128)S(1)}, f32[2,128]{1,0:T(2,128)S(1)}, u32[]{:S(2)}, u32[]{:S(2)}) collective-permute-start(f32[2,128]{1,0:T(2,128)S(1)} %add.16), channel_id=1, source_target_pairs={{0,5},{1,4},{2,7},{3,6},{4,1},{5,0},{6,3},{7,2},{8,13},{9,12},{10,... | collective-permute-start | bytes 3080 | tf_op jit(solution)/shard_map/ppermute | solution.py:611
  15.0 0.0 collective-permute-done.3.late
  15.0 1.2 %finish.1 = (f32[384,8,128]{2,1,0:T(8,128)S(1)}, f32[384,8,128]{2,1,0:T(8,128)}, f32[2,128]{1,0:T(2,128)S(1)}) custom-call(f32[384,8,128]{2,1,0:T(8,128)S(1)} %get-tuple-element.29.given, f32[17,48,128]{2,1,0:T(8,128)S(1)} %get-tuple-element.34.changes_core, f32[17,48,128]{2,1,0:T(8,128)S(1)} %get-tuple-element.38.changes_chip, ...), custom_call_target="tpu_custom_call", output_to_operand_aliasing={{0}: (0, {})} | custom-call | bytes 3145728 | tf_op jit(solution)/shard_map/finish/pallas_call | solution.py:764
  16.2 0.3 %collective-permute-done.6 = f32[2,128]{1,0:T(2,128)S(1)} collective-permute-done((f32[2,128]{1,0:T(2,128)S(1)}, f32[2,128]{1,0:T(2,128)S(1)}, u32[]{:S(2)}, u32[]{:S(2)}) %collective-permute-start.6) | collective-permute-done | bytes 1056 | tf_op jit(solution)/shard_map/ppermute | solution.py:611
  16.6 2.5 %collective-permute-start.7 = (f32[2,128]{1,0:T(2,128)S(1)}, f32[2,128]{1,0:T(2,128)S(1)}, u32[]{:S(2)}, u32[]{:S(2)}) collective-permute-start(f32[2,128]{1,0:T(2,128)S(1)} %add_add_fusion), channel_id=1, source_target_pairs={{0,9},{1,8},{2,11},{3,10},{4,13},{5,12},{6,15},{7,14},{8,1},{9,0},... | collective-permute-start | bytes 3080 | tf_op jit(solution)/shard_map/ppermute | solution.py:611
  19.0 1.4 %collective-permute-done.7 = f32[2,128]{1,0:T(2,128)S(1)} collective-permute-done((f32[2,128]{1,0:T(2,128)S(1)}, f32[2,128]{1,0:T(2,128)S(1)}, u32[]{:S(2)}, u32[]{:S(2)}) %collective-permute-start.7) | collective-permute-done | bytes 1056 | tf_op jit(solution)/shard_map/ppermute | solution.py:611
  20.5 0.6 %add.19 = f32[2,128]{1,0:T(2,128)} add(f32[2,128]{1,0:T(2,128)S(1)} %add_add_fusion, f32[2,128]{1,0:T(2,128)S(1)} %collective-permute-done.7) | non-fusion elementwise | flops 256 | bytes 3072 | tf_op jit(solution)/shard_map/add | solution.py:782
  (4 shorter events, 0.0 us)
Async XLA Ops:
  2.3 6.3 %collective-permute-start.2 = (f32[240,128]{1,0:T(8,128)S(1)}, f32[240,128]{1,0:T(8,128)S(1)}, u32[]{:S(2)}, u32[]{:S(2)}) collective-permute-start(f32[240,128]{1,0:T(8,128)S(1)} %get-tuple-element.36.sent), channel_id=1, source_target_pairs={{1,2},{2,1},{3,4},{4,3},{5,6},{6,5},{7,8},{8,7},{9,10},{10,9},{11,... | collective-permute-start | bytes 368648 | tf_op jit(solution)/shard_map/ppermute | solution.py:622
  5.3 3.1 %collective-permute-start = (f32[144,128]{1,0:T(8,128)S(1)}, f32[144,128]{1,0:T(8,128)S(1)}, u32[]{:S(2)}, u32[]{:S(2)}) collective-permute-start(f32[144,128]{1,0:T(8,128)S(1)} %get-tuple-element.32.sent_a), channel_id=1, source_target_pairs={{0,1},{1,0},{2,3},{3,2},{4,5},{5,4},{6,7},{7,6},{8,9},{9,8},{10,11... | collective-permute-start | bytes 221192 | tf_op jit(solution)/shard_map/ppermute | solution.py:611
  5.5 2.9 %collective-permute-start.1 = (f32[144,128]{1,0:T(8,128)S(1)}, f32[144,128]{1,0:T(8,128)S(1)}, u32[]{:S(2)}, u32[]{:S(2)}) collective-permute-start(f32[144,128]{1,0:T(8,128)S(1)} %get-tuple-element.33.sent_b), channel_id=1, source_target_pairs={{0,1},{1,0},{2,3},{3,2},{4,5},{5,4},{6,7},{7,6},{8,9},{9,8},{10,11... | collective-permute-start | bytes 221192 | tf_op jit(solution)/shard_map/ppermute | solution.py:611
  7.2 7.8 %collective-permute-start.3 = (f32[144,128]{1,0:T(8,128)S(1)}, f32[144,128]{1,0:T(8,128)S(1)}, u32[]{:S(2)}, u32[]{:S(2)}) collective-permute-start(f32[144,128]{1,0:T(8,128)S(1)} %get-tuple-element.37.late), channel_id=1, source_target_pairs={{1,2},{2,1},{3,4},{4,3},{5,6},{6,5},{7,8},{8,7},{9,10},{10,9},{11,... | collective-permute-start | bytes 221192 | tf_op jit(solution)/shard_map/ppermute | solution.py:622
  8.7 1.3 %collective-permute-start.4 = (f32[2,128]{1,0:T(2,128)S(1)}, f32[2,128]{1,0:T(2,128)S(1)}, u32[]{:S(2)}, u32[]{:S(2)}) collective-permute-start(f32[2,128]{1,0:T(2,128)S(1)} %get-tuple-element.40), channel_id=1, source_target_pairs={{0,1},{1,0},{2,3},{3,2},{4,5},{5,4},{6,7},{7,6},{8,9},{9,8},{10,11... | collective-permute-start | bytes 3080 | tf_op jit(solution)/shard_map/ppermute | solution.py:611
  10.0 3.6 %collective-permute-start.5 = (f32[2,128]{1,0:T(2,128)S(1)}, f32[2,128]{1,0:T(2,128)S(1)}, u32[]{:S(2)}, u32[]{:S(2)}) collective-permute-start(f32[2,128]{1,0:T(2,128)S(1)} %add.15), channel_id=1, source_target_pairs={{0,3},{1,2},{2,1},{3,0},{4,7},{5,6},{6,5},{7,4},{8,11},{9,10},{10,... | collective-permute-start | bytes 3080 | tf_op jit(solution)/shard_map/ppermute | solution.py:611
  13.6 3.0 %collective-permute-start.6 = (f32[2,128]{1,0:T(2,128)S(1)}, f32[2,128]{1,0:T(2,128)S(1)}, u32[]{:S(2)}, u32[]{:S(2)}) collective-permute-start(f32[2,128]{1,0:T(2,128)S(1)} %add.16), channel_id=1, source_target_pairs={{0,5},{1,4},{2,7},{3,6},{4,1},{5,0},{6,3},{7,2},{8,13},{9,12},{10,... | collective-permute-start | bytes 3080 | tf_op jit(solution)/shard_map/ppermute | solution.py:611
  16.6 3.9 %collective-permute-start.7 = (f32[2,128]{1,0:T(2,128)S(1)}, f32[2,128]{1,0:T(2,128)S(1)}, u32[]{:S(2)}, u32[]{:S(2)}) collective-permute-start(f32[2,128]{1,0:T(2,128)S(1)} %add_add_fusion), channel_id=1, source_target_pairs={{0,9},{1,8},{2,11},{3,10},{4,13},{5,12},{6,15},{7,14},{8,1},{9,0},... | collective-permute-start | bytes 3080 | tf_op jit(solution)/shard_map/ppermute | solution.py:611

commit v11 on v9

--- a/solution.py
+++ b/solution.py
@@ -14,7 +14,7 @@
 SOON = 5
 LATE = 2
 PUSHED = ((0, 0), (0, 1), (1, 0), (0, -1))
-GROUPS = (16, 8, 4, 2)
+GROUPS = (24, 16, 8, 4, 2)
 ROOM = 16 << 20
 
 

time: 21.2 us -> 21.2 us (level)
  starting transfers between devices: 11.1 us -> 11.4 us
  Pallas kernels: 4.75 us -> 4.48 us
    pallas_call x1, Pallas kernels: 1.61 us -> 1.34 us  [shards(): pl.pallas_call(functools.partial(bulk_kernel, sizes), out_shape=(pltpu.VM...]
    ppermute x6, starting transfers between devices: 6.95 us -> 7.21 us  [swap_with(): return lax.ppermute(value, 'gx', [(i, i ^ mask) for i in range(size)])]
  transfers between devices with their start and end apart: 8 -> 8, of which waited for: 4 -> 4; matrix products, arithmetic and copies ran while one was open for 0% -> 0% of each run, Pallas kernels for 15% -> 13%
where the time goes in v11:
time: 21.2 us; the launch traced here: 21 us
  starting transfers between devices  11.4 us (54%)
  Pallas kernels  4.48 us (21%)
  waiting for transfers between devices  3.87 us (18%)
  between operations  0.68 us (3%)
  other arithmetic  0.58 us (3%)
    ppermute x6, starting transfers between devices, swap_with(): return lax.ppermute(value, 'gx', [(i, i ^ mask) for i in range(size)])  7.21 us
    ppermute x2, starting transfers between devices, swap_over_chips(): return lax.ppermute(value, ('groups', 'gx'), route)  4.2 us
    ppermute x6, waiting for transfers between devices, swap_with(): return lax.ppermute(value, 'gx', [(i, i ^ mask) for i in range(size)])  3.86 us
    pallas_call x1, Pallas kernels, shards(): pl.pallas_call(functools.partial(edge_kernel, sizes), out_shape=(pltpu.VM...  1.67 us
    pallas_call x1, Pallas kernels, shards(): pl.pallas_call(functools.partial(bulk_kernel, sizes), out_shape=(pltpu.VM...  1.34 us
    pallas_call x1, Pallas kernels, shards(): pl.pallas_call(functools.partial(finish_kernel, sizes), out_shape=(pltpu....  1.22 us
    add x3, other arithmetic, shards(): totals = totals + swap_with(totals, size, mask | 1)  0.57 us
  transfers between devices with their start and end apart: 8, of which 4 were waited for; matrix products, arithmetic and copies ran while one was open for 0% of the time, Pallas kernels for 13%

profile of v11, /device:TPU:0, one launch (start us, length us, event | category | flops | bytes accessed | tf_op | source)
XLA Modules:
  0.0 21.0 jit_solution(5578085811886992154)
XLA Ops:
  0.6 1.7 %edges.1 = (f32[384,8,128]{2,1,0:T(8,128)S(1)}, bf16[6,384,128]{2,1,0:T(8,128)(2,1)S(1)}, s32[48]{0:T(128)S(4)}, f32[128,128]{1,0:T(8,128)S(1)}, f32[144,128]{1,...) custom-call(f32[384,8,128]{2,1,0:T(8,128)} %bitcast.9, ...), custom_call_target="tpu_custom_call" | custom-call | tf_op jit(solution)/shard_map/edges/pallas_call | solution.py:667
  2.3 3.0 %collective-permute-start.2 = (f32[240,128]{1,0:T(8,128)S(1)}, f32[240,128]{1,0:T(8,128)S(1)}, u32[]{:S(2)}, u32[]{:S(2)}) collective-permute-start(f32[240,128]{1,0:T(8,128)S(1)} %get-tuple-element.36.sent), channel_id=1, source_target_pairs={{1,2},{2,1},{3,4},{4,3},{5,6},{6,5},{7,8},{8,7},{9,10},{10,9},{11,... | collective-permute-start | bytes 368648 | tf_op jit(solution)/shard_map/ppermute | solution.py:624
  5.3 0.1 collective-permute-start
  5.5 0.4 %collective-permute-start.1 = (f32[144,128]{1,0:T(8,128)S(1)}, f32[144,128]{1,0:T(8,128)S(1)}, u32[]{:S(2)}, u32[]{:S(2)}) collective-permute-start(f32[144,128]{1,0:T(8,128)S(1)} %get-tuple-element.33.sent_b), channel_id=1, source_target_pairs={{0,1},{1,0},{2,3},{3,2},{4,5},{5,4},{6,7},{7,6},{8,9},{9,8},{10,11... | collective-permute-start | bytes 221192 | tf_op jit(solution)/shard_map/ppermute | solution.py:613
  5.8 1.3 %bulk.1 = (f32[384,8,128]{2,1,0:T(8,128)S(1)}, f32[6,384,128]{2,1,0:T(8,128)S(1)}, f32[16,128]{1,0:T(8,128)S(1)}, f32[96,128]{1,0:T(8,128)S(1)}) custom-call(f32[384,8,128]{2,1,0:T(8,128)S(1)} %get-tuple-element.22.given, bf16[6,384,128]{2,1,0:T(8,128)(2,1)S(1)} %get-tuple-element.23.forward, ...), custom_call_target="tpu_custom_call", output_to_operand_aliasing={{0}: (0, {}), {3}: (6, {})} | custom-call | flops 7864320 | bytes 3145728 | tf_op jit(solution)/shard_map/bulk/pallas_call | solution.py:710
  7.2 1.2 %collective-permute-start.3 = (f32[96,128]{1,0:T(8,128)S(1)}, f32[96,128]{1,0:T(8,128)S(1)}, u32[]{:S(2)}, u32[]{:S(2)}) collective-permute-start(f32[96,128]{1,0:T(8,128)S(1)} %get-tuple-element.37.late), channel_id=1, source_target_pairs={{1,2},{2,1},{3,4},{4,3},{5,6},{6,5},{7,8},{8,7},{9,10},{10,9},{11,... | collective-permute-start | bytes 147464 | tf_op jit(solution)/shard_map/ppermute | solution.py:624
  8.4 0.0 collective-permute-done.got_a
  8.4 0.0 collective-permute-done.1.got_b
  8.4 0.2 %join_core.1 = (f32[17,48,128]{2,1,0:T(8,128)S(1)}, f32[16,128]{1,0:T(8,128)S(1)}) custom-call(f32[16,128]{1,0:T(8,128)S(1)} %get-tuple-element.30.sums_in, f32[6,384,128]{2,1,0:T(8,128)S(1)} %get-tuple-element.31.weights, f32[144,128]{1,0:T(8,128)S(1)} %get-tuple-element.32.sent_a, f32[144,128]{1,0:T(8,128)S(1)} %get-tuple-element.33.sent_b, ...), custom_call_target="tpu_custom_call" | custom-call | tf_op jit(solution)/shard_map/join_core/pallas_call | solution.py:736
  8.6 0.0 collective-permute-done.2.got.soon
  8.6 0.5 %collective-permute-start.4 = (f32[2,128]{1,0:T(2,128)S(1)}, f32[2,128]{1,0:T(2,128)S(1)}, u32[]{:S(2)}, u32[]{:S(2)}) collective-permute-start(f32[2,128]{1,0:T(2,128)S(1)} %get-tuple-element.40), channel_id=1, source_target_pairs={{0,1},{1,0},{2,3},{3,2},{4,5},{5,4},{6,7},{7,6},{8,9},{9,8},{10,11... | collective-permute-start | bytes 3080 | tf_op jit(solution)/shard_map/ppermute | solution.py:613
  9.1 0.8 %collective-permute-done.4 = f32[2,128]{1,0:T(2,128)S(1)} collective-permute-done((f32[2,128]{1,0:T(2,128)S(1)}, f32[2,128]{1,0:T(2,128)S(1)}, u32[]{:S(2)}, u32[]{:S(2)}) %collective-permute-start.4) | collective-permute-done | bytes 1056 | tf_op jit(solution)/shard_map/ppermute | solution.py:613
  10.0 2.3 %collective-permute-start.5 = (f32[2,128]{1,0:T(2,128)S(1)}, f32[2,128]{1,0:T(2,128)S(1)}, u32[]{:S(2)}, u32[]{:S(2)}) collective-permute-start(f32[2,128]{1,0:T(2,128)S(1)} %add.15), channel_id=1, source_target_pairs={{0,3},{1,2},{2,1},{3,0},{4,7},{5,6},{6,5},{7,4},{8,11},{9,10},{10,... | collective-permute-start | bytes 3080 | tf_op jit(solution)/shard_map/ppermute | solution.py:613
  12.3 1.3 %collective-permute-done.5 = f32[2,128]{1,0:T(2,128)S(1)} collective-permute-done((f32[2,128]{1,0:T(2,128)S(1)}, f32[2,128]{1,0:T(2,128)S(1)}, u32[]{:S(2)}, u32[]{:S(2)}) %collective-permute-start.5) | collective-permute-done | bytes 1056 | tf_op jit(solution)/shard_map/ppermute | solution.py:613
  13.6 1.5 %collective-permute-start.6 = (f32[2,128]{1,0:T(2,128)S(1)}, f32[2,128]{1,0:T(2,128)S(1)}, u32[]{:S(2)}, u32[]{:S(2)}) collective-permute-start(f32[2,128]{1,0:T(2,128)S(1)} %add.16), channel_id=1, source_target_pairs={{0,5},{1,4},{2,7},{3,6},{4,1},{5,0},{6,3},{7,2},{8,13},{9,12},{10,... | collective-permute-start | bytes 3080 | tf_op jit(solution)/shard_map/ppermute | solution.py:613
  15.0 0.0 collective-permute-done.3.late
  15.0 1.2 %finish.1 = (f32[384,8,128]{2,1,0:T(8,128)S(1)}, f32[384,8,128]{2,1,0:T(8,128)}, f32[2,128]{1,0:T(2,128)S(1)}) custom-call(f32[384,8,128]{2,1,0:T(8,128)S(1)} %get-tuple-element.29.given, f32[17,48,128]{2,1,0:T(8,128)S(1)} %get-tuple-element.34.changes_core, f32[17,48,128]{2,1,0:T(8,128)S(1)} %get-tuple-element.38.changes_chip, ...), custom_call_target="tpu_custom_call", output_to_operand_aliasing={{0}: (0, {})} | custom-call | bytes 3145728 | tf_op jit(solution)/shard_map/finish/pallas_call | solution.py:766
  16.2 0.3 %collective-permute-done.6 = f32[2,128]{1,0:T(2,128)S(1)} collective-permute-done((f32[2,128]{1,0:T(2,128)S(1)}, f32[2,128]{1,0:T(2,128)S(1)}, u32[]{:S(2)}, u32[]{:S(2)}) %collective-permute-start.6) | collective-permute-done | bytes 1056 | tf_op jit(solution)/shard_map/ppermute | solution.py:613
  16.6 2.5 %collective-permute-start.7 = (f32[2,128]{1,0:T(2,128)S(1)}, f32[2,128]{1,0:T(2,128)S(1)}, u32[]{:S(2)}, u32[]{:S(2)}) collective-permute-start(f32[2,128]{1,0:T(2,128)S(1)} %add_add_fusion), channel_id=1, source_target_pairs={{0,9},{1,8},{2,11},{3,10},{4,13},{5,12},{6,15},{7,14},{8,1},{9,0},... | collective-permute-start | bytes 3080 | tf_op jit(solution)/shard_map/ppermute | solution.py:613
  19.0 1.4 %collective-permute-done.7 = f32[2,128]{1,0:T(2,128)S(1)} collective-permute-done((f32[2,128]{1,0:T(2,128)S(1)}, f32[2,128]{1,0:T(2,128)S(1)}, u32[]{:S(2)}, u32[]{:S(2)}) %collective-permute-start.7) | collective-permute-done | bytes 1056 | tf_op jit(solution)/shard_map/ppermute | solution.py:613
  20.5 0.6 %add.19 = f32[2,128]{1,0:T(2,128)} add(f32[2,128]{1,0:T(2,128)S(1)} %add_add_fusion, f32[2,128]{1,0:T(2,128)S(1)} %collective-permute-done.7) | non-fusion elementwise | flops 256 | bytes 3072 | tf_op jit(solution)/shard_map/add | solution.py:784
  (4 shorter events, 0.0 us)
Async XLA Ops:
  2.3 6.3 %collective-permute-start.2 = (f32[240,128]{1,0:T(8,128)S(1)}, f32[240,128]{1,0:T(8,128)S(1)}, u32[]{:S(2)}, u32[]{:S(2)}) collective-permute-start(f32[240,128]{1,0:T(8,128)S(1)} %get-tuple-element.36.sent), channel_id=1, source_target_pairs={{1,2},{2,1},{3,4},{4,3},{5,6},{6,5},{7,8},{8,7},{9,10},{10,9},{11,... | collective-permute-start | bytes 368648 | tf_op jit(solution)/shard_map/ppermute | solution.py:624
  5.3 3.1 %collective-permute-start = (f32[144,128]{1,0:T(8,128)S(1)}, f32[144,128]{1,0:T(8,128)S(1)}, u32[]{:S(2)}, u32[]{:S(2)}) collective-permute-start(f32[144,128]{1,0:T(8,128)S(1)} %get-tuple-element.32.sent_a), channel_id=1, source_target_pairs={{0,1},{1,0},{2,3},{3,2},{4,5},{5,4},{6,7},{7,6},{8,9},{9,8},{10,11... | collective-permute-start | bytes 221192 | tf_op jit(solution)/shard_map/ppermute | solution.py:613
  5.5 2.9 %collective-permute-start.1 = (f32[144,128]{1,0:T(8,128)S(1)}, f32[144,128]{1,0:T(8,128)S(1)}, u32[]{:S(2)}, u32[]{:S(2)}) collective-permute-start(f32[144,128]{1,0:T(8,128)S(1)} %get-tuple-element.33.sent_b), channel_id=1, source_target_pairs={{0,1},{1,0},{2,3},{3,2},{4,5},{5,4},{6,7},{7,6},{8,9},{9,8},{10,11... | collective-permute-start | bytes 221192 | tf_op jit(solution)/shard_map/ppermute | solution.py:613
  7.2 7.8 %collective-permute-start.3 = (f32[96,128]{1,0:T(8,128)S(1)}, f32[96,128]{1,0:T(8,128)S(1)}, u32[]{:S(2)}, u32[]{:S(2)}) collective-permute-start(f32[96,128]{1,0:T(8,128)S(1)} %get-tuple-element.37.late), channel_id=1, source_target_pairs={{1,2},{2,1},{3,4},{4,3},{5,6},{6,5},{7,8},{8,7},{9,10},{10,9},{11,... | collective-permute-start | bytes 147464 | tf_op jit(solution)/shard_map/ppermute | solution.py:624
  8.6 1.3 %collective-permute-start.4 = (f32[2,128]{1,0:T(2,128)S(1)}, f32[2,128]{1,0:T(2,128)S(1)}, u32[]{:S(2)}, u32[]{:S(2)}) collective-permute-start(f32[2,128]{1,0:T(2,128)S(1)} %get-tuple-element.40), channel_id=1, source_target_pairs={{0,1},{1,0},{2,3},{3,2},{4,5},{5,4},{6,7},{7,6},{8,9},{9,8},{10,11... | collective-permute-start | bytes 3080 | tf_op jit(solution)/shard_map/ppermute | solution.py:613
  10.0 3.6 %collective-permute-start.5 = (f32[2,128]{1,0:T(2,128)S(1)}, f32[2,128]{1,0:T(2,128)S(1)}, u32[]{:S(2)}, u32[]{:S(2)}) collective-permute-start(f32[2,128]{1,0:T(2,128)S(1)} %add.15), channel_id=1, source_target_pairs={{0,3},{1,2},{2,1},{3,0},{4,7},{5,6},{6,5},{7,4},{8,11},{9,10},{10,... | collective-permute-start | bytes 3080 | tf_op jit(solution)/shard_map/ppermute | solution.py:613
  13.6 3.0 %collective-permute-start.6 = (f32[2,128]{1,0:T(2,128)S(1)}, f32[2,128]{1,0:T(2,128)S(1)}, u32[]{:S(2)}, u32[]{:S(2)}) collective-permute-start(f32[2,128]{1,0:T(2,128)S(1)} %add.16), channel_id=1, source_target_pairs={{0,5},{1,4},{2,7},{3,6},{4,1},{5,0},{6,3},{7,2},{8,13},{9,12},{10,... | collective-permute-start | bytes 3080 | tf_op jit(solution)/shard_map/ppermute | solution.py:613
  16.6 3.9 %collective-permute-start.7 = (f32[2,128]{1,0:T(2,128)S(1)}, f32[2,128]{1,0:T(2,128)S(1)}, u32[]{:S(2)}, u32[]{:S(2)}) collective-permute-start(f32[2,128]{1,0:T(2,128)S(1)} %add_add_fusion), channel_id=1, source_target_pairs={{0,9},{1,8},{2,11},{3,10},{4,13},{5,12},{6,15},{7,14},{8,1},{9,0},... | collective-permute-start | bytes 3080 | tf_op jit(solution)/shard_map/ppermute | solution.py:613
